TPU v7x, 32 devices: a whole 2x2x4 slice. The times are simulated.
32 devices in a mesh: groups: 2 (over y), shard: 4 (over z), width: 2 (over x), rep: 2 (over core).
Axes of the slice: x: 2, y: 2, z: 4, core: 2. Of those that a mesh axis runs over, the one named last changes fastest.
Arguments:
- source_vecs: bfloat16 [16384, 1024], P(('groups', 'shard', 'rep'), 'width'), parts along dimension 0
- target_vecs: bfloat16 [16384, 1024], P(('groups', 'shard', 'rep'), 'width'), parts along dimension 0
- fwd_owner: int32 [16384, 4], P(('groups', 'shard', 'rep')), parts along dimension 0, may hold values from 0 to 7, all different within a row; in each aligned block of 1024 rows (0 to 1023, 1024 to 2047, ...) at most 640 rows name the same one
- fwd_row: int32 [16384, 4], P(('groups', 'shard', 'rep')), parts along dimension 0, may hold values from 0 to 1023
- bwd_owner: int32 [16384, 4], P(('groups', 'shard', 'rep')), parts along dimension 0, may hold values from 0 to 7, all different within a row; in each aligned block of 1024 rows (0 to 1023, 1024 to 2047, ...) at most 640 rows name the same one
- bwd_row: int32 [16384, 4], P(('groups', 'shard', 'rep')), parts along dimension 0, may hold values from 0 to 1023
- cand_lists: int32 [8, 16], P('groups'), parts along dimension 0, may hold values from 0 to 31, as said below
Outputs:
- best_margin: float32 [16384, 16], P(('groups', 'shard', 'rep'), 'width'), parts along dimension 0
- fwd_mean: float32 [16384], P(('groups', 'shard', 'rep')), parts along dimension 0
- bwd_mean: bfloat16 [16384], P(('groups', 'shard', 'rep')), parts along dimension 0
There are 2 independent parts, one for each index of `groups`. A program takes and returns all parts, laid end to end along the dimension named above; each array names one. Nothing has to cross between parts.
Inputs may be any that keep to these rules, and one draw needn't show every extreme that they name: fwd_owner[i, k] * 1024 + fwd_row[i, k] is a target sentence; the 4 owners of a row differ, and among the 1024 rows of one device at most 640 name one owner. bwd_owner[j, k] * 1024 + bwd_row[j, k] is a source sentence; the 4 owners of a row differ, and among the 1024 rows of one device at most 640 name one owner. `cand_lists`: each list names 16 different target blocks; block b lies on the device of index b // 4 along shard+rep, and at most 2 blocks of one list lie on one device.
All inputs are finite; a program needn't handle non-finite values.
Results may differ from a plain program's by a relative error of at most 0.0057.
Values may be sent and summed in bfloat16 or wider, within the bound.
No kernel may reach another device: no remote copies, remote signals or barrier semaphores. Data moves between devices by JAX's collectives and lax.ppermute only.
A program may use at most 128 MiB of HBM per device.

v0:
```python
import math

import jax
import jax.numpy as jnp
from jax import lax
from jax.sharding import PartitionSpec as P

D = 1024
K = 4
CAND = 16
BLOCK = 256
ROWS = 1024


EPS = 1e-05


def normalize(vectors, total_sq):
    scale = lax.rsqrt(total_sq / D + EPS)
    return (vectors.astype(jnp.float32) * scale[:, None]).astype(jnp.bfloat16)


def slot_ranks(owner_ids, owners):
    flat = owner_ids.reshape(-1)
    onehot = (flat[:, None] == jnp.arange(owners, dtype=jnp.int32)[None, :]).astype(jnp.int32)
    running = jnp.cumsum(onehot, axis=0)
    ranks = jnp.sum(running * onehot, axis=1) - 1
    return ranks.reshape(owner_ids.shape)


def request_table(owner_ids, row_ids, owners, slot_count):
    ranks = slot_ranks(owner_ids, owners)
    places = (owner_ids * slot_count + ranks).reshape(-1)
    table = jnp.zeros((owners * slot_count,), jnp.int32).at[places].set(row_ids.reshape(-1))
    return (table.reshape(owners, slot_count), places)


def answer(asked, local_rows):
    picked = jnp.take(local_rows, asked.reshape(-1), axis=0)
    return picked.reshape(asked.shape[0], asked.shape[1], local_rows.shape[1])


def neighbour_terms(replies, places, normed):
    flat = replies.reshape(-1, replies.shape[2])
    rows = jnp.take(flat, places, axis=0).reshape(normed.shape[0], K, flat.shape[1])
    return jnp.einsum("rkc,rc->rk", rows, normed, preferred_element_type=jnp.float32)


def owned_slots(lists, owner, per_owner, blocks_dev):
    holders = lists // blocks_dev
    mine = (holders == owner).astype(jnp.int32)
    ranks = jnp.cumsum(mine, axis=1) - 1
    slots = jnp.arange(per_owner, dtype=jnp.int32)
    pick = mine[:, None, :] * (ranks[:, None, :] == slots[None, :, None]).astype(jnp.int32)
    return jnp.sum(pick * (lists % blocks_dev)[:, None, :], axis=2)


def on_device(source_vecs, target_vecs, fwd_owner, fwd_row, bwd_owner, bwd_row, cand_lists):
    rep_count = lax.axis_size("rep")
    shard_count = lax.axis_size("shard")
    width_count = lax.axis_size("width")
    owners = shard_count * rep_count
    per_owner = max(1, CAND // owners)
    slot_count = 5 * ROWS * K // (4 * owners)
    local_rows = source_vecs.shape[0]
    columns = source_vecs.shape[1]
    blocks_dev = local_rows // BLOCK
    per_width = CAND // width_count
    root = math.sqrt(D)
    src_sq, tgt_sq = lax.psum(
        (
            jnp.sum(jnp.square(source_vecs.astype(jnp.float32)), axis=1),
            jnp.sum(jnp.square(target_vecs.astype(jnp.float32)), axis=1),
        ),
        "width",
    )
    src_normed = normalize(source_vecs, src_sq)
    tgt_normed = normalize(target_vecs, tgt_sq)
    fwd_table, fwd_places = request_table(fwd_owner, fwd_row, owners, slot_count)
    bwd_table, bwd_places = request_table(bwd_owner, bwd_row, owners, slot_count)
    fwd_asked, bwd_asked = (
        lax.all_to_all(fwd_table, ("shard", "rep"), split_axis=0, concat_axis=0, tiled=True),
        lax.all_to_all(bwd_table, ("shard", "rep"), split_axis=0, concat_axis=0, tiled=True),
    )
    fwd_reply, bwd_reply = (
        lax.all_to_all(
            answer(fwd_asked, tgt_normed), ("shard", "rep"), split_axis=0, concat_axis=0, tiled=True
        ),
        lax.all_to_all(
            answer(bwd_asked, src_normed), ("shard", "rep"), split_axis=0, concat_axis=0, tiled=True
        ),
    )
    fwd_part = neighbour_terms(fwd_reply, fwd_places, src_normed)
    bwd_part = neighbour_terms(bwd_reply, bwd_places, tgt_normed)
    fwd_dots, bwd_dots = lax.psum((fwd_part, bwd_part), "width")
    fwd_mean = jnp.mean(fwd_dots / root, axis=1)
    bwd_mean = jnp.mean(bwd_dots / root, axis=1).astype(jnp.bfloat16)
    shard_index = lax.axis_index("shard")
    rep_index = lax.axis_index("rep")
    owner_index = shard_index * rep_count + rep_index
    local_blocks = tgt_normed.reshape(blocks_dev, BLOCK, columns)
    local_means = bwd_mean.reshape(blocks_dev, BLOCK)
    local_ids = owned_slots(cand_lists, owner_index, per_owner, blocks_dev)
    own_list = lax.dynamic_index_in_dim(cand_lists, shard_index, 0, keepdims=False)
    holders = own_list // blocks_dev
    ranks = slot_ranks(holders, owners)
    peer_ids = jnp.repeat(local_ids, rep_count, axis=0).reshape(-1)
    got_blocks, got_means = (
        lax.all_to_all(
            jnp.take(local_blocks, peer_ids, axis=0),
            ("shard", "rep"),
            split_axis=0,
            concat_axis=0,
            tiled=True,
        ),
        lax.all_to_all(
            jnp.take(local_means, peer_ids, axis=0),
            ("shard", "rep"),
            split_axis=0,
            concat_axis=0,
            tiled=True,
        ),
    )
    positions = holders * per_owner + ranks
    listed_blocks = jnp.take(got_blocks, positions, axis=0)
    listed_means = jnp.take(got_means, positions, axis=0)
    wide_blocks = lax.all_to_all(listed_blocks, "width", split_axis=0, concat_axis=2, tiled=True)
    width_means = lax.dynamic_slice_in_dim(
        listed_means, lax.axis_index("width") * per_width, per_width, 0
    ).astype(jnp.float32)
    scores = jnp.einsum(
        "rd,cbd->crb",
        lax.all_gather(src_normed, "width", axis=1, tiled=True),
        wide_blocks,
        preferred_element_type=jnp.float32,
    )
    margin = scores / root - 0.5 * (fwd_mean[None, :, None] + width_means[:, None, :])
    best_margin = jnp.transpose(jnp.max(margin, axis=2))
    return (best_margin, fwd_mean, bwd_mean)


def solution(mesh):
    in_specs = (
        P(("groups", "shard", "rep"), "width"),
        P(("groups", "shard", "rep"), "width"),
        P(("groups", "shard", "rep"), None),
        P(("groups", "shard", "rep"), None),
        P(("groups", "shard", "rep"), None),
        P(("groups", "shard", "rep"), None),
        P("groups", None),
    )
    out_specs = (
        P(("groups", "shard", "rep"), "width"),
        P(("groups", "shard", "rep")),
        P(("groups", "shard", "rep")),
    )
    return jax.shard_map(
        on_device, mesh=mesh, in_specs=in_specs, out_specs=out_specs, check_vma=False
    )
```

profile of v0, /device:TPU:0, one launch (start us, length us, event | category | flops | bytes accessed | tf_op | source)
XLA Modules:
  0.0 577.8 jit_solution(12711725326964046139)
XLA Ops:
  14.5 16.1 %scatter_custom_fusion = s32[5120]{0:T(1024)} fusion(s32[4096]{0:T(1024)S(1)} %bitcast.106, s32[4096]{0:T(1024)S(1)} %reshape.424, s32[]{:T(128)} %constant.158.clone.1), kind=kCustom, calls=%fused_computation.68 | custom fusion | bytes 20484 | tf_op jit(solution)/shard_map/scatter | solution.py:34
  30.6 6.3 %all-to-all-start.2 = ((s32[8,1,640]{2,1,0:T(1,128)}), s32[8,1,640]{2,1,0:T(1,128)S(1)}, u32[]{:S(2)}, u32[]{:S(2)}) async-start(s32[8,1,640]{2,1,0:T(1,128)} %bitcast.12), calls=%async_computation.2 | async-start | bytes 40960 | tf_op jit(solution)/shard_map/all_to_all | solution.py:82
  38.9 5.0 all-reduce.1
  54.7 16.1 %scatter_custom_fusion.1 = s32[5120]{0:T(1024)} fusion(s32[4096]{0:T(1024)S(1)} %bitcast.105, s32[4096]{0:T(1024)S(1)} %reshape.432, s32[]{:T(128)} %constant.158.clone.1), kind=kCustom, calls=%fused_computation.66 | custom fusion | bytes 20484 | tf_op jit(solution)/shard_map/scatter | solution.py:34
  73.6 5.1 all-to-all-start.4
  78.7 4.7 broadcast_select_fusion.2
  84.4 4.5 all-to-all-start
  88.9 21.3 %gather_fusion.4 = bf16[5120,512]{1,0:T(8,128)(2,1)} fusion(bf16[1024,512]{1,0:T(8,128)(2,1)S(1)} %fusion.2, s32[5120]{0:T(1024)S(1)} %fusion.16), kind=kCustom, calls=%fused_computation.clone | custom fusion | bytes 10506240 | tf_op jit(solution)/shard_map/jit(_take)/gather | solution.py:39
  110.3 7.2 %broadcast_select_fusion.1 = bf16[5120,512]{1,0:T(8,128)(2,1)} fusion(bf16[5120,512]{1,0:T(8,128)(2,1)} %gather_fusion.4, pred[5120]{0:T(1024)(128)(4,1)S(1)} %compare_and_fusion.1), kind=kLoop, calls=%fused_computation.13 | loop fusion | flops 2621440 | bytes 10490880 | tf_op jit(solution)/shard_map/jit(_take)/select_n | solution.py:39
  117.5 65.4 %all-to-all-done = bf16[16,256,512]{2,1,0:T(8,128)(2,1)} async-done(((bf16[16,256,512]{2,1,0:T(8,128)(2,1)}), bf16[16,256,512]{2,1,0:T(8,128)(2,1)}, u32[]{:S(2)}, u32[]{:S(2)}) %all-to-all-start) | async-done | bytes 4194336 | tf_op jit(solution)/shard_map/all_to_all | solution.py:109
  182.9 4.8 all-to-all-start.3
  188.1 21.4 %gather_fusion.6 = bf16[5120,512]{1,0:T(8,128)(2,1)} fusion(bf16[1024,512]{1,0:T(8,128)(2,1)S(1)} %fusion.4, s32[5120]{0:T(1024)S(1)} %fusion.17), kind=kCustom, calls=%fused_computation.2.clone | custom fusion | bytes 10506240 | tf_op jit(solution)/shard_map/jit(_take)/gather | solution.py:39
  209.5 7.1 %broadcast_select_fusion = bf16[5120,512]{1,0:T(8,128)(2,1)} fusion(bf16[5120,512]{1,0:T(8,128)(2,1)} %gather_fusion.6, pred[5120]{0:T(1024)(128)(4,1)S(1)} %compare_and_fusion), kind=kLoop, calls=%fused_computation.12 | loop fusion | flops 2621440 | bytes 10490880 | tf_op jit(solution)/shard_map/jit(_take)/select_n | solution.py:39
  216.6 87.5 %all-to-all-done.3 = bf16[8,640,512]{2,1,0:T(8,128)(2,1)} async-done(((bf16[8,640,512]{2,1,0:T(8,128)(2,1)}), bf16[8,640,512]{2,1,0:T(8,128)(2,1)}, u32[]{:S(2)}, u32[]{:S(2)}) %all-to-all-start.3) | async-done | bytes 5242912 | tf_op jit(solution)/shard_map/all_to_all | solution.py:86
  304.1 4.8 all-to-all-start.5
  311.8 5.0 gather_fusion.1
  316.7 20.5 %gather_fusion.5 = bf16[4096,512]{1,0:T(8,128)(2,1)} fusion(bf16[5120,512]{1,0:T(8,128)(2,1)} %bitcast.15, s32[4096]{0:T(1024)S(1)} %fusion.18), kind=kCustom, calls=%fused_computation.1.clone | custom fusion | bytes 8404992 | tf_op jit(solution)/shard_map/jit(_take)/gather | solution.py:45
  337.3 3.9 broadcast_select_fusion.5
  341.2 7.1 %reshape.347 = bf16[1024,4,512]{2,1,0:T(4,128)(2,1)} reshape(bf16[4096,512]{1,0:T(8,128)(2,1)} %broadcast_select_fusion.5) | data formatting | bytes 8388608 | tf_op jit(solution)/shard_map/reshape | solution.py:45
  348.3 5.8 %fusion.8 = f32[1024,1,4]{2,1,0:T(1,128)S(1)} fusion(bf16[1024,4,512]{2,1,0:T(4,128)(2,1)} %reshape.347, bf16[1024,512,1]{1,0,2:T(8,128)(2,1)S(1)} %copy-done.6), kind=kOutput, calls=%fused_computation.29 | convolution fusion | flops 4194304 | bytes 5259264 | tf_op jit(solution)/shard_map/rkc,rc->rk/dot_general | solution.py:46
  354.4 70.9 %all-to-all-done.5 = bf16[8,640,512]{2,1,0:T(8,128)(2,1)} async-done(((bf16[8,640,512]{2,1,0:T(8,128)(2,1)}), bf16[8,640,512]{2,1,0:T(8,128)(2,1)}, u32[]{:S(2)}, u32[]{:S(2)}) %all-to-all-start.5) | async-done | bytes 5242912 | tf_op jit(solution)/shard_map/all_to_all | solution.py:89
  425.3 20.6 %gather_fusion.7 = bf16[4096,512]{1,0:T(8,128)(2,1)} fusion(bf16[5120,512]{1,0:T(8,128)(2,1)} %bitcast.23, s32[4096]{0:T(1024)S(1)} %fusion.19), kind=kCustom, calls=%fused_computation.3.clone | custom fusion | bytes 8404992 | tf_op jit(solution)/shard_map/jit(_take)/gather | solution.py:45
  445.9 4.0 broadcast_select_fusion.4
  449.8 6.9 %reshape.355 = bf16[1024,4,512]{2,1,0:T(4,128)(2,1)} reshape(bf16[4096,512]{1,0:T(8,128)(2,1)} %broadcast_select_fusion.4) | data formatting | bytes 8388608 | tf_op jit(solution)/shard_map/reshape | solution.py:45
  456.8 5.8 %fusion.6 = f32[1024,1,4]{2,1,0:T(1,128)S(1)} fusion(bf16[1024,4,512]{2,1,0:T(4,128)(2,1)} %reshape.355, bf16[1024,512,1]{1,0,2:T(8,128)(2,1)S(1)} %fusion.35), kind=kOutput, calls=%fused_computation.27 | convolution fusion | flops 4194304 | bytes 5259264 | tf_op jit(solution)/shard_map/rkc,rc->rk/dot_general | solution.py:46
  462.9 8.5 %all-reduce = (f32[1024,4]{0,1:T(4,128)S(1)}, f32[1024,4]{0,1:T(4,128)S(1)}) all-reduce(f32[1024,4]{0,1:T(4,128)S(1)} %bitcast.102, f32[1024,4]{0,1:T(4,128)S(1)} %bitcast.101), channel_id=1, replica_groups=mesh['groups'=2,'shard'=4,'width'=2,'rep'=2] {'width'}, use_global_device_ids=true, to_apply=%region_18.21 | all-reduce | flops 8192 | bytes 65536 | tf_op jit(solution)/shard_map/psum | solution.py:95
  472.7 3.6 all-to-all-start.6
  476.3 4.6 broadcast_select_fusion.3
  481.8 5.6 all-to-all-start.1
  489.0 68.6 %all-to-all-done.1 = bf16[16,256,512]{2,1,0:T(8,128)(2,1)} async-done(((bf16[16,256,512]{2,1,0:T(8,128)(2,1)}), bf16[16,256,512]{2,1,0:T(8,128)(2,1)}, u32[]{:S(2)}, u32[]{:S(2)}) %all-to-all-start.1) | async-done | bytes 4194336 | tf_op jit(solution)/shard_map/all_to_all | solution.py:127
  557.5 4.7 copy.62
  562.3 8.7 %fusion = f32[8,1024]{1,0:T(8,128)} fusion(f32[8,256]{1,0:T(8,128)S(1)} %fusion.25, f32[1024]{0:T(1024)S(1)} %broadcast_multiply_fusion, bf16[8,256,1024]{2,1,0:T(8,128)(2,1)} %bitcast.96, bf16[1024,1024]{1,0:T(8,128)(2,1)} %all-gather.2.cloned.1.call-done), kind=kOutput, calls=%fused_computation.11 | convolution fusion | flops 4305444864 | bytes 6336512 | tf_op jit(solution)/shard_map/rd,cbd->crb/dot_general | solution.py:131
  (123 shorter events, 31.1 us)
Async XLA Ops:
  7.2 6.8 %copy-start.8 = (s32[1024,4]{0,1:T(4,128)S(1)}, s32[1024,4]{0,1:T(4,128)}, u32[]{:S(2)}) copy-start(s32[1024,4]{0,1:T(4,128)} %param.14) | copy-start | bytes 49156
  7.2 29.7 %copy-start.7 = (s32[1024,4]{0,1:T(4,128)S(1)}, s32[1024,4]{0,1:T(4,128)}, u32[]{:S(2)}) copy-start(s32[1024,4]{0,1:T(4,128)} %param.15) | copy-start | bytes 49156
  7.2 30.5 %copy-start.10 = (s32[4,16]{1,0:T(4,128)S(1)}, s32[4,16]{1,0:T(4,128)}, u32[]{:S(2)}) copy-start(s32[4,16]{1,0:T(4,128)} %param.17) | copy-start | bytes 772
  7.2 31.2 %copy-start.1 = (bf16[1024,512]{1,0:T(8,128)(2,1)S(1)}, bf16[1024,512]{1,0:T(8,128)(2,1)}, u32[]{:S(2)}) copy-start(bf16[1024,512]{1,0:T(8,128)(2,1)} %param.11) | copy-start | bytes 3145732
  7.2 31.2 %copy-start.2 = (bf16[1024,512]{1,0:T(8,128)(2,1)S(1)}, bf16[1024,512]{1,0:T(8,128)(2,1)}, u32[]{:S(2)}) copy-start(bf16[1024,512]{1,0:T(8,128)(2,1)} %param.12) | copy-start | bytes 3145732
  13.6 30.3 %copy-start.3 = (s32[1024,4]{1,0:T(8,128)}, s32[1024,4]{1,0:T(8,128)S(1)}, u32[]{:S(2)}) copy-start(s32[1024,4]{1,0:T(8,128)S(1)} %copy.47) | copy-start | bytes 49156
  30.6 43.0 %all-to-all-start.2 = ((s32[8,1,640]{2,1,0:T(1,128)}), s32[8,1,640]{2,1,0:T(1,128)S(1)}, u32[]{:S(2)}, u32[]{:S(2)}) async-start(s32[8,1,640]{2,1,0:T(1,128)} %bitcast.12), calls=%async_computation.2 | async-start | bytes 40960 | tf_op jit(solution)/shard_map/all_to_all | solution.py:82
  37.2 15.2 %copy-start.9 = (s32[1024,4]{0,1:T(4,128)S(1)}, s32[1024,4]{0,1:T(4,128)}, u32[]{:S(2)}) copy-start(s32[1024,4]{0,1:T(4,128)} %param.16) | copy-start | bytes 49156
  73.6 10.8 %all-to-all-start.4 = ((s32[8,1,640]{2,1,0:T(1,128)}), s32[8,1,640]{2,1,0:T(1,128)S(1)}, u32[]{:S(2)}, u32[]{:S(2)}) async-start(s32[8,1,640]{2,1,0:T(1,128)} %bitcast.20), calls=%async_computation.4 | async-start | bytes 40960 | tf_op jit(solution)/shard_map/all_to_all | solution.py:83
  84.4 98.6 %all-to-all-start = ((bf16[16,256,512]{2,1,0:T(8,128)(2,1)}), bf16[16,256,512]{2,1,0:T(8,128)(2,1)}, u32[]{:S(2)}, u32[]{:S(2)}) async-start(bf16[16,256,512]{2,1,0:T(8,128)(2,1)} %broadcast_select_fusion.2), calls=%async_computation | async-start | bytes 8388608 | tf_op jit(solution)/shard_map/all_to_all | solution.py:109
  182.9 121.1 %all-to-all-start.3 = ((bf16[8,640,512]{2,1,0:T(8,128)(2,1)}), bf16[8,640,512]{2,1,0:T(8,128)(2,1)}, u32[]{:S(2)}, u32[]{:S(2)}) async-start(bf16[8,640,512]{2,1,0:T(8,128)(2,1)} %bitcast.95), calls=%async_computation.3 | async-start | bytes 10485760 | tf_op jit(solution)/shard_map/all_to_all | solution.py:86
  188.1 21.4 %copy-start = (bf16[1024,512]{1,0:T(8,128)(2,1)}, bf16[1024,512]{1,0:T(8,128)(2,1)S(1)}, u32[]{:S(2)}) copy-start(bf16[1024,512]{1,0:T(8,128)(2,1)S(1)} %fusion.4) | copy-start | bytes 3145732
  304.1 4.8 copy-start.4
  304.1 5.1 copy-start.5
  304.1 121.3 %all-to-all-start.5 = ((bf16[8,640,512]{2,1,0:T(8,128)(2,1)}), bf16[8,640,512]{2,1,0:T(8,128)(2,1)}, u32[]{:S(2)}, u32[]{:S(2)}) async-start(bf16[8,640,512]{2,1,0:T(8,128)(2,1)} %bitcast.94), calls=%async_computation.5 | async-start | bytes 10485760 | tf_op jit(solution)/shard_map/all_to_all | solution.py:89
  341.2 7.1 %copy-start.6 = (bf16[1024,512,1]{1,0,2:T(8,128)(2,1)S(1)}, bf16[1024,512,1]{1,0,2:T(8,128)(2,1)}, u32[]{:S(2)}) copy-start(bf16[1024,512,1]{1,0,2:T(8,128)(2,1)} %fusion.34) | copy-start | bytes 3145732
  471.4 9.5 %copy-start.11 = (bf16[1024]{0:T(1024)(128)(2,1)}, bf16[1024]{0:T(1024)(128)(2,1)S(1)}, u32[]{:S(2)}) copy-start(bf16[1024]{0:T(1024)(128)(2,1)S(1)} %multiply_convert_fusion) | copy-start | bytes 6148
  472.7 9.1 %all-to-all-start.6 = ((bf16[8,2,256]{2,1,0:T(2,128)(2,1)}), bf16[8,2,256]{2,1,0:T(2,128)(2,1)S(1)}, u32[]{:S(2)}, u32[]{:S(2)}) async-start(bf16[8,2,256]{2,1,0:T(2,128)(2,1)} %broadcast_select_fusion.6), calls=%async_computation.6 | async-start | bytes 16384 | tf_op jit(solution)/shard_map/all_to_all | solution.py:116
  481.8 75.7 %all-to-all-start.1 = ((bf16[16,256,512]{2,1,0:T(8,128)(2,1)}), bf16[16,256,512]{2,1,0:T(8,128)(2,1)}, u32[]{:S(2)}, u32[]{:S(2)}) async-start(bf16[16,256,512]{2,1,0:T(8,128)(2,1)} %broadcast_select_fusion.3), calls=%async_computation.1 | async-start | bytes 8388608 | tf_op jit(solution)/shard_map/all_to_all | solution.py:127
  487.4 74.8 %all-gather.2.cloned.1.call-start = ((), (), s32[]{:S(2)}) async-start(), calls=%async_computation.7 | async-start | bytes 3145728 | tf_op jit(solution)/shard_map/all_gather | solution.py:133
  488.3 74.0 %copy-start.12 = (f32[1024]{0:T(1024)}, f32[1024]{0:T(1024)S(1)}, u32[]{:S(2)}) copy-start(f32[1024]{0:T(1024)S(1)} %broadcast_multiply_fusion) | copy-start | bytes 12292
Sparse Core Ops, SparseCore 0:
  489.8 56.6 all-gather.1
where the time goes:
time: 579 us; the launch traced here: 578 us
  waiting for transfers between devices  295 us (51%)
  local copies, waits for them, and re-layouts  158 us (27%)
  other arithmetic  42.1 us (7%)
  starting transfers between devices  34.8 us (6%)
  matrix products  20.3 us (4%)
  between operations  14.6 us (3%)
  blocking collectives  13.5 us (2%)
    all_to_all x1, waiting for transfers between devices, on_device(): lax.all_to_all(answer(fwd_asked, tgt_normed), ('shard', 'rep'), split_axi...  87.5 us
    all_to_all x1, waiting for transfers between devices, on_device(): lax.all_to_all(answer(bwd_asked, src_normed), ('shard', 'rep'), split_axi...  70.9 us
    all_to_all x1, waiting for transfers between devices, on_device(): lax.all_to_all(listed_blocks, 'width', split_axis=0, concat_axis=2, tiled...  68.6 us
    all_to_all x1, waiting for transfers between devices, on_device(): lax.all_to_all(jnp.take(local_blocks, peer_ids, axis=0), ('shard', 'rep')...  65.4 us
    gather x2, local copies, waits for them, and re-layouts, answer(): picked = jnp.take(local_rows, asked.reshape(-1), axis=0)  42.7 us
    gather x2, local copies, waits for them, and re-layouts, neighbour_terms(): jnp.take(flat, places, axis=0).reshape(normed.shape[0], K, flat.shape[1])  41.1 us
    scatter x2, local copies, waits for them, and re-layouts, request_table(): jnp.zeros((owners * slot_count,), jnp.int32).at[places]  32.2 us
    select_n x2, other arithmetic, answer(): picked = jnp.take(local_rows, asked.reshape(-1), axis=0)  14.3 us
  transfers between devices with their start and end apart: 8, of which 6 were waited for; matrix products, arithmetic and copies ran while one was open for 26% of the time, Pallas kernels for 0%

commit v1 on v0

v1 whole, which is shorter than its diff:
```python
import functools
import math

import jax
import jax.numpy as jnp
from jax import lax
from jax.experimental import pallas as pl
from jax.experimental.pallas import tpu as pltpu
from jax.sharding import PartitionSpec as P

D = 1024
K = 4
CAND = 16
BLOCK = 256
EPS = 1e-05
LANES = 128
TILE = 256
MIB = 1 << 20


def normalize_kernel(*refs):
    chunks, out_ref = refs[:-1], refs[-1]
    cols = chunks[0].shape[1]
    values = [ref[...].astype(jnp.float32) for ref in chunks]
    total = sum(jnp.sum(v * v, axis=1, keepdims=True) for v in values)
    scale = lax.rsqrt(total / D + EPS)
    for d, v in enumerate(values):
        out_ref[:, d * cols : (d + 1) * cols] = (v * scale).astype(jnp.bfloat16)


def normalize_rows(chunks):
    rows, cols = chunks[0].shape
    return pl.pallas_call(
        normalize_kernel,
        grid=(rows // TILE,),
        in_specs=[pl.BlockSpec((TILE, cols), lambda i: (i, 0))] * len(chunks),
        out_specs=pl.BlockSpec((TILE, cols * len(chunks)), lambda i: (i, 0)),
        out_shape=jax.ShapeDtypeStruct((rows, cols * len(chunks)), jnp.bfloat16),
        compiler_params=pltpu.CompilerParams(vmem_limit_bytes=16 * MIB),
        cost_estimate=pl.CostEstimate(
            flops=4 * rows * D, bytes_accessed=4 * rows * D, transcendentals=rows
        ),
    )(*chunks)


def dots_kernel(reps, width, pairs, sc_ref, *refs):
    fidx_ref, bidx_ref = refs[:2]
    src_refs = refs[2 : 2 + reps]
    chunk_refs = refs[2 + reps : 2 + reps + width * pairs]
    p_in, f_in, s_ref, p_ref, f_ref, tgt, picks, bsum = refs[2 + reps + width * pairs :]
    del p_in
    step = pl.program_id(0)
    rows, cols = chunk_refs[0].shape
    length = sc_ref[3]

    @pl.when(step == 0)
    def _():
        values = []
        for d in range(width):
            value = chunk_refs[d][...].astype(jnp.float32)
            for other in range(1, pairs):
                value = value + chunk_refs[other * width + d][...].astype(jnp.float32)
            values.append(value)
        total = sum(jnp.sum(v * v, axis=1, keepdims=True) for v in values)
        scale = lax.rsqrt(total / D + EPS)
        for d, v in enumerate(values):
            tgt[:, d * cols : (d + 1) * cols] = (v * scale).astype(jnp.bfloat16)
        bidx = bidx_ref[...]
        for e in range(reps):
            place = bidx - sc_ref[4 + e]
            hit = (place >= 0) & (place < length)
            place = jnp.sum(jnp.where(hit, place + 1, 0), axis=1, keepdims=True) - 1
            picks[e] = jnp.broadcast_to(place, (rows, LANES))
        bsum[...] = jnp.zeros_like(bsum)

    row_ids = lax.broadcasted_iota(jnp.int32, (rows, TILE), 0)
    lane_ids = lax.broadcasted_iota(jnp.int32, (rows, LANES), 1)
    for e in range(reps):
        dots = lax.dot_general(
            tgt[...],
            src_refs[e][...],
            (((1,), (1,)), ((), ())),
            preferred_element_type=jnp.float32,
        )
        s_ref[e] = dots
        place = fidx_ref[e] - sc_ref[0]
        hit = (place >= 0) & (place < rows)
        place = jnp.sum(jnp.where(hit, place + 1, 0), axis=0, keepdims=True) - 1
        picked = jnp.sum(jnp.where(row_ids == place, dots, 0.0), axis=0, keepdims=True)
        f_ref[e] = f_in[e] + picked
        for g in range(TILE // LANES):
            first = step * TILE + g * LANES
            hit = picks[e] - first == lane_ids
            bsum[...] += jnp.where(hit, dots[:, g * LANES : (g + 1) * LANES], 0.0)

    @pl.when(step == pl.num_programs(0) - 1)
    def _():
        p_ref[0] = jnp.sum(jnp.transpose(bsum[...]), axis=0, keepdims=True)


def dots_call(scalars, fidx, bidx, sources, chunks, bwd_parts, fwd_parts):
    reps = len(sources)
    pairs, width = len(chunks), len(chunks[0])
    length = sources[0].shape[0]
    rows, cols = chunks[0][0].shape
    n_in = 2 + reps + width * pairs
    flat = [c for pair in chunks for c in pair]
    return pl.pallas_call(
        functools.partial(dots_kernel, reps, width, pairs),
        grid_spec=pltpu.PrefetchScalarGridSpec(
            num_scalar_prefetch=1,
            grid=(length // TILE,),
            in_specs=[
                pl.BlockSpec((reps, K, TILE), lambda j, sc: (0, 0, j)),
                pl.BlockSpec((rows, K), lambda j, sc: (sc[1], 0)),
            ]
            + [pl.BlockSpec((TILE, D), lambda j, sc: (j, 0))] * reps
            + [pl.BlockSpec((rows, cols), lambda j, sc: (0, 0))] * (width * pairs)
            + [
                pl.BlockSpec((1, 1, rows), lambda j, sc: (sc[2], 0, 0)),
                pl.BlockSpec((reps, 1, TILE), lambda j, sc: (0, 0, j)),
            ],
            out_specs=[
                pl.BlockSpec((reps, rows, TILE), lambda j, sc: (0, 0, j)),
                pl.BlockSpec((1, 1, rows), lambda j, sc: (sc[2], 0, 0)),
                pl.BlockSpec((reps, 1, TILE), lambda j, sc: (0, 0, j)),
            ],
            scratch_shapes=[
                pltpu.VMEM((rows, D), jnp.bfloat16),
                pltpu.VMEM((reps, rows, LANES), jnp.int32),
                pltpu.VMEM((rows, LANES), jnp.float32),
            ],
        ),
        out_shape=[
            jax.ShapeDtypeStruct((reps, rows, length), jnp.float32),
            jax.ShapeDtypeStruct(bwd_parts.shape, jnp.float32),
            jax.ShapeDtypeStruct(fwd_parts.shape, jnp.float32),
        ],
        input_output_aliases={n_in + 1: 1, n_in + 2: 2},
        compiler_params=pltpu.CompilerParams(vmem_limit_bytes=24 * MIB),
        cost_estimate=pl.CostEstimate(
            flops=2 * reps * length * rows * D,
            bytes_accessed=reps * length * (2 * D + 4 * rows) + 2 * rows * D,
            transcendentals=rows,
        ),
    )(scalars, fidx, bidx, *sources, *flat, bwd_parts, fwd_parts)


def margin_kernel(slots, terms, reps, sc_ref, *refs):
    s_refs = refs[:slots]
    p_refs = refs[slots : slots + terms]
    f_ref, e_ref, means, halves = refs[slots + terms :]
    step = pl.program_id(0)
    rows = s_refs[0].shape[1]
    parts = rows // BLOCK

    @pl.when(step == 0)
    def _():
        total = p_refs[0][:, 0, :]
        for ref in p_refs[1:]:
            total = total + ref[:, 0, :]
        mean = (total / (K * math.sqrt(D))).astype(jnp.bfloat16).astype(jnp.float32)
        means[...] = mean
        for t in range(slots):
            row = means[pl.ds(sc_ref[2 + t], 1), :]
            halves[t] = 0.5 * jnp.transpose(jnp.broadcast_to(row, (LANES, rows)))

    for e in range(reps):
        at = lax.rem(sc_ref[0] + e, reps)
        for t in range(slots):
            for g in range(TILE // LANES):
                lanes = slice(g * LANES, (g + 1) * LANES)
                margin = s_refs[t][e, :, lanes] * (1.0 / math.sqrt(D)) - halves[t]
                for b in range(parts):
                    top = jnp.max(margin[b * BLOCK : (b + 1) * BLOCK], axis=0, keepdims=True)
                    e_ref[at, t * parts + b : t * parts + b + 1, lanes] = top
        e_ref[at, slots * parts : slots * parts + 1, :] = f_ref[e]
        start = pl.multiple_of(lax.rem(step, rows // TILE) * TILE, LANES)
        e_ref[at, slots * parts + 1 : slots * parts + 2, :] = means[
            pl.ds(sc_ref[1], 1), pl.ds(start, TILE)
        ]


def margin_call(scalars, dots, bwd_terms, fwd_parts):
    slots, terms = len(dots), len(bwd_terms)
    reps, rows, length = dots[0].shape
    lines = slots * (rows // BLOCK) + 2
    lines = -(-lines // 8) * 8
    planes = bwd_terms[0].shape[0]
    return pl.pallas_call(
        functools.partial(margin_kernel, slots, terms, reps),
        grid_spec=pltpu.PrefetchScalarGridSpec(
            num_scalar_prefetch=1,
            grid=(length // TILE,),
            in_specs=[pl.BlockSpec((reps, rows, TILE), lambda j, sc: (0, 0, j))] * slots
            + [pl.BlockSpec(bwd_terms[0].shape, lambda j, sc: (0, 0, 0))] * terms
            + [pl.BlockSpec((reps, 1, TILE), lambda j, sc: (0, 0, j))],
            out_specs=pl.BlockSpec((reps, lines, TILE), lambda j, sc: (0, 0, j)),
            scratch_shapes=[
                pltpu.VMEM((planes, rows), jnp.float32),
                pltpu.VMEM((slots, rows, LANES), jnp.float32),
            ],
        ),
        out_shape=jax.ShapeDtypeStruct((reps, lines, length), jnp.float32),
        compiler_params=pltpu.CompilerParams(vmem_limit_bytes=48 * MIB),
        cost_estimate=pl.CostEstimate(
            flops=3 * slots * reps * rows * length,
            bytes_accessed=4 * slots * reps * rows * length,
            transcendentals=0,
        ),
    )(scalars, *dots, *bwd_terms, fwd_parts)


def final_kernel(width, reps, planes, slots, parts, sc_ref, list_ref, g_ref, best_ref, fwd_ref, bwd_ref):
    shard, wide, rep = sc_ref[0], sc_ref[1], sc_ref[2]
    fwd_line = slots * parts
    fwd = g_ref[0, 0, fwd_line : fwd_line + 1, :]
    for g in range(1, width * reps):
        fwd = fwd + g_ref[g, 0, fwd_line : fwd_line + 1, :]
    fwd = fwd / (K * math.sqrt(D))
    fwd_ref[...] = fwd
    rows = parts * BLOCK
    for v in range(width):
        part = g_ref[v * reps + rep, 0, fwd_line + 1 : fwd_line + 2, 0:rows]
        bwd_ref[:, v * rows : (v + 1) * rows] = part.astype(jnp.bfloat16)
    half = 0.5 * fwd
    per_width = best_ref.shape[0]
    both = (planes - 1) // 2
    for c in range(per_width):
        block = list_ref[wide * per_width + c]
        per_dev = parts * width
        holder = block // per_dev
        local = block - holder * per_dev
        plane = holder // reps
        peer = (local // parts) * reps + holder - plane * reps
        hops = jnp.abs(shard - plane)
        near = 2 * hops - 1 + jnp.where(plane > shard, 1, 0)
        slot = jnp.where(hops == 0, 0, jnp.where(hops <= both, near, both + hops))
        line = slot * parts + local - (local // parts) * parts
        best_ref[c : c + 1, :] = g_ref[peer, 0, pl.ds(line, 1), :] - half


def final_call(scalars, own_list, gathered, width, reps, planes, slots, parts):
    lines, length = gathered.shape[2:]
    per_width = CAND // width
    return pl.pallas_call(
        functools.partial(final_kernel, width, reps, planes, slots, parts),
        grid_spec=pltpu.PrefetchScalarGridSpec(
            num_scalar_prefetch=2,
            grid=(1,),
            in_specs=[
                pl.BlockSpec((width * reps, 1, lines, length), lambda j, sc, ls: (0, sc[2], 0, 0))
            ],
            out_specs=[
                pl.BlockSpec((per_width, length), lambda j, sc, ls: (0, 0)),
                pl.BlockSpec((1, length), lambda j, sc, ls: (0, 0)),
                pl.BlockSpec((1, length), lambda j, sc, ls: (0, 0)),
            ],
        ),
        out_shape=[
            jax.ShapeDtypeStruct((per_width, length), jnp.float32),
            jax.ShapeDtypeStruct((1, length), jnp.float32),
            jax.ShapeDtypeStruct((1, length), jnp.bfloat16),
        ],
        compiler_params=pltpu.CompilerParams(vmem_limit_bytes=16 * MIB),
    )(scalars, own_list, gathered)


def on_device(source_vecs, target_vecs, fwd_owner, fwd_row, bwd_owner, bwd_row, cand_lists):
    reps = lax.axis_size("rep")
    planes = lax.axis_size("shard")
    width = lax.axis_size("width")
    shard = lax.axis_index("shard")
    wide = lax.axis_index("width")
    rep = lax.axis_index("rep")
    length = source_vecs.shape[0]
    rows = length // width
    parts = rows // BLOCK

    def part_of(values, index):
        return lax.dynamic_slice_in_dim(values, index * rows, rows, 0)

    def shift(values, axis, count, by):
        return lax.ppermute(values, axis, [((i + by) % count, i) for i in range(count)])

    own = [part_of(target_vecs, wide)]
    for d in range(1, width):
        sent = part_of(target_vecs, lax.rem(wide + width - d, width))
        own.append(shift(sent, "width", width, d))
    arrivals = {}
    for way, by in (("up", 1), ("down", -1)):
        arrivals[way, 0] = own
        for hop in range(1, planes):
            pairs = [(i, i + by) for i in range(planes) if 0 <= i + by * 1 < planes]
            pairs = [(i, j) for i, j in pairs if 0 <= j - by * hop < planes]
            arrivals[way, hop] = [
                lax.ppermute(c, "shard", pairs) for c in arrivals[way, hop - 1]
            ]
    sources = [source_vecs] + [shift(source_vecs, "width", width, d) for d in range(1, width)]
    src = [normalize_rows(sources)]
    for e in range(1, reps):
        src.append(shift(src[0], "rep", reps, e))

    fidx_own = jnp.transpose(fwd_owner * length + fwd_row)
    fidx = jnp.stack([fidx_own] + [shift(fidx_own, "rep", reps, e) for e in range(1, reps)])
    bidx = lax.all_gather(
        part_of(bwd_owner * length + bwd_row, wide), "shard", axis=0, tiled=True
    )
    bases = [(shard * reps + lax.rem(rep + e, reps)) * length for e in range(reps)]
    bwd_parts = jnp.zeros((planes + 1, 1, rows), jnp.float32)
    fwd_parts = jnp.zeros((reps, 1, length), jnp.float32)
    both = (planes - 1) // 2
    steps = [(shard, True, [own])]
    for hop in range(1, planes):
        below, above = shard - hop, shard + hop
        if hop <= both:
            steps.append((below, below >= 0, [arrivals["up", hop]]))
            steps.append((above, above < planes, [arrivals["down", hop]]))
        else:
            plane = jnp.where(below >= 0, below, above)
            valid = (below >= 0) | (above < planes)
            steps.append((plane, valid, [arrivals["up", hop], arrivals["down", hop]]))
    dots, kept = [], []
    for plane, valid, chunks in steps:
        base = (plane * reps + rep) * length + wide * rows
        place = jnp.clip(plane, 0, planes - 1)
        row = jnp.where(valid, plane, planes)
        far = -2 * planes * reps * length
        scalars = jnp.stack(
            [jnp.where(valid, base, -far), place, row, jnp.int32(length)] + bases
        ).astype(jnp.int32)
        out, bwd_parts, fwd_parts = dots_call(
            scalars, fidx, bidx, src, chunks, bwd_parts, fwd_parts
        )
        dots.append(out)
        kept.append(place)
    terms = [bwd_parts]
    if planes <= 4:
        for d in range(1, planes):
            terms.append(shift(terms[0], "shard", planes, d))
    else:
        terms = [lax.psum(terms[0], "shard")]
    scalars = jnp.stack([rep, shard] + kept).astype(jnp.int32)
    lines = margin_call(scalars, dots, terms, fwd_parts)
    gathered = lax.all_gather(lines, ("width", "rep"), axis=0, tiled=False)
    own_list = lax.dynamic_index_in_dim(cand_lists, shard, 0, keepdims=False)
    scalars = jnp.stack([shard, wide, rep]).astype(jnp.int32)
    best, fwd_mean, bwd_mean = final_call(
        scalars, own_list, gathered, width, reps, planes, len(dots), parts
    )
    return (jnp.transpose(best), fwd_mean.reshape(-1), bwd_mean.reshape(-1))


def solution(mesh):
    in_specs = (
        P(("groups", "shard", "rep"), "width"),
        P(("groups", "shard", "rep"), "width"),
        P(("groups", "shard", "rep"), None),
        P(("groups", "shard", "rep"), None),
        P(("groups", "shard", "rep"), None),
        P(("groups", "shard", "rep"), None),
        P("groups", None),
    )
    out_specs = (
        P(("groups", "shard", "rep"), "width"),
        P(("groups", "shard", "rep")),
        P(("groups", "shard", "rep")),
    )
    return jax.shard_map(
        on_device, mesh=mesh, in_specs=in_specs, out_specs=out_specs, check_vma=False
    )
```

time: 579 us -> 186 us (0.32)
  waiting for transfers between devices: 295 us -> 46 us
  local copies, waits for them, and re-layouts: 158 us -> 17 us
  Pallas kernels: 0 us -> 44.3 us
  other arithmetic: 42.1 us -> 0.7 us
  blocking collectives: 13.5 us -> 45.5 us
  matrix products: 20.3 us -> 0 us
  between operations: 14.6 us -> 1.1 us
    all_to_all x7 -> x0, waiting for transfers between devices: 294 us -> none  [the longest x1 87.5 us: on_device(): lax.all_to_all(answer(fwd_asked, tgt_normed), ('shard', 'rep'), split_axi...]
    gather x9 -> x0, local copies, waits for them, and re-layouts: 92.8 us -> none  [the longest x2 42.7 us: answer(): picked = jnp.take(local_rows, asked.reshape(-1), axis=0)]
    ppermute x0 -> x19, waiting for transfers between devices: none -> 46 us  [the longest x7 35.5 us: shift(): lax.ppermute(values, axis, [((i + by) % count, i) for i in range(count)])]
    all_gather x0 -> x2, blocking collectives: none -> 45.5 us  [the longest x1 38.3 us: on_device(): lax.all_gather(part_of(bwd_owner * length + bwd_row, wide), 'shard', axis...]
    pallas_call x0 -> x8, Pallas kernels: none -> 44.3 us  [the longest x5 33.9 us: dots_call(): pl.pallas_call(functools.partial(dots_kernel, reps, width, pairs), grid_s...]
    all_to_all x7 -> x0, starting transfers between devices: 34.7 us -> none  [the longest x1 6.33 us: on_device(): lax.all_to_all(fwd_table, ('shard', 'rep'), split_axis=0, concat_axis=0,...]
    select_n x13 -> x0, other arithmetic: 32.2 us -> none  [the longest x2 14.3 us: answer(): picked = jnp.take(local_rows, asked.reshape(-1), axis=0)]
    scatter x2 -> x0, local copies, waits for them, and re-layouts: 32.2 us -> none  [request_table(): jnp.zeros((owners * slot_count,), jnp.int32).at[places]]
  transfers between devices with their start and end apart: 8 -> 19, of which waited for: 6 -> 7; matrix products, arithmetic and copies ran while one was open for 26% -> 1% of each run, Pallas kernels for 0% -> 15%
where the time goes in v1:
time: 186 us; the launch traced here: 185 us
  waiting for transfers between devices  46 us (25%)
  blocking collectives  45.5 us (24%)
  Pallas kernels  44.3 us (24%)
  starting transfers between devices  30.1 us (16%)
  local copies, waits for them, and re-layouts  17 us (9%)
    all_gather x1, blocking collectives, on_device(): lax.all_gather(part_of(bwd_owner * length + bwd_row, wide), 'shard', axis...  38.3 us
    ppermute x7, waiting for transfers between devices, shift(): lax.ppermute(values, axis, [((i + by) % count, i) for i in range(count)])  35.5 us
    pallas_call x5, Pallas kernels, dots_call(): pl.pallas_call(functools.partial(dots_kernel, reps, width, pairs), grid_s...  33.9 us
    ppermute x12, starting transfers between devices, on_device(): lax.ppermute(c, 'shard', pairs)  20.8 us
    unnamed x29, local copies, waits for them, and re-layouts  15.2 us
    ppermute x12, waiting for transfers between devices, on_device(): lax.ppermute(c, 'shard', pairs)  10.6 us
    ppermute x7, starting transfers between devices, shift(): lax.ppermute(values, axis, [((i + by) % count, i) for i in range(count)])  9.31 us
    pallas_call x1, Pallas kernels, margin_call(): pl.pallas_call(functools.partial(margin_kernel, slots, terms, reps), grid...  8.14 us
  transfers between devices with their start and end apart: 19, of which 7 were waited for; matrix products, arithmetic and copies ran while one was open for 1% of the time, Pallas kernels for 15%

profile of v1, /device:TPU:0, one launch (start us, length us, event | category | flops | bytes accessed | tf_op | source)
XLA Modules:
  0.0 184.7 jit_solution(13128260467480053950)
XLA Ops:
  0.6 3.0 %collective-permute-start.1 = (bf16[1024,512]{1,0:T(8,128)(2,1)}, bf16[1024,512]{1,0:T(8,128)(2,1)S(1)}, u32[]{:S(2)}, u32[]{:S(2)}) collective-permute-start(bf16[1024,512]{1,0:T(8,128)(2,1)} %refs_0_.1), channel_id=1, source_target_pairs={{2,0},{0,2},{3,1},{1,3},{6,4},{4,6},{7,5},{5,7},{10,8},{8,10},{11,... | collective-permute-start | bytes 3145736 | tf_op jit(solution)/shard_map/ppermute | solution.py:284
  3.7 23.4 %collective-permute-done.1.refs_1_ = bf16[1024,512]{1,0:T(8,128)(2,1)S(1)} collective-permute-done((bf16[1024,512]{1,0:T(8,128)(2,1)}, bf16[1024,512]{1,0:T(8,128)(2,1)S(1)}, u32[]{:S(2)}, u32[]{:S(2)}) %collective-permute-start.1) | collective-permute-done | bytes 1048608 | tf_op jit(solution)/shard_map/ppermute | solution.py:284
  30.5 1.8 collective-permute-start.3
  32.6 4.3 %collective-permute-start.4 = (bf16[512,512]{1,0:T(8,128)(2,1)S(1)}, bf16[512,512]{1,0:T(8,128)(2,1)}, u32[]{:S(2)}, u32[]{:S(2)}) collective-permute-start(bf16[512,512]{1,0:T(8,128)(2,1)S(1)} %get-tuple-element.40.refs_4_), channel_id=1, source_target_pairs={{0,4},{4,8},{8,12},{1,5},{5,9},{9,13},{2,6},{6,10},{10,14},{3,7},{... | collective-permute-start | bytes 1572872 | tf_op jit(solution)/shard_map/ppermute | solution.py:297
  38.2 6.7 %collective-permute-done.3.refs_5_ = bf16[512,512]{1,0:T(8,128)(2,1)S(1)} collective-permute-done((bf16[512,512]{1,0:T(8,128)(2,1)S(1)}, bf16[512,512]{1,0:T(8,128)(2,1)S(1)}, u32[]{:S(2)}, u32[]{:S(2)}) %collective-permute-start.3) | collective-permute-done | bytes 524320 | tf_op jit(solution)/shard_map/ppermute | solution.py:284
  44.9 4.5 %collective-permute-start.5 = (bf16[512,512]{1,0:T(8,128)(2,1)S(1)}, bf16[512,512]{1,0:T(8,128)(2,1)}, u32[]{:S(2)}, u32[]{:S(2)}) collective-permute-start(bf16[512,512]{1,0:T(8,128)(2,1)S(1)} %collective-permute-done.3.refs_5_), channel_id=1, source_target_pairs={{0,4},{4,8},{8,12},{1,5},{5,9},{9,13},{2,6},{6,10},{10,14},{3,7},{... | collective-permute-start | bytes 1572872 | tf_op jit(solution)/shard_map/ppermute | solution.py:297
  49.4 1.3 collective-permute-start.7
  51.5 1.5 collective-permute-start.8
  53.0 1.3 collective-permute-start.10
  54.3 5.5 %collective-permute-done.5.refs_5_ = bf16[512,512]{1,0:T(8,128)(2,1)} collective-permute-done((bf16[512,512]{1,0:T(8,128)(2,1)S(1)}, bf16[512,512]{1,0:T(8,128)(2,1)}, u32[]{:S(2)}, u32[]{:S(2)}) %collective-permute-start.5) | collective-permute-done | bytes 524320 | tf_op jit(solution)/shard_map/ppermute | solution.py:297
  59.7 1.4 collective-permute-start.9
  61.2 5.1 %collective-permute-done.7.refs_5_ = bf16[512,512]{1,0:T(8,128)(2,1)} collective-permute-done((bf16[512,512]{1,0:T(8,128)(2,1)S(1)}, bf16[512,512]{1,0:T(8,128)(2,1)}, u32[]{:S(2)}, u32[]{:S(2)}) %collective-permute-start.7) | collective-permute-done | bytes 524320 | tf_op jit(solution)/shard_map/ppermute | solution.py:297
  68.3 38.3 %all_gather.9.refs_1_ = s32[2048,4]{1,0:T(8,128)S(1)} all-gather(s32[512,4]{1,0:T(8,128)S(1)} %copy.41), channel_id=1, replica_groups=mesh['groups'=2,'shard'=4,'width'=2,'rep'=2] {'shard'}, dimensions={0}, use_global_device_ids=true | all-gather | bytes 40960 | tf_op jit(solution)/shard_map/all_gather | solution.py:306
  107.4 1.3 collective-permute-start.14
  109.4 1.3 collective-permute-start.15
  111.8 6.5 %shard_map.95 = (f32[2,512,1024]{2,1,0:T(8,128)S(1)}, f32[5,1,512]{2,1,0:T(1,128)S(1)}, f32[2,1,1024]{2,1,0:T(1,128)S(1)}) custom-call(s32[6]{0:T(128)S(1)} %stack.116.sc_ref, s32[2,4,1024]{2,1,0:T(4,128)S(1)} %pad_add_fusion.refs_0_, s32[2048,4]{1,0:T(8,128)S(1)} %all_gather.9.refs_1_, ...), custom_call_target="tpu_custom_call", output_to_operand_aliasing={{1}: (7, {}), {2}: (8, {})} | custom-call | flops 2147483648 | bytes 9437184 | tf_op jit(solution)/shard_map/pallas_call | solution.py:108
  118.3 2.0 %copy-done.1 = f32[2,512,1024]{2,1,0:T(8,128)} copy-done((f32[2,512,1024]{2,1,0:T(8,128)}, f32[2,512,1024]{2,1,0:T(8,128)S(1)}, u32[]{:S(2)}) %copy-start.1) | copy-done | bytes 4194328
  120.3 6.8 %shard_map.96 = (f32[2,512,1024]{2,1,0:T(8,128)S(1)}, f32[5,1,512]{2,1,0:T(1,128)S(1)}, f32[2,1,1024]{2,1,0:T(1,128)S(1)}) custom-call(s32[6]{0:T(128)S(1)} %stack.122.sc_ref, s32[2,4,1024]{2,1,0:T(4,128)S(1)} %pad_add_fusion.refs_0_, s32[2048,4]{1,0:T(8,128)S(1)} %all_gather.9.refs_1_, ...), custom_call_target="tpu_custom_call", output_to_operand_aliasing={{1}: (7, {}), {2}: (8, {})} | custom-call | flops 2147483648 | bytes 9437184 | tf_op jit(solution)/shard_map/pallas_call | solution.py:108
  127.1 2.0 %copy-done.3 = f32[2,512,1024]{2,1,0:T(8,128)} copy-done((f32[2,512,1024]{2,1,0:T(8,128)}, f32[2,512,1024]{2,1,0:T(8,128)S(1)}, u32[]{:S(2)}) %copy-start.3) | copy-done | bytes 4194328
  129.1 6.7 %shard_map.97 = (f32[2,512,1024]{2,1,0:T(8,128)S(1)}, f32[5,1,512]{2,1,0:T(1,128)S(1)}, f32[2,1,1024]{2,1,0:T(1,128)S(1)}) custom-call(s32[6]{0:T(128)S(1)} %stack.125.sc_ref, s32[2,4,1024]{2,1,0:T(4,128)S(1)} %pad_add_fusion.refs_0_, s32[2048,4]{1,0:T(8,128)S(1)} %all_gather.9.refs_1_, ...), custom_call_target="tpu_custom_call", output_to_operand_aliasing={{1}: (7, {}), {2}: (8, {})} | custom-call | flops 2147483648 | bytes 9437184 | tf_op jit(solution)/shard_map/pallas_call | solution.py:108
  135.8 2.0 %copy-done.4 = f32[2,512,1024]{2,1,0:T(8,128)} copy-done((f32[2,512,1024]{2,1,0:T(8,128)}, f32[2,512,1024]{2,1,0:T(8,128)S(1)}, u32[]{:S(2)}) %copy-start.4) | copy-done | bytes 4194328
  137.8 7.3 %shard_map.98 = (f32[2,512,1024]{2,1,0:T(8,128)S(1)}, f32[5,1,512]{2,1,0:T(1,128)S(1)}, f32[2,1,1024]{2,1,0:T(1,128)S(1)}) custom-call(s32[6]{0:T(128)S(1)} %stack.128.sc_ref, s32[2,4,1024]{2,1,0:T(4,128)S(1)} %pad_add_fusion.refs_0_, s32[2048,4]{1,0:T(8,128)S(1)} %all_gather.9.refs_1_, ...), custom_call_target="tpu_custom_call", output_to_operand_aliasing={{1}: (9, {}), {2}: (10, {})} | custom-call | flops 2147483648 | bytes 9437184 | tf_op jit(solution)/shard_map/pallas_call | solution.py:108
  145.1 1.9 %copy-done.5 = f32[2,512,1024]{2,1,0:T(8,128)} copy-done((f32[2,512,1024]{2,1,0:T(8,128)}, f32[2,512,1024]{2,1,0:T(8,128)S(1)}, u32[]{:S(2)}) %copy-start.5) | copy-done | bytes 4194328
  147.0 6.6 %shard_map.99 = (f32[2,512,1024]{2,1,0:T(8,128)S(1)}, f32[5,1,512]{2,1,0:T(1,128)S(1)}, f32[2,1,1024]{2,1,0:T(1,128)S(1)}) custom-call(s32[6]{0:T(128)S(1)} %stack.131.sc_ref, s32[2,4,1024]{2,1,0:T(4,128)S(1)} %pad_add_fusion.refs_0_, s32[2048,4]{1,0:T(8,128)S(1)} %all_gather.9.refs_1_, ...), custom_call_target="tpu_custom_call", output_to_operand_aliasing={{1}: (9, {}), {2}: (10, {})} | custom-call | flops 2147483648 | bytes 9437184 | tf_op jit(solution)/shard_map/pallas_call | solution.py:108
  153.7 2.0 %copy-done.6 = f32[2,512,1024]{2,1,0:T(8,128)} copy-done((f32[2,512,1024]{2,1,0:T(8,128)}, f32[2,512,1024]{2,1,0:T(8,128)S(1)}, u32[]{:S(2)}) %copy-start.6) | copy-done | bytes 4194328
  156.5 3.3 %collective-permute-start.17 = (f32[5,1,512]{2,1,0:T(1,128)S(1)}, f32[5,1,512]{2,1,0:T(1,128)S(1)}, u32[]{:S(2)}, u32[]{:S(2)}) collective-permute-start(f32[5,1,512]{2,1,0:T(1,128)S(1)} %get-tuple-element.34.refs_5_), channel_id=1, source_target_pairs={{8,0},{12,4},{0,8},{4,12},{9,1},{13,5},{1,9},{5,13},{10,2},{14,6},... | collective-permute-start | bytes 30728 | tf_op jit(solution)/shard_map/ppermute | solution.py:284
  160.0 1.6 collective-permute-done.17.refs_7_
  161.6 3.7 %collective-permute-done.18.refs_8_ = f32[5,1,512]{2,1,0:T(1,128)S(1)} collective-permute-done((f32[5,1,512]{2,1,0:T(1,128)S(1)}, f32[5,1,512]{2,1,0:T(1,128)S(1)}, u32[]{:S(2)}, u32[]{:S(2)}) %collective-permute-start.18) | collective-permute-done | bytes 10272 | tf_op jit(solution)/shard_map/ppermute | solution.py:284
  165.3 2.2 %copy-done.2 = f32[2,512,1024]{2,1,0:T(8,128)S(1)} copy-done((f32[2,512,1024]{2,1,0:T(8,128)S(1)}, f32[2,512,1024]{2,1,0:T(8,128)}, u32[]{:S(2)}) %copy-start.2) | copy-done | bytes 4194328
  167.5 8.1 %shard_map.100 = f32[2,16,1024]{2,1,0:T(8,128)S(1)} custom-call(s32[7]{0:T(128)S(1)} %stack.112.sc_ref, f32[2,512,1024]{2,1,0:T(8,128)S(1)} %copy-done.2, f32[2,512,1024]{2,1,0:T(8,128)} %copy-done.3, f32[2,512,1024]{2,1,0:T(8,128)} %copy-done.4, f32[2,512,1024]{2,1,0:T(8,128)} %copy-done.5, f32[2,512,1024]{2,1,0:T(8,128)} %copy-done.6, ...), custom_call_target="tpu_custom_call" | custom-call | flops 15728640 | bytes 20971520 | tf_op jit(solution)/shard_map/pallas_call | solution.py:190
  175.6 7.2 %all-gather = f32[8,16,1024]{2,1,0:T(8,128)S(1)} all-gather(f32[2,16,1024]{2,1,0:T(8,128)S(1)} %shard_map.100), channel_id=2, replica_groups=mesh['groups'=2,'shard'=4,'width'=2,'rep'=2] {'width','rep'}, dimensions={0}, use_global_device_ids=true | all-gather | bytes 655360 | tf_op jit(solution)/shard_map/all_gather | solution.py:345
  182.8 1.3 shard_map.101
  (60 shorter events, 11.9 us)
Async XLA Ops:
  0.6 159.2 %copy-start = (s32[4,16]{1,0:T(4,128)S(1)}, s32[4,16]{1,0:T(4,128)}, u32[]{:S(2)}) copy-start(s32[4,16]{1,0:T(4,128)} %param.13) | copy-start | bytes 772
  0.6 26.4 %collective-permute-start.1 = (bf16[1024,512]{1,0:T(8,128)(2,1)}, bf16[1024,512]{1,0:T(8,128)(2,1)S(1)}, u32[]{:S(2)}, u32[]{:S(2)}) collective-permute-start(bf16[1024,512]{1,0:T(8,128)(2,1)} %refs_0_.1), channel_id=1, source_target_pairs={{2,0},{0,2},{3,1},{1,3},{6,4},{4,6},{7,5},{5,7},{10,8},{8,10},{11,... | collective-permute-start | bytes 3145736 | tf_op jit(solution)/shard_map/ppermute | solution.py:284
  27.0 1.2 copy-start.7
  28.2 4.1 %copy-start.10 = (s32[1024,4]{0,1:T(4,128)S(1)}, s32[1024,4]{0,1:T(4,128)}, u32[]{:S(2)}) copy-start(s32[1024,4]{0,1:T(4,128)} %param.10) | copy-start | bytes 49156
  28.2 4.1 %copy-start.11 = (s32[1024,4]{0,1:T(4,128)S(1)}, s32[1024,4]{0,1:T(4,128)}, u32[]{:S(2)}) copy-start(s32[1024,4]{0,1:T(4,128)} %param.9) | copy-start | bytes 49156
  28.2 39.4 %copy-start.12 = (s32[1024,4]{0,1:T(4,128)S(1)}, s32[1024,4]{0,1:T(4,128)}, u32[]{:S(2)}) copy-start(s32[1024,4]{0,1:T(4,128)} %param.12) | copy-start | bytes 49156
  28.3 39.4 %copy-start.13 = (s32[1024,4]{0,1:T(4,128)S(1)}, s32[1024,4]{0,1:T(4,128)}, u32[]{:S(2)}) copy-start(s32[1024,4]{0,1:T(4,128)} %param.11) | copy-start | bytes 49156
  29.1 81.6 %collective-permute-start.2 = (bf16[1024,1024]{1,0:T(8,128)(2,1)S(1)}, bf16[1024,1024]{1,0:T(8,128)(2,1)}, u32[]{:S(2)}, u32[]{:S(2)}) collective-permute-start(bf16[1024,1024]{1,0:T(8,128)(2,1)S(1)} %shard_map.94.refs_2_), channel_id=1, source_target_pairs={{1,0},{0,1},{3,2},{2,3},{5,4},{4,5},{7,6},{6,7},{9,8},{8,9},{11,10... | collective-permute-start | bytes 6291464 | tf_op jit(solution)/shard_map/ppermute | solution.py:284
  30.5 14.4 %collective-permute-start.3 = (bf16[512,512]{1,0:T(8,128)(2,1)S(1)}, bf16[512,512]{1,0:T(8,128)(2,1)S(1)}, u32[]{:S(2)}, u32[]{:S(2)}) collective-permute-start(bf16[512,512]{1,0:T(8,128)(2,1)S(1)} %get-tuple-element.39), channel_id=1, source_target_pairs={{2,0},{0,2},{3,1},{1,3},{6,4},{4,6},{7,5},{5,7},{10,8},{8,10},{11,... | collective-permute-start | bytes 1572872 | tf_op jit(solution)/shard_map/ppermute | solution.py:284
  32.3 17.1 %collective-permute-start = (s32[4,1024]{1,0:T(4,128)S(1)}, s32[4,1024]{1,0:T(4,128)S(1)}, u32[]{:S(2)}, u32[]{:S(2)}) collective-permute-start(s32[4,1024]{1,0:T(4,128)S(1)} %get-tuple-element.42), channel_id=1, source_target_pairs={{1,0},{0,1},{3,2},{2,3},{5,4},{4,5},{7,6},{6,7},{9,8},{8,9},{11,10... | collective-permute-start | bytes 49160 | tf_op jit(solution)/shard_map/ppermute | solution.py:284
  32.6 18.9 %collective-permute-start.4 = (bf16[512,512]{1,0:T(8,128)(2,1)S(1)}, bf16[512,512]{1,0:T(8,128)(2,1)}, u32[]{:S(2)}, u32[]{:S(2)}) collective-permute-start(bf16[512,512]{1,0:T(8,128)(2,1)S(1)} %get-tuple-element.40.refs_4_), channel_id=1, source_target_pairs={{0,4},{4,8},{8,12},{1,5},{5,9},{9,13},{2,6},{6,10},{10,14},{3,7},{... | collective-permute-start | bytes 1572872 | tf_op jit(solution)/shard_map/ppermute | solution.py:297
  36.9 16.1 %collective-permute-start.6 = (bf16[512,512]{1,0:T(8,128)(2,1)S(1)}, bf16[512,512]{1,0:T(8,128)(2,1)S(1)}, u32[]{:S(2)}, u32[]{:S(2)}) collective-permute-start(bf16[512,512]{1,0:T(8,128)(2,1)S(1)} %get-tuple-element.40.refs_4_), channel_id=1, source_target_pairs={{4,0},{8,4},{12,8},{5,1},{9,5},{13,9},{6,2},{10,6},{14,10},{7,3},{... | collective-permute-start | bytes 1572872 | tf_op jit(solution)/shard_map/ppermute | solution.py:297
  44.9 14.9 %collective-permute-start.5 = (bf16[512,512]{1,0:T(8,128)(2,1)S(1)}, bf16[512,512]{1,0:T(8,128)(2,1)}, u32[]{:S(2)}, u32[]{:S(2)}) collective-permute-start(bf16[512,512]{1,0:T(8,128)(2,1)S(1)} %collective-permute-done.3.refs_5_), channel_id=1, source_target_pairs={{0,4},{4,8},{8,12},{1,5},{5,9},{9,13},{2,6},{6,10},{10,14},{3,7},{... | collective-permute-start | bytes 1572872 | tf_op jit(solution)/shard_map/ppermute | solution.py:297
  49.4 16.8 %collective-permute-start.7 = (bf16[512,512]{1,0:T(8,128)(2,1)S(1)}, bf16[512,512]{1,0:T(8,128)(2,1)}, u32[]{:S(2)}, u32[]{:S(2)}) collective-permute-start(bf16[512,512]{1,0:T(8,128)(2,1)S(1)} %collective-permute-done.3.refs_5_), channel_id=1, source_target_pairs={{4,0},{8,4},{12,8},{5,1},{9,5},{13,9},{6,2},{10,6},{14,10},{7,3},{... | collective-permute-start | bytes 1572872 | tf_op jit(solution)/shard_map/ppermute | solution.py:297
  51.5 55.2 %collective-permute-start.8 = (bf16[512,512]{1,0:T(8,128)(2,1)}, bf16[512,512]{1,0:T(8,128)(2,1)}, u32[]{:S(2)}, u32[]{:S(2)}) collective-permute-start(bf16[512,512]{1,0:T(8,128)(2,1)} %collective-permute-done.4.refs_4_), channel_id=1, source_target_pairs={{4,8},{8,12},{5,9},{9,13},{6,10},{10,14},{7,11},{11,15},{20,24},{2... | collective-permute-start | bytes 1572872 | tf_op jit(solution)/shard_map/ppermute | solution.py:297
  53.0 54.4 %collective-permute-start.10 = (bf16[512,512]{1,0:T(8,128)(2,1)S(1)}, bf16[512,512]{1,0:T(8,128)(2,1)}, u32[]{:S(2)}, u32[]{:S(2)}) collective-permute-start(bf16[512,512]{1,0:T(8,128)(2,1)S(1)} %collective-permute-done.6.refs_4_), channel_id=1, source_target_pairs={{4,0},{8,4},{5,1},{9,5},{6,2},{10,6},{7,3},{11,7},{20,16},{24,20},... | collective-permute-start | bytes 1572872 | tf_op jit(solution)/shard_map/ppermute | solution.py:297
  59.7 48.9 %collective-permute-start.9 = (bf16[512,512]{1,0:T(8,128)(2,1)}, bf16[512,512]{1,0:T(8,128)(2,1)}, u32[]{:S(2)}, u32[]{:S(2)}) collective-permute-start(bf16[512,512]{1,0:T(8,128)(2,1)} %collective-permute-done.5.refs_5_), channel_id=1, source_target_pairs={{4,8},{8,12},{5,9},{9,13},{6,10},{10,14},{7,11},{11,15},{20,24},{2... | collective-permute-start | bytes 1572872 | tf_op jit(solution)/shard_map/ppermute | solution.py:297
  66.3 43.1 %collective-permute-start.11 = (bf16[512,512]{1,0:T(8,128)(2,1)}, bf16[512,512]{1,0:T(8,128)(2,1)}, u32[]{:S(2)}, u32[]{:S(2)}) collective-permute-start(bf16[512,512]{1,0:T(8,128)(2,1)} %collective-permute-done.7.refs_5_), channel_id=1, source_target_pairs={{4,0},{8,4},{5,1},{9,5},{6,2},{10,6},{7,3},{11,7},{20,16},{24,20},... | collective-permute-start | bytes 1572872 | tf_op jit(solution)/shard_map/ppermute | solution.py:297
  106.7 40.3 %collective-permute-start.12 = (bf16[512,512]{1,0:T(8,128)(2,1)}, bf16[512,512]{1,0:T(8,128)(2,1)S(1)}, u32[]{:S(2)}, u32[]{:S(2)}) collective-permute-start(bf16[512,512]{1,0:T(8,128)(2,1)} %collective-permute-done.8.refs_4_), channel_id=1, source_target_pairs={{8,12},{9,13},{10,14},{11,15},{24,28},{25,29},{26,30},{27,31}} | collective-permute-start | bytes 1572872 | tf_op jit(solution)/shard_map/ppermute | solution.py:297
  107.4 39.6 %collective-permute-start.14 = (bf16[512,512]{1,0:T(8,128)(2,1)}, bf16[512,512]{1,0:T(8,128)(2,1)S(1)}, u32[]{:S(2)}, u32[]{:S(2)}) collective-permute-start(bf16[512,512]{1,0:T(8,128)(2,1)} %collective-permute-done.10.refs_6_), channel_id=1, source_target_pairs={{4,0},{5,1},{6,2},{7,3},{20,16},{21,17},{22,18},{23,19}} | collective-permute-start | bytes 1572872 | tf_op jit(solution)/shard_map/ppermute | solution.py:297
  108.7 38.3 %collective-permute-start.13 = (bf16[512,512]{1,0:T(8,128)(2,1)}, bf16[512,512]{1,0:T(8,128)(2,1)S(1)}, u32[]{:S(2)}, u32[]{:S(2)}) collective-permute-start(bf16[512,512]{1,0:T(8,128)(2,1)} %collective-permute-done.9.refs_5_), channel_id=1, source_target_pairs={{8,12},{9,13},{10,14},{11,15},{24,28},{25,29},{26,30},{27,31}} | collective-permute-start | bytes 1572872 | tf_op jit(solution)/shard_map/ppermute | solution.py:297
  109.4 37.6 %collective-permute-start.15 = (bf16[512,512]{1,0:T(8,128)(2,1)}, bf16[512,512]{1,0:T(8,128)(2,1)S(1)}, u32[]{:S(2)}, u32[]{:S(2)}) collective-permute-start(bf16[512,512]{1,0:T(8,128)(2,1)} %collective-permute-done.11.refs_7_), channel_id=1, source_target_pairs={{4,0},{5,1},{6,2},{7,3},{20,16},{21,17},{22,18},{23,19}} | collective-permute-start | bytes 1572872 | tf_op jit(solution)/shard_map/ppermute | solution.py:297
  110.7 1.0 copy-start.9
  118.3 2.0 %copy-start.1 = (f32[2,512,1024]{2,1,0:T(8,128)}, f32[2,512,1024]{2,1,0:T(8,128)S(1)}, u32[]{:S(2)}) copy-start(f32[2,512,1024]{2,1,0:T(8,128)S(1)} %get-tuple-element.21.refs_0_) | copy-start | bytes 12582916
  127.1 2.0 %copy-start.3 = (f32[2,512,1024]{2,1,0:T(8,128)}, f32[2,512,1024]{2,1,0:T(8,128)S(1)}, u32[]{:S(2)}) copy-start(f32[2,512,1024]{2,1,0:T(8,128)S(1)} %get-tuple-element.24.refs_1_) | copy-start | bytes 12582916
  135.8 2.0 %copy-start.4 = (f32[2,512,1024]{2,1,0:T(8,128)}, f32[2,512,1024]{2,1,0:T(8,128)S(1)}, u32[]{:S(2)}) copy-start(f32[2,512,1024]{2,1,0:T(8,128)S(1)} %get-tuple-element.27.refs_2_) | copy-start | bytes 12582916
  145.1 1.9 %copy-start.5 = (f32[2,512,1024]{2,1,0:T(8,128)}, f32[2,512,1024]{2,1,0:T(8,128)S(1)}, u32[]{:S(2)}) copy-start(f32[2,512,1024]{2,1,0:T(8,128)S(1)} %get-tuple-element.30.refs_3_) | copy-start | bytes 12582916
  153.7 2.0 %copy-start.6 = (f32[2,512,1024]{2,1,0:T(8,128)}, f32[2,512,1024]{2,1,0:T(8,128)S(1)}, u32[]{:S(2)}) copy-start(f32[2,512,1024]{2,1,0:T(8,128)S(1)} %get-tuple-element.33.refs_4_) | copy-start | bytes 12582916
  155.7 4.3 %collective-permute-start.16 = (f32[5,1,512]{2,1,0:T(1,128)S(1)}, f32[5,1,512]{2,1,0:T(1,128)S(1)}, u32[]{:S(2)}, u32[]{:S(2)}) collective-permute-start(f32[5,1,512]{2,1,0:T(1,128)S(1)} %get-tuple-element.34.refs_5_), channel_id=1, source_target_pairs={{4,0},{8,4},{12,8},{0,12},{5,1},{9,5},{13,9},{1,13},{6,2},{10,6},{... | collective-permute-start | bytes 30728 | tf_op jit(solution)/shard_map/ppermute | solution.py:284
  156.5 5.0 %collective-permute-start.17 = (f32[5,1,512]{2,1,0:T(1,128)S(1)}, f32[5,1,512]{2,1,0:T(1,128)S(1)}, u32[]{:S(2)}, u32[]{:S(2)}) collective-permute-start(f32[5,1,512]{2,1,0:T(1,128)S(1)} %get-tuple-element.34.refs_5_), channel_id=1, source_target_pairs={{8,0},{12,4},{0,8},{4,12},{9,1},{13,5},{1,9},{5,13},{10,2},{14,6},... | collective-permute-start | bytes 30728 | tf_op jit(solution)/shard_map/ppermute | solution.py:284
  159.8 5.5 %collective-permute-start.18 = (f32[5,1,512]{2,1,0:T(1,128)S(1)}, f32[5,1,512]{2,1,0:T(1,128)S(1)}, u32[]{:S(2)}, u32[]{:S(2)}) collective-permute-start(f32[5,1,512]{2,1,0:T(1,128)S(1)} %get-tuple-element.34.refs_5_), channel_id=1, source_target_pairs={{12,0},{0,4},{4,8},{8,12},{13,1},{1,5},{5,9},{9,13},{14,2},{2,6},{... | collective-permute-start | bytes 30728 | tf_op jit(solution)/shard_map/ppermute | solution.py:284
  165.3 2.2 %copy-start.2 = (f32[2,512,1024]{2,1,0:T(8,128)S(1)}, f32[2,512,1024]{2,1,0:T(8,128)}, u32[]{:S(2)}) copy-start(f32[2,512,1024]{2,1,0:T(8,128)} %copy-done.1) | copy-start | bytes 12582916
  (1 other events, 0.8 us)

commit v2 on v1

v2 whole, which is shorter than its diff:
```python
import functools
import math

import jax
import jax.numpy as jnp
from jax import lax
from jax.experimental import pallas as pl
from jax.experimental.pallas import tpu as pltpu
from jax.sharding import PartitionSpec as P

D = 1024
K = 4
CAND = 16
BLOCK = 256
EPS = 1e-05
LANES = 128
TILE = 256
MIB = 1 << 20
CODE = 256
EXTRA = 16
VMEM_LIMIT = 56 * MIB
DOTS_LIMIT = 12 * MIB


def normalize_kernel(*refs):
    chunks, out_ref = refs[:-1], refs[-1]
    cols = chunks[0].shape[1]
    values = [ref[...].astype(jnp.float32) for ref in chunks]
    total = sum(jnp.sum(v * v, axis=1, keepdims=True) for v in values)
    scale = lax.rsqrt(total / D + EPS)
    for d, v in enumerate(values):
        out_ref[:, d * cols : (d + 1) * cols] = (v * scale).astype(jnp.bfloat16)


def normalize_rows(chunks):
    rows, cols = chunks[0].shape
    return pl.pallas_call(
        normalize_kernel,
        grid=(rows // TILE,),
        in_specs=[pl.BlockSpec((TILE, cols), lambda i: (i, 0))] * len(chunks),
        out_specs=pl.BlockSpec((TILE, cols * len(chunks)), lambda i: (i, 0)),
        out_shape=jax.ShapeDtypeStruct((rows, cols * len(chunks)), jnp.bfloat16),
        compiler_params=pltpu.CompilerParams(vmem_limit_bytes=16 * MIB),
        cost_estimate=pl.CostEstimate(
            flops=rows * D, bytes_accessed=rows * D, transcendentals=rows
        ),
    )(*chunks)


def plane_at(sc_ref, planes, hop, way):
    shard = sc_ref[0]
    if way in ("own", "up"):
        plane = shard - hop
    elif way == "down":
        plane = shard + hop
    else:
        plane = jnp.where(shard >= hop, shard - hop, shard + hop)
    return plane, (plane >= 0) & (plane < planes)


def dots_kernel(reps, width, pairs, planes, hop, way, sc_ref, *refs):
    first = hop == 0
    fidx_ref, src_refs = refs[0], refs[1 : 1 + reps]
    chunk_refs = refs[1 + reps : 1 + reps + width * pairs]
    refs = refs[1 + reps + width * pairs :]
    p_in, f_in = None, None
    if not first:
        p_in, f_in, refs = refs[0], refs[1], refs[2:]
    s_ref, p_ref, f_ref, tgt, picks, bsum = refs
    rows, cols = chunk_refs[-1].shape
    length = src_refs[0].shape[0]
    groups = length // LANES
    shard, wide, rep = sc_ref[0], sc_ref[1], sc_ref[2]
    plane, valid = plane_at(sc_ref, planes, hop, way)

    values = []
    for d in range(width):
        value = chunk_refs[d][...].astype(jnp.float32)
        for other in range(1, pairs):
            value = value + chunk_refs[other * width + d][...].astype(jnp.float32)
        if d == 0:
            codes = value[rows:]
            value = value[:rows]
        values.append(value)
    total = sum(jnp.sum(v * v, axis=1, keepdims=True) for v in values)
    scale = lax.rsqrt(total / D + EPS)
    for d, v in enumerate(values):
        tgt[:, d * cols : (d + 1) * cols] = (v * scale).astype(jnp.bfloat16)

    bidx = (codes[:K] * CODE + codes[K : 2 * K]).astype(jnp.int32)
    base = (plane * reps + rep) * length + wide * rows
    base = jnp.where(valid, base, 2 * planes * reps * length)
    lane_ids = lax.broadcasted_iota(jnp.int32, (8, LANES), 1)
    row_ids = lax.broadcasted_iota(jnp.int32, (8, length), 0)
    for e in range(reps):
        place = bidx - (shard * reps + lax.rem(rep + e, reps)) * length
        hit = (place >= 0) & (place < length)
        place = jnp.sum(jnp.where(hit, place + 1, 0), axis=0, keepdims=True) - 1
        place = jnp.broadcast_to(place.astype(jnp.float32), (LANES, rows))
        picks[...] = jnp.transpose(place).astype(jnp.int32)

        s_ref[e] = lax.dot_general(
            tgt[...],
            src_refs[e][...],
            (((1,), (1,)), ((), ())),
            preferred_element_type=jnp.float32,
        )
        place = fidx_ref[e] - base
        hit = (place >= 0) & (place < rows)
        place = jnp.sum(jnp.where(hit, place + 1, 0), axis=0, keepdims=True) - 1
        away = jnp.broadcast_to(place, (8, length)) - row_ids

        def one_line(i, total):
            line = pl.ds(pl.multiple_of(i * 8, 8), 8)
            dots = s_ref[e, line, :]
            pick = picks[line, :] - lane_ids
            part = jnp.zeros((8, LANES), jnp.float32)
            for g in range(groups):
                one = dots[:, g * LANES : (g + 1) * LANES]
                part = part + jnp.where(pick == g * LANES, one, 0.0)
            if e > 0:
                part = part + bsum[line, :]
            bsum[line, :] = part
            return total + jnp.where(away == i * 8, dots, 0.0)

        total = lax.fori_loop(
            0, rows // 8, one_line, jnp.zeros((8, length), jnp.float32), unroll=4
        )
        picked = jnp.sum(total, axis=0, keepdims=True)
        f_ref[e] = picked if first else f_in[e] + picked

    if not first:
        p_ref[...] = p_in[...]
    row = jnp.where(valid, plane, planes)
    p_ref[row] = jnp.sum(jnp.transpose(bsum[...]), axis=0, keepdims=True)


def dots_call(scalars, fidx, sources, chunks, state, planes, hop, way):
    reps = len(sources)
    pairs, width = len(chunks), len(chunks[0])
    length = sources[0].shape[0]
    rows = chunks[0][-1].shape[0]
    flat = [c for pair in chunks for c in pair]
    state = [] if state is None else state
    operands = [fidx, *sources, *flat, *state]
    vmem = pl.BlockSpec(memory_space=pltpu.VMEM)
    return pl.pallas_call(
        functools.partial(dots_kernel, reps, width, pairs, planes, hop, way),
        in_specs=[pl.BlockSpec(memory_space=pltpu.SMEM)] + [vmem] * len(operands),
        out_specs=[vmem] * 3,
        scratch_shapes=[
            pltpu.VMEM((rows, D), jnp.bfloat16),
            pltpu.VMEM((rows, LANES), jnp.int32),
            pltpu.VMEM((rows, LANES), jnp.float32),
        ],
        out_shape=[
            jax.ShapeDtypeStruct((reps, rows, length), jnp.float32),
            jax.ShapeDtypeStruct((planes + 1, 1, rows), jnp.float32),
            jax.ShapeDtypeStruct((reps, 1, length), jnp.float32),
        ],
        compiler_params=pltpu.CompilerParams(vmem_limit_bytes=DOTS_LIMIT),
        cost_estimate=pl.CostEstimate(
            flops=2 * reps * length * rows * D,
            bytes_accessed=4 * reps * length * rows,
            transcendentals=rows,
        ),
    )(scalars, *operands)


def margin_kernel(places, terms, sc_ref, *refs):
    slots = len(places)
    s_refs, p_refs, refs = refs[:slots], refs[slots : slots + terms], refs[slots + terms :]
    f_ref, e_ref, means, halves = refs
    reps, rows, lanes = s_refs[0].shape
    parts = rows // BLOCK
    planes = means.shape[0] - 1
    root = math.sqrt(D)

    @pl.when(pl.program_id(0) == 0)
    def _():
        total = p_refs[0][:, 0, :]
        for ref in p_refs[1:]:
            total = total + ref[:, 0, :]
        means[...] = (total / (K * root)).astype(jnp.bfloat16).astype(jnp.float32)
        for t, (hop, way) in enumerate(places):
            plane, _ = plane_at(sc_ref, planes, hop, way)
            row = means[pl.ds(jnp.clip(plane, 0, planes - 1), 1), :]
            halves[t] = (0.5 * root) * jnp.transpose(jnp.broadcast_to(row, (LANES, rows)))

    for e in range(reps):
        at = lax.rem(sc_ref[2] + e, reps)
        for t in range(slots):
            for b in range(parts):

                def one_line(i, top):
                    line = pl.ds(pl.multiple_of(b * BLOCK + i * 8, 8), 8)
                    half = jnp.concatenate([halves[t, line, :]] * (lanes // LANES), axis=1)
                    return jnp.maximum(top, s_refs[t][e, line, :] - half)

                top = jnp.full((8, lanes), -jnp.inf, jnp.float32)
                top = lax.fori_loop(0, BLOCK // 8, one_line, top, unroll=8)
                line = t * parts + b
                e_ref[at, line : line + 1, :] = jnp.max(top, axis=0, keepdims=True) * (1 / root)
        line = slots * parts
        e_ref[at, line : line + 1, :] = f_ref[e]
        mean = means[pl.ds(sc_ref[0], 1), :]
        for start in range(0, lanes, rows):
            e_ref[at, line + 1 : line + 2, start : start + min(rows, lanes)] = mean[:, :lanes]


def margin_call(scalars, dots, bwd_terms, fwd_parts, places, whole):
    terms, slots = len(bwd_terms), len(dots)
    reps, rows, length = dots[0].shape
    lines = -(-(slots * (rows // BLOCK) + 2) // 8) * 8
    tile = length if whole else rows
    if whole:
        s_spec = p_spec = f_spec = e_spec = pl.BlockSpec(memory_space=pltpu.VMEM)
    else:
        s_spec = pl.BlockSpec((reps, rows, tile), lambda j: (0, 0, j))
        p_spec = pl.BlockSpec(bwd_terms[0].shape, lambda j: (0, 0, 0))
        f_spec = pl.BlockSpec((reps, 1, tile), lambda j: (0, 0, j))
        e_spec = pl.BlockSpec((reps, lines, tile), lambda j: (0, 0, j))
    return pl.pallas_call(
        functools.partial(margin_kernel, places, terms),
        grid=(length // tile,),
        in_specs=[pl.BlockSpec(memory_space=pltpu.SMEM)]
        + [s_spec] * slots
        + [p_spec] * terms
        + [f_spec],
        out_specs=e_spec,
        scratch_shapes=[
            pltpu.VMEM((bwd_terms[0].shape[0], rows), jnp.float32),
            pltpu.VMEM((slots, rows, LANES), jnp.float32),
        ],
        out_shape=jax.ShapeDtypeStruct((reps, lines, length), jnp.float32),
        compiler_params=pltpu.CompilerParams(
            vmem_limit_bytes=DOTS_LIMIT if whole else VMEM_LIMIT
        ),
        cost_estimate=pl.CostEstimate(
            flops=rows * D, bytes_accessed=rows * D, transcendentals=0
        ),
    )(scalars, *dots, *bwd_terms, fwd_parts)


def final_kernel(width, reps, planes, slots, parts, sc_ref, list_ref, g_ref, best_ref, fwd_ref, bwd_ref):
    shard, wide, rep = sc_ref[0], sc_ref[1], sc_ref[2]
    both = (planes - 1) // 2
    fwd_line = slots * parts
    fwd = g_ref[0, 0, fwd_line : fwd_line + 1, :]
    for g in range(1, width * reps):
        fwd = fwd + g_ref[g, 0, fwd_line : fwd_line + 1, :]
    fwd = fwd / (K * math.sqrt(D))
    fwd_ref[...] = fwd
    rows = parts * BLOCK
    for v in range(width):
        part = g_ref[v * reps + rep, 0, fwd_line + 1 : fwd_line + 2, 0:rows]
        bwd_ref[:, v * rows : (v + 1) * rows] = part.astype(jnp.bfloat16)
    half = 0.5 * fwd
    per_width = best_ref.shape[0]
    for c in range(per_width):
        block = list_ref[wide * per_width + c]
        holder = block // (parts * width)
        local = block - holder * (parts * width)
        plane = holder // reps
        peer = (local // parts) * reps + holder - plane * reps
        hops = jnp.abs(shard - plane)
        near = 2 * hops - 1 + jnp.where(plane > shard, 1, 0)
        slot = jnp.where(hops == 0, 0, jnp.where(hops <= both, near, both + hops))
        line = slot * parts + local - (local // parts) * parts
        best_ref[c : c + 1, :] = g_ref[peer, 0, pl.ds(line, 1), :] - half


def final_call(scalars, own_list, gathered, width, reps, planes, slots, parts):
    lines, length = gathered.shape[2:]
    per_width = CAND // width
    return pl.pallas_call(
        functools.partial(final_kernel, width, reps, planes, slots, parts),
        grid_spec=pltpu.PrefetchScalarGridSpec(
            num_scalar_prefetch=2,
            grid=(1,),
            in_specs=[
                pl.BlockSpec((width * reps, 1, lines, length), lambda j, sc, ls: (0, sc[2], 0, 0))
            ],
            out_specs=[
                pl.BlockSpec((per_width, length), lambda j, sc, ls: (0, 0)),
                pl.BlockSpec((1, length), lambda j, sc, ls: (0, 0)),
                pl.BlockSpec((1, length), lambda j, sc, ls: (0, 0)),
            ],
        ),
        out_shape=[
            jax.ShapeDtypeStruct((per_width, length), jnp.float32),
            jax.ShapeDtypeStruct((1, length), jnp.float32),
            jax.ShapeDtypeStruct((1, length), jnp.bfloat16),
        ],
        compiler_params=pltpu.CompilerParams(vmem_limit_bytes=16 * MIB),
    )(scalars, own_list, gathered)


def together(*values):
    return lax.optimization_barrier(values)


def on_device(source_vecs, target_vecs, fwd_owner, fwd_row, bwd_owner, bwd_row, cand_lists):
    reps = lax.axis_size("rep")
    planes = lax.axis_size("shard")
    width = lax.axis_size("width")
    shard = lax.axis_index("shard")
    wide = lax.axis_index("width")
    rep = lax.axis_index("rep")
    length = source_vecs.shape[0]
    rows = length // width
    parts = rows // BLOCK

    def part_of(values, index, axis=0):
        return lax.dynamic_slice_in_dim(values, index * rows, rows, axis)

    def shift(values, axis, count, by):
        return lax.ppermute(values, axis, [((i + by) % count, i) for i in range(count)])

    bidx = part_of(jnp.transpose(bwd_owner * length + bwd_row), wide, 1)
    codes = [bidx // CODE, lax.rem(bidx, CODE), jnp.zeros((EXTRA - 2 * K, rows), jnp.int32)]
    codes = jnp.concatenate(codes).astype(jnp.bfloat16)
    first = [jnp.concatenate([part_of(target_vecs, wide), codes])]
    rest = []
    for d in range(1, width):
        sent = part_of(target_vecs, lax.rem(wide + width - d, width))
        rest.append(shift(sent, "width", width, d))
    fidx_own = jnp.transpose(fwd_owner * length + fwd_row)

    def over_reps(values):
        return jnp.stack([values] + [shift(values, "rep", reps, e) for e in range(1, reps)])

    fidx = over_reps(fidx_own)

    def moved(chunks, hop):
        out = []
        half = len(chunks) // 2
        ways = (chunks, chunks) if hop == 1 else (chunks[:half], chunks[half:])
        for by, side in zip((1, -1), ways):
            pairs = [(i, i + by) for i in range(planes) if 0 <= i + by < planes]
            pairs = [(i, j) for i, j in pairs if 0 <= j - by * hop < planes]
            out += [lax.ppermute(c, "shard", pairs) for c in side]
        return out

    both = (planes - 1) // 2
    dots, places, state = [], [], None
    scalars = jnp.stack([shard, wide, rep]).astype(jnp.int32)

    def arrived(hop, side):
        half = len(tails[hop]) // 2
        return [heads[hop][side]] + tails[hop][side * half : side * half + half]

    def use(hop):
        nonlocal state, fidx
        if hop == 0:
            calls = [("own", [first + tails[0]])]
        elif hop <= both:
            calls = [("up", [arrived(hop, 0)]), ("down", [arrived(hop, 1)])]
        else:
            calls = [("one", [arrived(hop, 0), arrived(hop, 1)])]
        for way, chunks in calls:
            out, *state = dots_call(scalars, fidx, src, chunks, state, planes, hop, way)
            dots.append(out)
            places.append((hop, way))

    heads, tails = {0: first}, {0: rest}
    heads[1] = moved(first, 1)
    got = together(*heads[1], *rest, source_vecs)
    heads[1], tails[0], held = list(got[:2]), list(got[2:-1]), got[-1]
    sources = [held] + [shift(held, "width", width, d) for d in range(1, width)]
    src = []
    for turn in range(2, planes + 1):
        if turn >= 4:
            for hop in range(len(set(h for h, _ in places)), turn - 2):
                use(hop)
            own_again, state[0] = together(fidx_own, state[0])
            fidx = over_reps(own_again)
            late, far = tails[turn - 2], heads[turn - 1]
            got = together(*late, *far, fidx)
            tails[turn - 2], heads[turn - 1] = list(got[: len(late)]), list(got[len(late) : -1])
            fidx = got[-1]
        fresh = moved(tails[turn - 2], turn - 1)
        ahead = moved(heads[turn - 1], turn) if turn < planes else []
        if turn == 2:
            got = together(*fresh, *ahead, *sources[1:])
            sources[1:] = got[len(fresh) + len(ahead) :]
            src = [normalize_rows(sources)]
            for e in range(1, reps):
                src.append(shift(src[0], "rep", reps, e))
        else:
            got = together(*fresh, *ahead)
        tails[turn - 1] = list(got[: len(fresh)])
        heads[turn] = list(got[len(fresh) : len(fresh) + len(ahead)])
    for hop in range(len(set(h for h, _ in places)), planes):
        use(hop)

    def over_planes(values):
        if planes > 4:
            return [lax.psum(values, "shard")]
        return [values] + [shift(values, "shard", planes, d) for d in range(1, planes)]

    lines = margin_call(
        scalars, dots, over_planes(state[0]), state[1], tuple(places), planes <= 4
    )
    gathered = lax.all_gather(lines, ("width", "rep"), axis=0, tiled=False)
    own_list = lax.dynamic_index_in_dim(cand_lists, shard, 0, keepdims=False)
    best, fwd_mean, bwd_mean = final_call(
        scalars, own_list, gathered, width, reps, planes, len(dots), parts
    )
    return (jnp.transpose(best), fwd_mean.reshape(-1), bwd_mean.reshape(-1))


def solution(mesh):
    in_specs = (
        P(("groups", "shard", "rep"), "width"),
        P(("groups", "shard", "rep"), "width"),
        P(("groups", "shard", "rep"), None),
        P(("groups", "shard", "rep"), None),
        P(("groups", "shard", "rep"), None),
        P(("groups", "shard", "rep"), None),
        P("groups", None),
    )
    out_specs = (
        P(("groups", "shard", "rep"), "width"),
        P(("groups", "shard", "rep")),
        P(("groups", "shard", "rep")),
    )
    return jax.shard_map(
        on_device, mesh=mesh, in_specs=in_specs, out_specs=out_specs, check_vma=False
    )
```

time: 186 us -> 140 us (0.75)
  blocking collectives: 45.5 us -> 6.51 us
  Pallas kernels: 44.3 us -> 33.8 us
    all_gather x1 -> x0, blocking collectives: 38.3 us -> none  [on_device(): lax.all_gather(part_of(bwd_owner * length + bwd_row, wide), 'shard', axis...]
    ppermute x12, waiting for transfers between devices: 10.6 us -> 26.2 us  [moved(): out += [lax.ppermute(c, 'shard', pairs) for c in side]]
    ppermute x7 -> x8, waiting for transfers between devices: 35.5 us -> 19.9 us  [shift(): lax.ppermute(values, axis, [((i + by) % count, i) for i in range(count)])]
    pallas_call x6, Pallas kernels: 42.1 us -> 31.6 us  [the longest x5 28.6 us: dots_call(): pl.pallas_call(functools.partial(dots_kernel, reps, width, pairs, planes,...]
    ppermute x12, starting transfers between devices: 20.8 us -> 24.8 us  [moved(): out += [lax.ppermute(c, 'shard', pairs) for c in side]]
    ppermute x7 -> x8, starting transfers between devices: 9.31 us -> 6.94 us  [shift(): lax.ppermute(values, axis, [((i + by) % count, i) for i in range(count)])]
    unnamed x29 -> x60, local copies, waits for them, and re-layouts: 15.2 us -> 16.9 us
  transfers between devices with their start and end apart: 19 -> 20, of which waited for: 7 -> 9; matrix products, arithmetic and copies ran while one was open for 1% -> 0% of each run, Pallas kernels for 15% -> 16%
where the time goes in v2:
time: 140 us; the launch traced here: 139 us
  waiting for transfers between devices  46.1 us (33%)
  Pallas kernels  33.8 us (24%)
  starting transfers between devices  31.8 us (23%)
  local copies, waits for them, and re-layouts  18.3 us (13%)
  blocking collectives  6.51 us (5%)
  other arithmetic  1.69 us (1%)
    pallas_call x5, Pallas kernels, dots_call(): pl.pallas_call(functools.partial(dots_kernel, reps, width, pairs, planes,...  28.6 us
    ppermute x12, waiting for transfers between devices, moved(): out += [lax.ppermute(c, 'shard', pairs) for c in side]  26.2 us
    ppermute x12, starting transfers between devices, moved(): out += [lax.ppermute(c, 'shard', pairs) for c in side]  24.8 us
    ppermute x8, waiting for transfers between devices, shift(): lax.ppermute(values, axis, [((i + by) % count, i) for i in range(count)])  19.9 us
    unnamed x60, local copies, waits for them, and re-layouts  16.9 us
    ppermute x8, starting transfers between devices, shift(): lax.ppermute(values, axis, [((i + by) % count, i) for i in range(count)])  6.94 us
    all_gather x1, blocking collectives, on_device(): gathered = lax.all_gather(lines, ('width', 'rep'), axis=0, tiled=False)  6.51 us
    pallas_call x1, Pallas kernels, margin_call(): pl.pallas_call(functools.partial(margin_kernel, places, terms), grid=(len...  2.97 us
  transfers between devices with their start and end apart: 20, of which 9 were waited for; matrix products, arithmetic and copies ran while one was open for 0% of the time, Pallas kernels for 16%

profile of v2, /device:TPU:0, one launch (start us, length us, event | category | flops | bytes accessed | tf_op | source)
XLA Modules:
  0.0 139.1 jit_solution(5880667364895888708)
XLA Ops:
  1.5 1.3 constant_dynamic-slice_fusion
  3.0 5.0 %collective-permute-start.1 = (bf16[528,512]{1,0:T(8,128)(2,1)S(1)}, bf16[528,512]{1,0:T(8,128)(2,1)S(1)}, u32[]{:S(2)}, u32[]{:S(2)}) collective-permute-start(bf16[528,512]{1,0:T(8,128)(2,1)S(1)} %maximum_maximum_fusion.refs_3_), channel_id=1, source_target_pairs={{0,4},{4,8},{8,12},{1,5},{5,9},{9,13},{2,6},{6,10},{10,14},{3,7},{... | collective-permute-start | bytes 1622024 | tf_op jit(solution)/shard_map/ppermute | solution.py:342
  8.0 1.3 collective-permute-start.2
  10.1 1.5 %collective-permute-start.3 = (bf16[512,512]{1,0:T(8,128)(2,1)S(1)}, bf16[512,512]{1,0:T(8,128)(2,1)S(1)}, u32[]{:S(2)}, u32[]{:S(2)}) collective-permute-start(bf16[512,512]{1,0:T(8,128)(2,1)S(1)} %get-tuple-element.83), channel_id=1, source_target_pairs={{2,0},{0,2},{3,1},{1,3},{6,4},{4,6},{7,5},{5,7},{10,8},{8,10},{11,... | collective-permute-start | bytes 1572872 | tf_op jit(solution)/shard_map/ppermute | solution.py:318
  11.6 11.9 %collective-permute-done.3.refs_4_ = bf16[512,512]{1,0:T(8,128)(2,1)S(1)} collective-permute-done((bf16[512,512]{1,0:T(8,128)(2,1)S(1)}, bf16[512,512]{1,0:T(8,128)(2,1)S(1)}, u32[]{:S(2)}, u32[]{:S(2)}) %collective-permute-start.3) | collective-permute-done | bytes 524320 | tf_op jit(solution)/shard_map/ppermute | solution.py:318
  23.6 1.5 %collective-permute-start.8 = (bf16[1024,512]{1,0:T(8,128)(2,1)S(1)}, bf16[1024,512]{1,0:T(8,128)(2,1)S(1)}, u32[]{:S(2)}, u32[]{:S(2)}) collective-permute-start(bf16[1024,512]{1,0:T(8,128)(2,1)S(1)} %copy-done.7), channel_id=1, source_target_pairs={{2,0},{0,2},{3,1},{1,3},{6,4},{4,6},{7,5},{5,7},{10,8},{8,10},{11,... | collective-permute-start | bytes 3145736 | tf_op jit(solution)/shard_map/ppermute | solution.py:318
  26.6 1.3 collective-permute-start.7
  28.7 7.7 %collective-permute-start.4 = (bf16[512,512]{1,0:T(8,128)(2,1)S(1)}, bf16[512,512]{1,0:T(8,128)(2,1)S(1)}, u32[]{:S(2)}, u32[]{:S(2)}) collective-permute-start(bf16[512,512]{1,0:T(8,128)(2,1)S(1)} %collective-permute-done.3.refs_4_), channel_id=1, source_target_pairs={{0,4},{4,8},{8,12},{1,5},{5,9},{9,13},{2,6},{6,10},{10,14},{3,7},{... | collective-permute-start | bytes 1572872 | tf_op jit(solution)/shard_map/ppermute | solution.py:342
  36.4 1.3 collective-permute-start.5
  38.5 7.0 %collective-permute-done.4.refs_4_ = bf16[512,512]{1,0:T(8,128)(2,1)S(1)} collective-permute-done((bf16[512,512]{1,0:T(8,128)(2,1)S(1)}, bf16[512,512]{1,0:T(8,128)(2,1)S(1)}, u32[]{:S(2)}, u32[]{:S(2)}) %collective-permute-start.4) | collective-permute-done | bytes 524320 | tf_op jit(solution)/shard_map/ppermute | solution.py:342
  45.5 9.6 %collective-permute-done.5.refs_4_ = bf16[512,512]{1,0:T(8,128)(2,1)S(1)} collective-permute-done((bf16[512,512]{1,0:T(8,128)(2,1)S(1)}, bf16[512,512]{1,0:T(8,128)(2,1)S(1)}, u32[]{:S(2)}, u32[]{:S(2)}) %collective-permute-start.5) | collective-permute-done | bytes 524320 | tf_op jit(solution)/shard_map/ppermute | solution.py:342
  58.5 3.1 %collective-permute-done = s32[4,1024]{1,0:T(4,128)S(1)} collective-permute-done((s32[4,1024]{1,0:T(4,128)S(1)}, s32[4,1024]{1,0:T(4,128)S(1)}, u32[]{:S(2)}, u32[]{:S(2)}) %collective-permute-start) | collective-permute-done | bytes 16416 | tf_op jit(solution)/shard_map/ppermute | solution.py:318
  61.7 1.5 %collective-permute-start.10 = (bf16[512,512]{1,0:T(8,128)(2,1)}, bf16[512,512]{1,0:T(8,128)(2,1)}, u32[]{:S(2)}, u32[]{:S(2)}) collective-permute-start(bf16[512,512]{1,0:T(8,128)(2,1)} %copy-done.24), channel_id=1, source_target_pairs={{4,8},{8,12},{5,9},{9,13},{6,10},{10,14},{7,11},{11,15},{20,24},{2... | collective-permute-start | bytes 1572872 | tf_op jit(solution)/shard_map/ppermute | solution.py:342
  63.2 1.3 collective-permute-start.11
  65.2 1.3 collective-permute-start.13
  68.6 5.5 %shard_map.95 = (f32[2,512,1024]{2,1,0:T(8,128)S(1)}, f32[5,1,512]{2,1,0:T(1,128)S(1)}, f32[2,1,1024]{2,1,0:T(1,128)S(1)}) custom-call(s32[3]{0:T(128)S(1)} %pad_add_fusion.2.sc_ref, s32[2,4,1024]{2,1,0:T(4,128)S(1)} %pad_add_fusion.refs_0_, bf16[1024,1024]{1,0:T(8,128)(2,1)S(1)} %shard_map.94.refs_1_, bf16[1024,1024]{1,0:T(8,128)(2,1)} %collective-permute-done.9.refs_2_, ...), custom_call_target="tpu_custom_call" | custom-call | flops 2147483648 | bytes 4194304 | tf_op jit(solution)/shard_map/pallas_call | solution.py:147
  74.1 2.0 %copy-done.1 = f32[2,512,1024]{2,1,0:T(8,128)} copy-done((f32[2,512,1024]{2,1,0:T(8,128)}, f32[2,512,1024]{2,1,0:T(8,128)S(1)}, u32[]{:S(2)}) %copy-start.1) | copy-done | bytes 4194328
  76.1 5.6 %shard_map.96 = (f32[2,512,1024]{2,1,0:T(8,128)S(1)}, f32[5,1,512]{2,1,0:T(1,128)S(1)}, f32[2,1,1024]{2,1,0:T(1,128)S(1)}) custom-call(s32[3]{0:T(128)S(1)} %pad_add_fusion.2.sc_ref, s32[2,4,1024]{2,1,0:T(4,128)S(1)} %pad_add_fusion.refs_0_, bf16[1024,1024]{1,0:T(8,128)(2,1)S(1)} %shard_map.94.refs_1_, bf16[1024,1024]{1,0:T(8,128)(2,1)} %collective-permute-done.9.refs_2_, ...), custom_call_target="tpu_custom_call" | custom-call | flops 2147483648 | bytes 4194304 | tf_op jit(solution)/shard_map/pallas_call | solution.py:147
  81.7 2.0 %copy-done.3 = f32[2,512,1024]{2,1,0:T(8,128)} copy-done((f32[2,512,1024]{2,1,0:T(8,128)}, f32[2,512,1024]{2,1,0:T(8,128)S(1)}, u32[]{:S(2)}) %copy-start.3) | copy-done | bytes 4194328
  83.7 5.6 %shard_map.97 = (f32[2,512,1024]{2,1,0:T(8,128)S(1)}, f32[5,1,512]{2,1,0:T(1,128)S(1)}, f32[2,1,1024]{2,1,0:T(1,128)S(1)}) custom-call(s32[3]{0:T(128)S(1)} %pad_add_fusion.2.sc_ref, s32[2,4,1024]{2,1,0:T(4,128)S(1)} %pad_add_fusion.refs_0_, bf16[1024,1024]{1,0:T(8,128)(2,1)S(1)} %shard_map.94.refs_1_, bf16[1024,1024]{1,0:T(8,128)(2,1)} %collective-permute-done.9.refs_2_, ...), custom_call_target="tpu_custom_call" | custom-call | flops 2147483648 | bytes 4194304 | tf_op jit(solution)/shard_map/pallas_call | solution.py:147
  89.3 2.1 %copy-done.5 = f32[2,512,1024]{2,1,0:T(8,128)} copy-done((f32[2,512,1024]{2,1,0:T(8,128)}, f32[2,512,1024]{2,1,0:T(8,128)S(1)}, u32[]{:S(2)}) %copy-start.5) | copy-done | bytes 4194328
  93.3 1.4 %collective-permute-start.15 = (bf16[512,512]{1,0:T(8,128)(2,1)}, bf16[512,512]{1,0:T(8,128)(2,1)}, u32[]{:S(2)}, u32[]{:S(2)}) collective-permute-start(bf16[512,512]{1,0:T(8,128)(2,1)} %collective-permute-done.10.refs_4_), channel_id=1, source_target_pairs={{8,12},{9,13},{10,14},{11,15},{24,28},{25,29},{26,30},{27,31}} | collective-permute-start | bytes 1572872 | tf_op jit(solution)/shard_map/ppermute | solution.py:342
  94.8 1.5 %collective-permute-start.16 = (bf16[512,512]{1,0:T(8,128)(2,1)}, bf16[512,512]{1,0:T(8,128)(2,1)}, u32[]{:S(2)}, u32[]{:S(2)}) collective-permute-start(bf16[512,512]{1,0:T(8,128)(2,1)} %collective-permute-done.11.refs_6_), channel_id=1, source_target_pairs={{4,0},{5,1},{6,2},{7,3},{20,16},{21,17},{22,18},{23,19}} | collective-permute-start | bytes 1572872 | tf_op jit(solution)/shard_map/ppermute | solution.py:342
  96.3 6.0 %shard_map.98 = (f32[2,512,1024]{2,1,0:T(8,128)S(1)}, f32[5,1,512]{2,1,0:T(1,128)S(1)}, f32[2,1,1024]{2,1,0:T(1,128)S(1)}) custom-call(s32[3]{0:T(128)S(1)} %pad_add_fusion.2.sc_ref, s32[2,4,1024]{2,1,0:T(4,128)S(1)} %pad_add_fusion.1.refs_0_, bf16[1024,1024]{1,0:T(8,128)(2,1)S(1)} %shard_map.94.refs_1_, bf16[1024,1024]{1,0:T(8,128)(2,1)} %collective-permute-done.9.refs_2_, ...), custom_call_target="tpu_custom_call" | custom-call | flops 2147483648 | bytes 4194304 | tf_op jit(solution)/shard_map/pallas_call | solution.py:147
  102.3 9.5 %collective-permute-done.16.refs_6_ = bf16[512,512]{1,0:T(8,128)(2,1)} collective-permute-done((bf16[512,512]{1,0:T(8,128)(2,1)}, bf16[512,512]{1,0:T(8,128)(2,1)}, u32[]{:S(2)}, u32[]{:S(2)}) %collective-permute-start.16) | collective-permute-done | bytes 524320 | tf_op jit(solution)/shard_map/ppermute | solution.py:342
  111.8 1.0 copy-done.19
  113.9 6.0 %shard_map.99 = (f32[2,512,1024]{2,1,0:T(8,128)S(1)}, f32[5,1,512]{2,1,0:T(1,128)S(1)}, f32[2,1,1024]{2,1,0:T(1,128)S(1)}) custom-call(s32[3]{0:T(128)S(1)} %pad_add_fusion.2.sc_ref, s32[2,4,1024]{2,1,0:T(4,128)S(1)} %pad_add_fusion.1.refs_0_, bf16[1024,1024]{1,0:T(8,128)(2,1)S(1)} %shard_map.94.refs_1_, bf16[1024,1024]{1,0:T(8,128)(2,1)} %collective-permute-done.9.refs_2_, ...), custom_call_target="tpu_custom_call" | custom-call | flops 2147483648 | bytes 4194304 | tf_op jit(solution)/shard_map/pallas_call | solution.py:147
  119.9 2.3 %collective-permute-start.17 = (f32[5,1,512]{2,1,0:T(1,128)S(1)}, f32[5,1,512]{2,1,0:T(1,128)S(1)}, u32[]{:S(2)}, u32[]{:S(2)}) collective-permute-start(f32[5,1,512]{2,1,0:T(1,128)S(1)} %get-tuple-element.78.refs_5_), channel_id=1, source_target_pairs={{4,0},{8,4},{12,8},{0,12},{5,1},{9,5},{13,9},{1,13},{6,2},{10,6},{... | collective-permute-start | bytes 30728 | tf_op jit(solution)/shard_map/ppermute | solution.py:318
  123.6 3.2 %collective-permute-done.18.refs_7_ = f32[5,1,512]{2,1,0:T(1,128)S(1)} collective-permute-done((f32[5,1,512]{2,1,0:T(1,128)S(1)}, f32[5,1,512]{2,1,0:T(1,128)S(1)}, u32[]{:S(2)}, u32[]{:S(2)}) %collective-permute-start.18) | collective-permute-done | bytes 10272 | tf_op jit(solution)/shard_map/ppermute | solution.py:318
  127.7 3.0 %shard_map.100 = f32[2,16,1024]{2,1,0:T(8,128)S(1)} custom-call(s32[3]{0:T(128)S(1)} %pad_add_fusion.2.sc_ref, f32[2,512,1024]{2,1,0:T(8,128)S(1)} %copy-done.2, f32[2,512,1024]{2,1,0:T(8,128)S(1)} %copy-done.4, f32[2,512,1024]{2,1,0:T(8,128)S(1)} %copy-done.6, f32[2,512,1024]{2,1,0:T(8,128)S(1)} %get-tuple-element.70.refs_3_, ...), custom_call_target="tpu_custom_call" | custom-call | flops 524288 | bytes 524288 | tf_op jit(solution)/shard_map/pallas_call | solution.py:223
  130.6 6.5 %all-gather = f32[8,16,1024]{2,1,0:T(8,128)S(1)} all-gather(f32[2,16,1024]{2,1,0:T(8,128)S(1)} %shard_map.100), channel_id=2, replica_groups=mesh['groups'=2,'shard'=4,'width'=2,'rep'=2] {'width','rep'}, dimensions={0}, use_global_device_ids=true | all-gather | bytes 655360 | tf_op jit(solution)/shard_map/all_gather | solution.py:405
  137.1 1.3 shard_map.101
  (88 shorter events, 17.3 us)
Async XLA Ops:
  0.6 122.2 %copy-start = (s32[4,16]{1,0:T(4,128)S(1)}, s32[4,16]{1,0:T(4,128)}, u32[]{:S(2)}) copy-start(s32[4,16]{1,0:T(4,128)} %param.13) | copy-start | bytes 772
  0.6 23.0 %copy-start.7 = (bf16[1024,512]{1,0:T(8,128)(2,1)S(1)}, bf16[1024,512]{1,0:T(8,128)(2,1)}, u32[]{:S(2)}) copy-start(bf16[1024,512]{1,0:T(8,128)(2,1)} %refs_0_) | copy-start | bytes 3145732
  3.0 20.5 %collective-permute-start.1 = (bf16[528,512]{1,0:T(8,128)(2,1)S(1)}, bf16[528,512]{1,0:T(8,128)(2,1)S(1)}, u32[]{:S(2)}, u32[]{:S(2)}) collective-permute-start(bf16[528,512]{1,0:T(8,128)(2,1)S(1)} %maximum_maximum_fusion.refs_3_), channel_id=1, source_target_pairs={{0,4},{4,8},{8,12},{1,5},{5,9},{9,13},{2,6},{6,10},{10,14},{3,7},{... | collective-permute-start | bytes 1622024 | tf_op jit(solution)/shard_map/ppermute | solution.py:342
  8.0 15.6 %collective-permute-start.2 = (bf16[528,512]{1,0:T(8,128)(2,1)S(1)}, bf16[528,512]{1,0:T(8,128)(2,1)S(1)}, u32[]{:S(2)}, u32[]{:S(2)}) collective-permute-start(bf16[528,512]{1,0:T(8,128)(2,1)S(1)} %maximum_maximum_fusion.refs_3_), channel_id=1, source_target_pairs={{4,0},{8,4},{12,8},{5,1},{9,5},{13,9},{6,2},{10,6},{14,10},{7,3},{... | collective-permute-start | bytes 1622024 | tf_op jit(solution)/shard_map/ppermute | solution.py:342
  10.1 47.7 %copy-start.28 = (s32[1024,4]{0,1:T(4,128)S(1)}, s32[1024,4]{0,1:T(4,128)}, u32[]{:S(2)}) copy-start(s32[1024,4]{0,1:T(4,128)} %param.10) | copy-start | bytes 49156
  10.1 47.7 %copy-start.29 = (s32[1024,4]{0,1:T(4,128)S(1)}, s32[1024,4]{0,1:T(4,128)}, u32[]{:S(2)}) copy-start(s32[1024,4]{0,1:T(4,128)} %param.9) | copy-start | bytes 49156
  10.1 13.4 %collective-permute-start.3 = (bf16[512,512]{1,0:T(8,128)(2,1)S(1)}, bf16[512,512]{1,0:T(8,128)(2,1)S(1)}, u32[]{:S(2)}, u32[]{:S(2)}) collective-permute-start(bf16[512,512]{1,0:T(8,128)(2,1)S(1)} %get-tuple-element.83), channel_id=1, source_target_pairs={{2,0},{0,2},{3,1},{1,3},{6,4},{4,6},{7,5},{5,7},{10,8},{8,10},{11,... | collective-permute-start | bytes 1572872 | tf_op jit(solution)/shard_map/ppermute | solution.py:318
  23.6 33.3 %collective-permute-start.8 = (bf16[1024,512]{1,0:T(8,128)(2,1)S(1)}, bf16[1024,512]{1,0:T(8,128)(2,1)S(1)}, u32[]{:S(2)}, u32[]{:S(2)}) collective-permute-start(bf16[1024,512]{1,0:T(8,128)(2,1)S(1)} %copy-done.7), channel_id=1, source_target_pairs={{2,0},{0,2},{3,1},{1,3},{6,4},{4,6},{7,5},{5,7},{10,8},{8,10},{11,... | collective-permute-start | bytes 3145736 | tf_op jit(solution)/shard_map/ppermute | solution.py:318
  25.1 30.0 %collective-permute-start.6 = (bf16[528,512]{1,0:T(8,128)(2,1)S(1)}, bf16[528,512]{1,0:T(8,128)(2,1)S(1)}, u32[]{:S(2)}, u32[]{:S(2)}) collective-permute-start(bf16[528,512]{1,0:T(8,128)(2,1)S(1)} %collective-permute-done.1.refs_3_), channel_id=1, source_target_pairs={{4,8},{8,12},{5,9},{9,13},{6,10},{10,14},{7,11},{11,15},{20,24},{2... | collective-permute-start | bytes 1622024 | tf_op jit(solution)/shard_map/ppermute | solution.py:342
  26.6 28.5 %collective-permute-start.7 = (bf16[528,512]{1,0:T(8,128)(2,1)S(1)}, bf16[528,512]{1,0:T(8,128)(2,1)S(1)}, u32[]{:S(2)}, u32[]{:S(2)}) collective-permute-start(bf16[528,512]{1,0:T(8,128)(2,1)S(1)} %collective-permute-done.2.refs_3_), channel_id=1, source_target_pairs={{4,0},{8,4},{5,1},{9,5},{6,2},{10,6},{7,3},{11,7},{20,16},{24,20},... | collective-permute-start | bytes 1622024 | tf_op jit(solution)/shard_map/ppermute | solution.py:342
  28.7 16.8 %collective-permute-start.4 = (bf16[512,512]{1,0:T(8,128)(2,1)S(1)}, bf16[512,512]{1,0:T(8,128)(2,1)S(1)}, u32[]{:S(2)}, u32[]{:S(2)}) collective-permute-start(bf16[512,512]{1,0:T(8,128)(2,1)S(1)} %collective-permute-done.3.refs_4_), channel_id=1, source_target_pairs={{0,4},{4,8},{8,12},{1,5},{5,9},{9,13},{2,6},{6,10},{10,14},{3,7},{... | collective-permute-start | bytes 1572872 | tf_op jit(solution)/shard_map/ppermute | solution.py:342
  36.4 18.7 %collective-permute-start.5 = (bf16[512,512]{1,0:T(8,128)(2,1)S(1)}, bf16[512,512]{1,0:T(8,128)(2,1)S(1)}, u32[]{:S(2)}, u32[]{:S(2)}) collective-permute-start(bf16[512,512]{1,0:T(8,128)(2,1)S(1)} %collective-permute-done.3.refs_4_), channel_id=1, source_target_pairs={{4,0},{8,4},{12,8},{5,1},{9,5},{13,9},{6,2},{10,6},{14,10},{7,3},{... | collective-permute-start | bytes 1572872 | tf_op jit(solution)/shard_map/ppermute | solution.py:342
  45.5 9.6 %copy-start.24 = (bf16[512,512]{1,0:T(8,128)(2,1)}, bf16[512,512]{1,0:T(8,128)(2,1)S(1)}, u32[]{:S(2)}) copy-start(bf16[512,512]{1,0:T(8,128)(2,1)S(1)} %collective-permute-done.4.refs_4_) | copy-start | bytes 1572868
  57.8 8.7 %collective-permute-start.9 = (bf16[1024,1024]{1,0:T(8,128)(2,1)S(1)}, bf16[1024,1024]{1,0:T(8,128)(2,1)}, u32[]{:S(2)}, u32[]{:S(2)}) collective-permute-start(bf16[1024,1024]{1,0:T(8,128)(2,1)S(1)} %shard_map.94.refs_1_), channel_id=1, source_target_pairs={{1,0},{0,1},{3,2},{2,3},{5,4},{4,5},{7,6},{6,7},{9,8},{8,9},{11,10... | collective-permute-start | bytes 6291464 | tf_op jit(solution)/shard_map/ppermute | solution.py:318
  57.9 3.8 %collective-permute-start = (s32[4,1024]{1,0:T(4,128)S(1)}, s32[4,1024]{1,0:T(4,128)S(1)}, u32[]{:S(2)}, u32[]{:S(2)}) collective-permute-start(s32[4,1024]{1,0:T(4,128)S(1)} %get-tuple-element.64), channel_id=1, source_target_pairs={{1,0},{0,1},{3,2},{2,3},{5,4},{4,5},{7,6},{6,7},{9,8},{8,9},{11,10... | collective-permute-start | bytes 49160 | tf_op jit(solution)/shard_map/ppermute | solution.py:318
  61.7 30.0 %collective-permute-start.10 = (bf16[512,512]{1,0:T(8,128)(2,1)}, bf16[512,512]{1,0:T(8,128)(2,1)}, u32[]{:S(2)}, u32[]{:S(2)}) collective-permute-start(bf16[512,512]{1,0:T(8,128)(2,1)} %copy-done.24), channel_id=1, source_target_pairs={{4,8},{8,12},{5,9},{9,13},{6,10},{10,14},{7,11},{11,15},{20,24},{2... | collective-permute-start | bytes 1572872 | tf_op jit(solution)/shard_map/ppermute | solution.py:342
  63.2 28.5 %collective-permute-start.11 = (bf16[512,512]{1,0:T(8,128)(2,1)}, bf16[512,512]{1,0:T(8,128)(2,1)}, u32[]{:S(2)}, u32[]{:S(2)}) collective-permute-start(bf16[512,512]{1,0:T(8,128)(2,1)} %copy-done.26), channel_id=1, source_target_pairs={{4,0},{8,4},{5,1},{9,5},{6,2},{10,6},{7,3},{11,7},{20,16},{24,20},... | collective-permute-start | bytes 1572872 | tf_op jit(solution)/shard_map/ppermute | solution.py:342
  64.4 27.3 %collective-permute-start.12 = (bf16[528,512]{1,0:T(8,128)(2,1)}, bf16[528,512]{1,0:T(8,128)(2,1)S(1)}, u32[]{:S(2)}, u32[]{:S(2)}) collective-permute-start(bf16[528,512]{1,0:T(8,128)(2,1)} %copy-done.10), channel_id=1, source_target_pairs={{8,12},{9,13},{10,14},{11,15},{24,28},{25,29},{26,30},{27,31}} | collective-permute-start | bytes 1622024 | tf_op jit(solution)/shard_map/ppermute | solution.py:342
  65.2 27.4 %collective-permute-start.13 = (bf16[528,512]{1,0:T(8,128)(2,1)}, bf16[528,512]{1,0:T(8,128)(2,1)S(1)}, u32[]{:S(2)}, u32[]{:S(2)}) collective-permute-start(bf16[528,512]{1,0:T(8,128)(2,1)} %copy-done.12), channel_id=1, source_target_pairs={{4,0},{5,1},{6,2},{7,3},{20,16},{21,17},{22,18},{23,19}} | collective-permute-start | bytes 1622024 | tf_op jit(solution)/shard_map/ppermute | solution.py:342
  76.1 7.6 %copy-start.15 = (bf16[528,512]{1,0:T(8,128)(2,1)S(1)}, bf16[528,512]{1,0:T(8,128)(2,1)}, u32[]{:S(2)}) copy-start(bf16[528,512]{1,0:T(8,128)(2,1)} %copy-done.14) | copy-start | bytes 1622020
  76.1 7.6 %copy-start.27 = (bf16[512,512]{1,0:T(8,128)(2,1)S(1)}, bf16[512,512]{1,0:T(8,128)(2,1)}, u32[]{:S(2)}) copy-start(bf16[512,512]{1,0:T(8,128)(2,1)} %copy-done.26) | copy-start | bytes 1572868
  83.7 12.6 %copy-start.11 = (bf16[528,512]{1,0:T(8,128)(2,1)S(1)}, bf16[528,512]{1,0:T(8,128)(2,1)}, u32[]{:S(2)}) copy-start(bf16[528,512]{1,0:T(8,128)(2,1)} %copy-done.10) | copy-start | bytes 1622020
  83.7 12.6 %copy-start.13 = (bf16[528,512]{1,0:T(8,128)(2,1)S(1)}, bf16[528,512]{1,0:T(8,128)(2,1)}, u32[]{:S(2)}) copy-start(bf16[528,512]{1,0:T(8,128)(2,1)} %copy-done.12) | copy-start | bytes 1622020
  91.3 2.0 %collective-permute-start.14 = (s32[4,1024]{1,0:T(4,128)S(1)}, s32[4,1024]{1,0:T(4,128)S(1)}, u32[]{:S(2)}, u32[]{:S(2)}) collective-permute-start(s32[4,1024]{1,0:T(4,128)S(1)} %get-tuple-element.64), channel_id=1, source_target_pairs={{1,0},{0,1},{3,2},{2,3},{5,4},{4,5},{7,6},{6,7},{9,8},{8,9},{11,10... | collective-permute-start | bytes 49160 | tf_op jit(solution)/shard_map/ppermute | solution.py:318
  93.3 9.0 %collective-permute-start.15 = (bf16[512,512]{1,0:T(8,128)(2,1)}, bf16[512,512]{1,0:T(8,128)(2,1)}, u32[]{:S(2)}, u32[]{:S(2)}) collective-permute-start(bf16[512,512]{1,0:T(8,128)(2,1)} %collective-permute-done.10.refs_4_), channel_id=1, source_target_pairs={{8,12},{9,13},{10,14},{11,15},{24,28},{25,29},{26,30},{27,31}} | collective-permute-start | bytes 1572872 | tf_op jit(solution)/shard_map/ppermute | solution.py:342
  94.8 17.0 %collective-permute-start.16 = (bf16[512,512]{1,0:T(8,128)(2,1)}, bf16[512,512]{1,0:T(8,128)(2,1)}, u32[]{:S(2)}, u32[]{:S(2)}) collective-permute-start(bf16[512,512]{1,0:T(8,128)(2,1)} %collective-permute-done.11.refs_6_), channel_id=1, source_target_pairs={{4,0},{5,1},{6,2},{7,3},{20,16},{21,17},{22,18},{23,19}} | collective-permute-start | bytes 1572872 | tf_op jit(solution)/shard_map/ppermute | solution.py:342
  96.3 31.4 %copy-start.4 = (f32[2,512,1024]{2,1,0:T(8,128)S(1)}, f32[2,512,1024]{2,1,0:T(8,128)}, u32[]{:S(2)}) copy-start(f32[2,512,1024]{2,1,0:T(8,128)} %copy-done.3) | copy-start | bytes 12582916
  96.3 31.4 %copy-start.6 = (f32[2,512,1024]{2,1,0:T(8,128)S(1)}, f32[2,512,1024]{2,1,0:T(8,128)}, u32[]{:S(2)}) copy-start(f32[2,512,1024]{2,1,0:T(8,128)} %copy-done.5) | copy-start | bytes 12582916
  113.9 13.8 %copy-start.2 = (f32[2,512,1024]{2,1,0:T(8,128)S(1)}, f32[2,512,1024]{2,1,0:T(8,128)}, u32[]{:S(2)}) copy-start(f32[2,512,1024]{2,1,0:T(8,128)} %copy-done.1) | copy-start | bytes 12582916
  119.9 3.7 %collective-permute-start.17 = (f32[5,1,512]{2,1,0:T(1,128)S(1)}, f32[5,1,512]{2,1,0:T(1,128)S(1)}, u32[]{:S(2)}, u32[]{:S(2)}) collective-permute-start(f32[5,1,512]{2,1,0:T(1,128)S(1)} %get-tuple-element.78.refs_5_), channel_id=1, source_target_pairs={{4,0},{8,4},{12,8},{0,12},{5,1},{9,5},{13,9},{1,13},{6,2},{10,6},{... | collective-permute-start | bytes 30728 | tf_op jit(solution)/shard_map/ppermute | solution.py:318
  122.2 4.6 %collective-permute-start.18 = (f32[5,1,512]{2,1,0:T(1,128)S(1)}, f32[5,1,512]{2,1,0:T(1,128)S(1)}, u32[]{:S(2)}, u32[]{:S(2)}) collective-permute-start(f32[5,1,512]{2,1,0:T(1,128)S(1)} %get-tuple-element.78.refs_5_), channel_id=1, source_target_pairs={{8,0},{12,4},{0,8},{4,12},{9,1},{13,5},{1,9},{5,13},{10,2},{14,6},... | collective-permute-start | bytes 30728 | tf_op jit(solution)/shard_map/ppermute | solution.py:318
  122.2 5.5 %collective-permute-start.19 = (f32[5,1,512]{2,1,0:T(1,128)S(1)}, f32[5,1,512]{2,1,0:T(1,128)S(1)}, u32[]{:S(2)}, u32[]{:S(2)}) collective-permute-start(f32[5,1,512]{2,1,0:T(1,128)S(1)} %get-tuple-element.78.refs_5_), channel_id=1, source_target_pairs={{12,0},{0,4},{4,8},{8,12},{13,1},{1,5},{5,9},{9,13},{14,2},{2,6},{... | collective-permute-start | bytes 30728 | tf_op jit(solution)/shard_map/ppermute | solution.py:318
  (18 other events, 32.8 us)

commit v3 on v2

--- a/solution.py
+++ b/solution.py
@@ -18,6 +18,7 @@
 MIB = 1 << 20
 CODE = 256
 EXTRA = 16
+AHEAD = 1
 VMEM_LIMIT = 56 * MIB
 DOTS_LIMIT = 12 * MIB
 
@@ -67,7 +68,7 @@
     if not first:
         p_in, f_in, refs = refs[0], refs[1], refs[2:]
     s_ref, p_ref, f_ref, tgt, picks, bsum = refs
-    rows, cols = chunk_refs[-1].shape
+    rows, cols = chunk_refs[0].shape
     length = src_refs[0].shape[0]
     groups = length // LANES
     shard, wide, rep = sc_ref[0], sc_ref[1], sc_ref[2]
@@ -78,7 +79,7 @@
         value = chunk_refs[d][...].astype(jnp.float32)
         for other in range(1, pairs):
             value = value + chunk_refs[other * width + d][...].astype(jnp.float32)
-        if d == 0:
+        if d == 1:
             codes = value[rows:]
             value = value[:rows]
         values.append(value)
@@ -139,7 +140,7 @@
     reps = len(sources)
     pairs, width = len(chunks), len(chunks[0])
     length = sources[0].shape[0]
-    rows = chunks[0][-1].shape[0]
+    rows = chunks[0][0].shape[0]
     flat = [c for pair in chunks for c in pair]
     state = [] if state is None else state
     operands = [fidx, *sources, *flat, *state]
@@ -317,13 +318,16 @@
     def shift(values, axis, count, by):
         return lax.ppermute(values, axis, [((i + by) % count, i) for i in range(count)])
 
-    bidx = part_of(jnp.transpose(bwd_owner * length + bwd_row), wide, 1)
-    codes = [bidx // CODE, lax.rem(bidx, CODE), jnp.zeros((EXTRA - 2 * K, rows), jnp.int32)]
+    bidx = jnp.transpose(bwd_owner * length + bwd_row)
+    codes = [bidx // CODE, lax.rem(bidx, CODE), jnp.zeros((EXTRA - 2 * K, length), jnp.int32)]
     codes = jnp.concatenate(codes).astype(jnp.bfloat16)
-    first = [jnp.concatenate([part_of(target_vecs, wide), codes])]
+    first = [part_of(target_vecs, wide)]
     rest = []
     for d in range(1, width):
-        sent = part_of(target_vecs, lax.rem(wide + width - d, width))
+        index = lax.rem(wide + width - d, width)
+        sent = part_of(target_vecs, index)
+        if d == 1:
+            sent = jnp.concatenate([sent, part_of(codes, index, 1)])
         rest.append(shift(sent, "width", width, d))
     fidx_own = jnp.transpose(fwd_owner * length + fwd_row)
 
@@ -343,56 +347,45 @@
         return out
 
     both = (planes - 1) // 2
+    queue = [(0, "own")]
+    for hop in range(1, planes):
+        queue += [(hop, "up"), (hop, "down")] if hop <= both else [(hop, "one")]
     dots, places, state = [], [], None
     scalars = jnp.stack([shard, wide, rep]).astype(jnp.int32)
+
+    heads, tails = {0: first}, {0: rest}
+    for hop in range(1, planes):
+        heads[hop] = moved(heads[hop - 1], hop)
+        if hop < 3:
+            tails[hop] = moved(tails[hop - 1], hop)
+    *_, fidx, held = together(*heads[1], *rest, fidx, source_vecs)
+    sources = [held] + [shift(held, "width", width, d) for d in range(1, width)]
+    got = together(*sources, *tails[1], *heads[2])
+    sources = list(got[:width])
+    src = [normalize_rows(sources)]
+    for e in range(1, reps):
+        src.append(shift(src[0], "rep", reps, e))
 
     def arrived(hop, side):
         half = len(tails[hop]) // 2
         return [heads[hop][side]] + tails[hop][side * half : side * half + half]
 
-    def use(hop):
-        nonlocal state, fidx
-        if hop == 0:
-            calls = [("own", [first + tails[0]])]
-        elif hop <= both:
-            calls = [("up", [arrived(hop, 0)]), ("down", [arrived(hop, 1)])]
-        else:
-            calls = [("one", [arrived(hop, 0), arrived(hop, 1)])]
-        for way, chunks in calls:
-            out, *state = dots_call(scalars, fidx, src, chunks, state, planes, hop, way)
-            dots.append(out)
-            places.append((hop, way))
-
-    heads, tails = {0: first}, {0: rest}
-    heads[1] = moved(first, 1)
-    got = together(*heads[1], *rest, source_vecs)
-    heads[1], tails[0], held = list(got[:2]), list(got[2:-1]), got[-1]
-    sources = [held] + [shift(held, "width", width, d) for d in range(1, width)]
-    src = []
-    for turn in range(2, planes + 1):
-        if turn >= 4:
-            for hop in range(len(set(h for h, _ in places)), turn - 2):
-                use(hop)
+    for place, (hop, way) in enumerate(queue):
+        if place == AHEAD:
             own_again, state[0] = together(fidx_own, state[0])
             fidx = over_reps(own_again)
-            late, far = tails[turn - 2], heads[turn - 1]
-            got = together(*late, *far, fidx)
-            tails[turn - 2], heads[turn - 1] = list(got[: len(late)]), list(got[len(late) : -1])
-            fidx = got[-1]
-        fresh = moved(tails[turn - 2], turn - 1)
-        ahead = moved(heads[turn - 1], turn) if turn < planes else []
-        if turn == 2:
-            got = together(*fresh, *ahead, *sources[1:])
-            sources[1:] = got[len(fresh) + len(ahead) :]
-            src = [normalize_rows(sources)]
-            for e in range(1, reps):
-                src.append(shift(src[0], "rep", reps, e))
+            *late, fidx = together(*tails[2], fidx)
+            tails[2] = list(late)
+            for later in range(3, planes):
+                tails[later] = moved(tails[later - 1], later)
+        if way == "own":
+            chunks = [first + rest]
         else:
-            got = together(*fresh, *ahead)
-        tails[turn - 1] = list(got[: len(fresh)])
-        heads[turn] = list(got[len(fresh) : len(fresh) + len(ahead)])
-    for hop in range(len(set(h for h, _ in places)), planes):
-        use(hop)
+            sides = {"up": (0,), "down": (1,), "one": (0, 1)}[way]
+            chunks = [arrived(hop, side) for side in sides]
+        out, *state = dots_call(scalars, fidx, src, chunks, state, planes, hop, way)
+        dots.append(out)
+        places.append((hop, way))
 
     def over_planes(values):
         if planes > 4:

time: 140 us -> 125 us (0.89)
  local copies, waits for them, and re-layouts: 18.3 us -> 10.9 us
  starting transfers between devices: 31.8 us -> 25.3 us
  waiting for transfers between devices: 46.1 us -> 44.4 us
    ppermute x8, waiting for transfers between devices: 19.9 us -> 8.07 us  [shift(): lax.ppermute(values, axis, [((i + by) % count, i) for i in range(count)])]
    ppermute x12, waiting for transfers between devices: 26.2 us -> 36.4 us  [moved(): out += [lax.ppermute(c, 'shard', pairs) for c in side]]
    unnamed x60 -> x28, local copies, waits for them, and re-layouts: 16.9 us -> 9.52 us
    ppermute x12, starting transfers between devices: 24.8 us -> 19.2 us  [moved(): out += [lax.ppermute(c, 'shard', pairs) for c in side]]
  transfers between devices with their start and end apart: 20 -> 20, of which waited for: 9 -> 10; matrix products, arithmetic and copies ran while one was open for 0% -> 1% of each run, Pallas kernels for 16% -> 18%
where the time goes in v3:
time: 125 us; the launch traced here: 124 us
  waiting for transfers between devices  44.4 us (36%)
  Pallas kernels  33.2 us (27%)
  starting transfers between devices  25.3 us (20%)
  local copies, waits for them, and re-layouts  10.9 us (9%)
  blocking collectives  7.17 us (6%)
  other arithmetic  2.32 us (2%)
    ppermute x12, waiting for transfers between devices, moved(): out += [lax.ppermute(c, 'shard', pairs) for c in side]  36.4 us
    pallas_call x5, Pallas kernels, dots_call(): pl.pallas_call(functools.partial(dots_kernel, reps, width, pairs, planes,...  28 us
    ppermute x12, starting transfers between devices, moved(): out += [lax.ppermute(c, 'shard', pairs) for c in side]  19.2 us
    unnamed x28, local copies, waits for them, and re-layouts  9.52 us
    ppermute x8, waiting for transfers between devices, shift(): lax.ppermute(values, axis, [((i + by) % count, i) for i in range(count)])  8.07 us
    all_gather x1, blocking collectives, on_device(): gathered = lax.all_gather(lines, ('width', 'rep'), axis=0, tiled=False)  7.17 us
    ppermute x8, starting transfers between devices, shift(): lax.ppermute(values, axis, [((i + by) % count, i) for i in range(count)])  6.09 us
    pallas_call x1, Pallas kernels, margin_call(): pl.pallas_call(functools.partial(margin_kernel, places, terms), grid=(len...  2.97 us
  transfers between devices with their start and end apart: 20, of which 10 were waited for; matrix products, arithmetic and copies ran while one was open for 1% of the time, Pallas kernels for 18%

profile of v3, /device:TPU:0, one launch (start us, length us, event | category | flops | bytes accessed | tf_op | source)
XLA Modules:
  0.0 124.2 jit_solution(15577347375882736795)
XLA Ops:
  1.5 1.3 %constant_dynamic-slice_fusion = (bf16[512,512]{1,0:T(8,128)(2,1)S(1)}, bf16[512,512]{1,0:T(8,128)(2,1)S(1)}) fusion(bf16[1024,512]{1,0:T(8,128)(2,1)} %param.8, s32[]{:T(128)S(6)} %select_n.18, s32[]{:T(128)S(6)} %select_n.17), kind=kLoop, calls=%fused_computation.21 | loop fusion | bytes 2097160 | tf_op jit(solution)/shard_map/dynamic_slice | solution.py:316
  2.9 3.0 %collective-permute-start.2 = (bf16[528,512]{1,0:T(8,128)(2,1)S(1)}, bf16[528,512]{1,0:T(8,128)(2,1)S(1)}, u32[]{:S(2)}, u32[]{:S(2)}) collective-permute-start(bf16[528,512]{1,0:T(8,128)(2,1)S(1)} %pad_maximum_fusion), channel_id=1, source_target_pairs={{2,0},{0,2},{3,1},{1,3},{6,4},{4,6},{7,5},{5,7},{10,8},{8,10},{11,... | collective-permute-start | bytes 1622024 | tf_op jit(solution)/shard_map/ppermute | solution.py:319
  5.9 3.5 %collective-permute-start = (bf16[512,512]{1,0:T(8,128)(2,1)S(1)}, bf16[512,512]{1,0:T(8,128)(2,1)S(1)}, u32[]{:S(2)}, u32[]{:S(2)}) collective-permute-start(bf16[512,512]{1,0:T(8,128)(2,1)S(1)} %get-tuple-element.58.refs_3_), channel_id=1, source_target_pairs={{0,4},{4,8},{8,12},{1,5},{5,9},{9,13},{2,6},{6,10},{10,14},{3,7},{... | collective-permute-start | bytes 1572872 | tf_op jit(solution)/shard_map/ppermute | solution.py:346
  9.4 1.3 %collective-permute-start.1 = (bf16[512,512]{1,0:T(8,128)(2,1)S(1)}, bf16[512,512]{1,0:T(8,128)(2,1)S(1)}, u32[]{:S(2)}, u32[]{:S(2)}) collective-permute-start(bf16[512,512]{1,0:T(8,128)(2,1)S(1)} %get-tuple-element.58.refs_3_), channel_id=1, source_target_pairs={{4,0},{8,4},{12,8},{5,1},{9,5},{13,9},{6,2},{10,6},{14,10},{7,3},{... | collective-permute-start | bytes 1572872 | tf_op jit(solution)/shard_map/ppermute | solution.py:346
  11.5 1.2 collective-permute-done.3
  12.7 7.6 %collective-permute-done.refs_3_ = bf16[512,512]{1,0:T(8,128)(2,1)S(1)} collective-permute-done((bf16[512,512]{1,0:T(8,128)(2,1)S(1)}, bf16[512,512]{1,0:T(8,128)(2,1)S(1)}, u32[]{:S(2)}, u32[]{:S(2)}) %collective-permute-start) | collective-permute-done | bytes 524320 | tf_op jit(solution)/shard_map/ppermute | solution.py:346
  20.3 4.1 %collective-permute-done.1.refs_3_ = bf16[512,512]{1,0:T(8,128)(2,1)S(1)} collective-permute-done((bf16[512,512]{1,0:T(8,128)(2,1)S(1)}, bf16[512,512]{1,0:T(8,128)(2,1)S(1)}, u32[]{:S(2)}, u32[]{:S(2)}) %collective-permute-start.1) | collective-permute-done | bytes 524320 | tf_op jit(solution)/shard_map/ppermute | solution.py:346
  25.0 4.3 %collective-permute-start.5 = (bf16[528,512]{1,0:T(8,128)(2,1)S(1)}, bf16[528,512]{1,0:T(8,128)(2,1)}, u32[]{:S(2)}, u32[]{:S(2)}) collective-permute-start(bf16[528,512]{1,0:T(8,128)(2,1)S(1)} %collective-permute-done.2.refs_4_), channel_id=1, source_target_pairs={{0,4},{4,8},{8,12},{1,5},{5,9},{9,13},{2,6},{6,10},{10,14},{3,7},{... | collective-permute-start | bytes 1622024 | tf_op jit(solution)/shard_map/ppermute | solution.py:346
  29.2 1.3 %collective-permute-start.6 = (bf16[528,512]{1,0:T(8,128)(2,1)S(1)}, bf16[528,512]{1,0:T(8,128)(2,1)S(1)}, u32[]{:S(2)}, u32[]{:S(2)}) collective-permute-start(bf16[528,512]{1,0:T(8,128)(2,1)S(1)} %collective-permute-done.2.refs_4_), channel_id=1, source_target_pairs={{4,0},{8,4},{12,8},{5,1},{9,5},{13,9},{6,2},{10,6},{14,10},{7,3},{... | collective-permute-start | bytes 1622024 | tf_op jit(solution)/shard_map/ppermute | solution.py:346
  32.8 1.3 %collective-permute-start.8 = (bf16[512,512]{1,0:T(8,128)(2,1)S(1)}, bf16[512,512]{1,0:T(8,128)(2,1)S(1)}, u32[]{:S(2)}, u32[]{:S(2)}) collective-permute-start(bf16[512,512]{1,0:T(8,128)(2,1)S(1)} %collective-permute-done.1.refs_3_), channel_id=1, source_target_pairs={{4,0},{8,4},{5,1},{9,5},{6,2},{10,6},{7,3},{11,7},{20,16},{24,20},... | collective-permute-start | bytes 1572872 | tf_op jit(solution)/shard_map/ppermute | solution.py:346
  34.9 19.4 %collective-permute-done.8.refs_5_ = bf16[512,512]{1,0:T(8,128)(2,1)S(1)} collective-permute-done((bf16[512,512]{1,0:T(8,128)(2,1)S(1)}, bf16[512,512]{1,0:T(8,128)(2,1)S(1)}, u32[]{:S(2)}, u32[]{:S(2)}) %collective-permute-start.8) | collective-permute-done | bytes 524320 | tf_op jit(solution)/shard_map/ppermute | solution.py:346
  55.1 1.2 copy-done.3
  57.3 1.5 %collective-permute-start.10 = (bf16[528,512]{1,0:T(8,128)(2,1)}, bf16[528,512]{1,0:T(8,128)(2,1)}, u32[]{:S(2)}, u32[]{:S(2)}) collective-permute-start(bf16[528,512]{1,0:T(8,128)(2,1)} %collective-permute-done.5.refs_4_), channel_id=1, source_target_pairs={{4,8},{8,12},{5,9},{9,13},{6,10},{10,14},{7,11},{11,15},{20,24},{2... | collective-permute-start | bytes 1622024 | tf_op jit(solution)/shard_map/ppermute | solution.py:346
  58.8 1.3 %collective-permute-start.11 = (bf16[528,512]{1,0:T(8,128)(2,1)S(1)}, bf16[528,512]{1,0:T(8,128)(2,1)}, u32[]{:S(2)}, u32[]{:S(2)}) collective-permute-start(bf16[528,512]{1,0:T(8,128)(2,1)S(1)} %collective-permute-done.6.refs_4_), channel_id=1, source_target_pairs={{4,0},{8,4},{5,1},{9,5},{6,2},{10,6},{7,3},{11,7},{20,16},{24,20},... | collective-permute-start | bytes 1622024 | tf_op jit(solution)/shard_map/ppermute | solution.py:346
  60.1 1.4 %collective-permute-done.9.refs_2_ = bf16[1024,1024]{1,0:T(8,128)(2,1)} collective-permute-done((bf16[1024,1024]{1,0:T(8,128)(2,1)S(1)}, bf16[1024,1024]{1,0:T(8,128)(2,1)}, u32[]{:S(2)}, u32[]{:S(2)}) %collective-permute-start.9) | collective-permute-done | bytes 2097184 | tf_op jit(solution)/shard_map/ppermute | solution.py:319
  62.6 5.5 %shard_map.95 = (f32[2,512,1024]{2,1,0:T(8,128)S(1)}, f32[5,1,512]{2,1,0:T(1,128)S(1)}, f32[2,1,1024]{2,1,0:T(1,128)S(1)}) custom-call(s32[3]{0:T(128)S(1)} %pad_add_fusion.2.sc_ref, s32[2,4,1024]{2,1,0:T(4,128)S(1)} %pad_add_fusion.refs_0_, bf16[1024,1024]{1,0:T(8,128)(2,1)S(1)} %shard_map.94.refs_1_, bf16[1024,1024]{1,0:T(8,128)(2,1)} %collective-permute-done.9.refs_2_, ...), custom_call_target="tpu_custom_call" | custom-call | flops 2147483648 | bytes 4194304 | tf_op jit(solution)/shard_map/pallas_call | solution.py:148
  68.1 2.0 %copy-done.1 = f32[2,512,1024]{2,1,0:T(8,128)} copy-done((f32[2,512,1024]{2,1,0:T(8,128)}, f32[2,512,1024]{2,1,0:T(8,128)S(1)}, u32[]{:S(2)}) %copy-start.1) | copy-done | bytes 4194328
  70.9 1.3 %collective-permute-start.15 = (bf16[512,512]{1,0:T(8,128)(2,1)}, bf16[512,512]{1,0:T(8,128)(2,1)S(1)}, u32[]{:S(2)}, u32[]{:S(2)}) collective-permute-start(bf16[512,512]{1,0:T(8,128)(2,1)} %copy-done.12), channel_id=1, source_target_pairs={{4,0},{5,1},{6,2},{7,3},{20,16},{21,17},{22,18},{23,19}} | collective-permute-start | bytes 1572872 | tf_op jit(solution)/shard_map/ppermute | solution.py:346
  72.2 3.2 %collective-permute-done.11.refs_6_ = bf16[528,512]{1,0:T(8,128)(2,1)} collective-permute-done((bf16[528,512]{1,0:T(8,128)(2,1)S(1)}, bf16[528,512]{1,0:T(8,128)(2,1)}, u32[]{:S(2)}, u32[]{:S(2)}) %collective-permute-start.11) | collective-permute-done | bytes 540704 | tf_op jit(solution)/shard_map/ppermute | solution.py:346
  76.1 1.5 %collective-permute-start.16 = (bf16[528,512]{1,0:T(8,128)(2,1)}, bf16[528,512]{1,0:T(8,128)(2,1)S(1)}, u32[]{:S(2)}, u32[]{:S(2)}) collective-permute-start(bf16[528,512]{1,0:T(8,128)(2,1)} %collective-permute-done.11.refs_6_), channel_id=1, source_target_pairs={{4,0},{5,1},{6,2},{7,3},{20,16},{21,17},{22,18},{23,19}} | collective-permute-start | bytes 1622024 | tf_op jit(solution)/shard_map/ppermute | solution.py:346
  78.6 5.6 %shard_map.96 = (f32[2,512,1024]{2,1,0:T(8,128)S(1)}, f32[5,1,512]{2,1,0:T(1,128)S(1)}, f32[2,1,1024]{2,1,0:T(1,128)S(1)}) custom-call(s32[3]{0:T(128)S(1)} %pad_add_fusion.2.sc_ref, s32[2,4,1024]{2,1,0:T(4,128)S(1)} %pad_add_fusion.1.refs_0_, bf16[1024,1024]{1,0:T(8,128)(2,1)S(1)} %shard_map.94.refs_1_, bf16[1024,1024]{1,0:T(8,128)(2,1)} %collective-permute-done.9.refs_2_, ...), custom_call_target="tpu_custom_call" | custom-call | flops 2147483648 | bytes 4194304 | tf_op jit(solution)/shard_map/pallas_call | solution.py:148
  85.3 5.5 %shard_map.97 = (f32[2,512,1024]{2,1,0:T(8,128)S(1)}, f32[5,1,512]{2,1,0:T(1,128)S(1)}, f32[2,1,1024]{2,1,0:T(1,128)S(1)}) custom-call(s32[3]{0:T(128)S(1)} %pad_add_fusion.2.sc_ref, s32[2,4,1024]{2,1,0:T(4,128)S(1)} %pad_add_fusion.1.refs_0_, bf16[1024,1024]{1,0:T(8,128)(2,1)S(1)} %shard_map.94.refs_1_, bf16[1024,1024]{1,0:T(8,128)(2,1)} %collective-permute-done.9.refs_2_, ...), custom_call_target="tpu_custom_call" | custom-call | flops 2147483648 | bytes 4194304 | tf_op jit(solution)/shard_map/pallas_call | solution.py:148
  90.8 5.9 %shard_map.98 = (f32[2,512,1024]{2,1,0:T(8,128)S(1)}, f32[5,1,512]{2,1,0:T(1,128)S(1)}, f32[2,1,1024]{2,1,0:T(1,128)S(1)}) custom-call(s32[3]{0:T(128)S(1)} %pad_add_fusion.2.sc_ref, s32[2,4,1024]{2,1,0:T(4,128)S(1)} %pad_add_fusion.1.refs_0_, bf16[1024,1024]{1,0:T(8,128)(2,1)S(1)} %shard_map.94.refs_1_, bf16[1024,1024]{1,0:T(8,128)(2,1)} %collective-permute-done.9.refs_2_, ...), custom_call_target="tpu_custom_call" | custom-call | flops 2147483648 | bytes 4194304 | tf_op jit(solution)/shard_map/pallas_call | solution.py:148
  96.7 2.1 %collective-permute-done.16.refs_6_ = bf16[528,512]{1,0:T(8,128)(2,1)S(1)} collective-permute-done((bf16[528,512]{1,0:T(8,128)(2,1)}, bf16[528,512]{1,0:T(8,128)(2,1)S(1)}, u32[]{:S(2)}, u32[]{:S(2)}) %collective-permute-start.16) | collective-permute-done | bytes 540704 | tf_op jit(solution)/shard_map/ppermute | solution.py:346
  98.8 5.6 %shard_map.99 = (f32[2,512,1024]{2,1,0:T(8,128)S(1)}, f32[5,1,512]{2,1,0:T(1,128)S(1)}, f32[2,1,1024]{2,1,0:T(1,128)S(1)}) custom-call(s32[3]{0:T(128)S(1)} %pad_add_fusion.2.sc_ref, s32[2,4,1024]{2,1,0:T(4,128)S(1)} %pad_add_fusion.1.refs_0_, bf16[1024,1024]{1,0:T(8,128)(2,1)S(1)} %shard_map.94.refs_1_, bf16[1024,1024]{1,0:T(8,128)(2,1)} %collective-permute-done.9.refs_2_, ...), custom_call_target="tpu_custom_call" | custom-call | flops 2147483648 | bytes 4194304 | tf_op jit(solution)/shard_map/pallas_call | solution.py:148
  104.4 1.5 %collective-permute-start.17 = (f32[5,1,512]{2,1,0:T(1,128)S(1)}, f32[5,1,512]{2,1,0:T(1,128)S(1)}, u32[]{:S(2)}, u32[]{:S(2)}) collective-permute-start(f32[5,1,512]{2,1,0:T(1,128)S(1)} %get-tuple-element.52.refs_5_), channel_id=1, source_target_pairs={{4,0},{8,4},{12,8},{0,12},{5,1},{9,5},{13,9},{1,13},{6,2},{10,6},{... | collective-permute-start | bytes 30728 | tf_op jit(solution)/shard_map/ppermute | solution.py:319
  106.7 1.4 %collective-permute-done.17.refs_6_ = f32[5,1,512]{2,1,0:T(1,128)S(1)} collective-permute-done((f32[5,1,512]{2,1,0:T(1,128)S(1)}, f32[5,1,512]{2,1,0:T(1,128)S(1)}, u32[]{:S(2)}, u32[]{:S(2)}) %collective-permute-start.17) | collective-permute-done | bytes 10272 | tf_op jit(solution)/shard_map/ppermute | solution.py:319
  108.1 2.5 %collective-permute-done.18.refs_7_ = f32[5,1,512]{2,1,0:T(1,128)S(1)} collective-permute-done((f32[5,1,512]{2,1,0:T(1,128)S(1)}, f32[5,1,512]{2,1,0:T(1,128)S(1)}, u32[]{:S(2)}, u32[]{:S(2)}) %collective-permute-start.18) | collective-permute-done | bytes 10272 | tf_op jit(solution)/shard_map/ppermute | solution.py:319
  110.6 1.5 %collective-permute-done.19.refs_8_ = f32[5,1,512]{2,1,0:T(1,128)S(1)} collective-permute-done((f32[5,1,512]{2,1,0:T(1,128)S(1)}, f32[5,1,512]{2,1,0:T(1,128)S(1)}, u32[]{:S(2)}, u32[]{:S(2)}) %collective-permute-start.19) | collective-permute-done | bytes 10272 | tf_op jit(solution)/shard_map/ppermute | solution.py:319
  112.1 3.0 %shard_map.100 = f32[2,16,1024]{2,1,0:T(8,128)S(1)} custom-call(s32[3]{0:T(128)S(1)} %pad_add_fusion.2.sc_ref, f32[2,512,1024]{2,1,0:T(8,128)S(1)} %copy-done.2, f32[2,512,1024]{2,1,0:T(8,128)S(1)} %get-tuple-element.40.refs_1_, f32[2,512,1024]{2,1,0:T(8,128)S(1)} %get-tuple-element.43.refs_2_, f32[2,512,1024]{2,1,0:T(8,128)S(1)} %get-tuple-element.48.refs_3_, ...), custom_call_target="tpu_custom_call" | custom-call | flops 524288 | bytes 524288 | tf_op jit(solution)/shard_map/pallas_call | solution.py:224
  115.1 7.2 %all-gather = f32[8,16,1024]{2,1,0:T(8,128)S(1)} all-gather(f32[2,16,1024]{2,1,0:T(8,128)S(1)} %shard_map.100), channel_id=2, replica_groups=mesh['groups'=2,'shard'=4,'width'=2,'rep'=2] {'width','rep'}, dimensions={0}, use_global_device_ids=true | all-gather | bytes 655360 | tf_op jit(solution)/shard_map/all_gather | solution.py:398
  122.3 1.3 %shard_map.101 = (f32[8,1024]{1,0:T(8,128)}, f32[1,1024]{1,0:T(1,128)}, bf16[1,1024]{1,0:T(2,128)(2,1)S(1)}) custom-call(s32[3]{0:T(128)S(1)} %pad_add_fusion.2.sc_ref, s32[16]{0:T(128)S(1)} %fusion.8.list_ref, f32[4,2,16,1024]{3,2,1,0:T(8,128)S(1)} %bitcast.38), custom_call_target="tpu_custom_call" | custom-call | tf_op jit(solution)/shard_map/pallas_call | solution.py:277
  (57 shorter events, 13.2 us)
Async XLA Ops:
  0.6 106.0 %copy-start = (s32[4,16]{1,0:T(4,128)S(1)}, s32[4,16]{1,0:T(4,128)}, u32[]{:S(2)}) copy-start(s32[4,16]{1,0:T(4,128)} %param.13) | copy-start | bytes 772
  2.9 21.5 %collective-permute-start.2 = (bf16[528,512]{1,0:T(8,128)(2,1)S(1)}, bf16[528,512]{1,0:T(8,128)(2,1)S(1)}, u32[]{:S(2)}, u32[]{:S(2)}) collective-permute-start(bf16[528,512]{1,0:T(8,128)(2,1)S(1)} %pad_maximum_fusion), channel_id=1, source_target_pairs={{2,0},{0,2},{3,1},{1,3},{6,4},{4,6},{7,5},{5,7},{10,8},{8,10},{11,... | collective-permute-start | bytes 1622024 | tf_op jit(solution)/shard_map/ppermute | solution.py:319
  5.9 14.4 %collective-permute-start = (bf16[512,512]{1,0:T(8,128)(2,1)S(1)}, bf16[512,512]{1,0:T(8,128)(2,1)S(1)}, u32[]{:S(2)}, u32[]{:S(2)}) collective-permute-start(bf16[512,512]{1,0:T(8,128)(2,1)S(1)} %get-tuple-element.58.refs_3_), channel_id=1, source_target_pairs={{0,4},{4,8},{8,12},{1,5},{5,9},{9,13},{2,6},{6,10},{10,14},{3,7},{... | collective-permute-start | bytes 1572872 | tf_op jit(solution)/shard_map/ppermute | solution.py:346
  9.4 15.0 %collective-permute-start.1 = (bf16[512,512]{1,0:T(8,128)(2,1)S(1)}, bf16[512,512]{1,0:T(8,128)(2,1)S(1)}, u32[]{:S(2)}, u32[]{:S(2)}) collective-permute-start(bf16[512,512]{1,0:T(8,128)(2,1)S(1)} %get-tuple-element.58.refs_3_), channel_id=1, source_target_pairs={{4,0},{8,4},{12,8},{5,1},{9,5},{13,9},{6,2},{10,6},{14,10},{7,3},{... | collective-permute-start | bytes 1572872 | tf_op jit(solution)/shard_map/ppermute | solution.py:346
  11.5 1.2 collective-permute-start.3
  24.4 30.7 %collective-permute-start.4 = (bf16[1024,512]{1,0:T(8,128)(2,1)}, bf16[1024,512]{1,0:T(8,128)(2,1)S(1)}, u32[]{:S(2)}, u32[]{:S(2)}) collective-permute-start(bf16[1024,512]{1,0:T(8,128)(2,1)} %refs_0_), channel_id=1, source_target_pairs={{2,0},{0,2},{3,1},{1,3},{6,4},{4,6},{7,5},{5,7},{10,8},{8,10},{11,... | collective-permute-start | bytes 3145736 | tf_op jit(solution)/shard_map/ppermute | solution.py:319
  25.0 29.3 %collective-permute-start.5 = (bf16[528,512]{1,0:T(8,128)(2,1)S(1)}, bf16[528,512]{1,0:T(8,128)(2,1)}, u32[]{:S(2)}, u32[]{:S(2)}) collective-permute-start(bf16[528,512]{1,0:T(8,128)(2,1)S(1)} %collective-permute-done.2.refs_4_), channel_id=1, source_target_pairs={{0,4},{4,8},{8,12},{1,5},{5,9},{9,13},{2,6},{6,10},{10,14},{3,7},{... | collective-permute-start | bytes 1622024 | tf_op jit(solution)/shard_map/ppermute | solution.py:346
  29.2 25.1 %collective-permute-start.6 = (bf16[528,512]{1,0:T(8,128)(2,1)S(1)}, bf16[528,512]{1,0:T(8,128)(2,1)S(1)}, u32[]{:S(2)}, u32[]{:S(2)}) collective-permute-start(bf16[528,512]{1,0:T(8,128)(2,1)S(1)} %collective-permute-done.2.refs_4_), channel_id=1, source_target_pairs={{4,0},{8,4},{12,8},{5,1},{9,5},{13,9},{6,2},{10,6},{14,10},{7,3},{... | collective-permute-start | bytes 1622024 | tf_op jit(solution)/shard_map/ppermute | solution.py:346
  31.3 3.6 %collective-permute-start.7 = (bf16[512,512]{1,0:T(8,128)(2,1)S(1)}, bf16[512,512]{1,0:T(8,128)(2,1)S(1)}, u32[]{:S(2)}, u32[]{:S(2)}) collective-permute-start(bf16[512,512]{1,0:T(8,128)(2,1)S(1)} %collective-permute-done.refs_3_), channel_id=1, source_target_pairs={{4,8},{8,12},{5,9},{9,13},{6,10},{10,14},{7,11},{11,15},{20,24},{2... | collective-permute-start | bytes 1572872 | tf_op jit(solution)/shard_map/ppermute | solution.py:346
  32.8 21.5 %collective-permute-start.8 = (bf16[512,512]{1,0:T(8,128)(2,1)S(1)}, bf16[512,512]{1,0:T(8,128)(2,1)S(1)}, u32[]{:S(2)}, u32[]{:S(2)}) collective-permute-start(bf16[512,512]{1,0:T(8,128)(2,1)S(1)} %collective-permute-done.1.refs_3_), channel_id=1, source_target_pairs={{4,0},{8,4},{5,1},{9,5},{6,2},{10,6},{7,3},{11,7},{20,16},{24,20},... | collective-permute-start | bytes 1572872 | tf_op jit(solution)/shard_map/ppermute | solution.py:346
  34.1 0.8 copy-start.6
  34.9 19.4 %copy-start.10 = (bf16[512,512]{1,0:T(8,128)(2,1)}, bf16[512,512]{1,0:T(8,128)(2,1)S(1)}, u32[]{:S(2)}) copy-start(bf16[512,512]{1,0:T(8,128)(2,1)S(1)} %collective-permute-done.7.refs_3_) | copy-start | bytes 1572868
  54.3 0.8 copy-start.12
  55.1 1.2 copy-start.3
  57.2 4.4 %collective-permute-start.9 = (bf16[1024,1024]{1,0:T(8,128)(2,1)S(1)}, bf16[1024,1024]{1,0:T(8,128)(2,1)}, u32[]{:S(2)}, u32[]{:S(2)}) collective-permute-start(bf16[1024,1024]{1,0:T(8,128)(2,1)S(1)} %shard_map.94.refs_1_), channel_id=1, source_target_pairs={{1,0},{0,1},{3,2},{2,3},{5,4},{4,5},{7,6},{6,7},{9,8},{8,9},{11,10... | collective-permute-start | bytes 6291464 | tf_op jit(solution)/shard_map/ppermute | solution.py:319
  57.3 14.9 %collective-permute-start.10 = (bf16[528,512]{1,0:T(8,128)(2,1)}, bf16[528,512]{1,0:T(8,128)(2,1)}, u32[]{:S(2)}, u32[]{:S(2)}) collective-permute-start(bf16[528,512]{1,0:T(8,128)(2,1)} %collective-permute-done.5.refs_4_), channel_id=1, source_target_pairs={{4,8},{8,12},{5,9},{9,13},{6,10},{10,14},{7,11},{11,15},{20,24},{2... | collective-permute-start | bytes 1622024 | tf_op jit(solution)/shard_map/ppermute | solution.py:346
  58.8 16.7 %collective-permute-start.11 = (bf16[528,512]{1,0:T(8,128)(2,1)S(1)}, bf16[528,512]{1,0:T(8,128)(2,1)}, u32[]{:S(2)}, u32[]{:S(2)}) collective-permute-start(bf16[528,512]{1,0:T(8,128)(2,1)S(1)} %collective-permute-done.6.refs_4_), channel_id=1, source_target_pairs={{4,0},{8,4},{5,1},{9,5},{6,2},{10,6},{7,3},{11,7},{20,16},{24,20},... | collective-permute-start | bytes 1622024 | tf_op jit(solution)/shard_map/ppermute | solution.py:346
  61.6 1.0 copy-start.5
  68.1 2.0 %copy-start.1 = (f32[2,512,1024]{2,1,0:T(8,128)}, f32[2,512,1024]{2,1,0:T(8,128)S(1)}, u32[]{:S(2)}) copy-start(f32[2,512,1024]{2,1,0:T(8,128)S(1)} %get-tuple-element.34.refs_0_) | copy-start | bytes 12582916
  70.1 2.1 %collective-permute-start.12 = (s32[4,1024]{1,0:T(4,128)S(1)}, s32[4,1024]{1,0:T(4,128)S(1)}, u32[]{:S(2)}, u32[]{:S(2)}) collective-permute-start(s32[4,1024]{1,0:T(4,128)S(1)} %get-tuple-element.36), channel_id=1, source_target_pairs={{1,0},{0,1},{3,2},{2,3},{5,4},{4,5},{7,6},{6,7},{9,8},{8,9},{11,10... | collective-permute-start | bytes 49160 | tf_op jit(solution)/shard_map/ppermute | solution.py:319
  70.2 26.5 %collective-permute-start.13 = (bf16[512,512]{1,0:T(8,128)(2,1)}, bf16[512,512]{1,0:T(8,128)(2,1)S(1)}, u32[]{:S(2)}, u32[]{:S(2)}) collective-permute-start(bf16[512,512]{1,0:T(8,128)(2,1)} %copy-done.10), channel_id=1, source_target_pairs={{8,12},{9,13},{10,14},{11,15},{24,28},{25,29},{26,30},{27,31}} | collective-permute-start | bytes 1572872 | tf_op jit(solution)/shard_map/ppermute | solution.py:346
  70.9 25.8 %collective-permute-start.15 = (bf16[512,512]{1,0:T(8,128)(2,1)}, bf16[512,512]{1,0:T(8,128)(2,1)S(1)}, u32[]{:S(2)}, u32[]{:S(2)}) collective-permute-start(bf16[512,512]{1,0:T(8,128)(2,1)} %copy-done.12), channel_id=1, source_target_pairs={{4,0},{5,1},{6,2},{7,3},{20,16},{21,17},{22,18},{23,19}} | collective-permute-start | bytes 1572872 | tf_op jit(solution)/shard_map/ppermute | solution.py:346
  75.4 21.3 %collective-permute-start.14 = (bf16[528,512]{1,0:T(8,128)(2,1)}, bf16[528,512]{1,0:T(8,128)(2,1)S(1)}, u32[]{:S(2)}, u32[]{:S(2)}) collective-permute-start(bf16[528,512]{1,0:T(8,128)(2,1)} %collective-permute-done.10.refs_4_), channel_id=1, source_target_pairs={{8,12},{9,13},{10,14},{11,15},{24,28},{25,29},{26,30},{27,31}} | collective-permute-start | bytes 1622024 | tf_op jit(solution)/shard_map/ppermute | solution.py:346
  76.1 22.7 %collective-permute-start.16 = (bf16[528,512]{1,0:T(8,128)(2,1)}, bf16[528,512]{1,0:T(8,128)(2,1)S(1)}, u32[]{:S(2)}, u32[]{:S(2)}) collective-permute-start(bf16[528,512]{1,0:T(8,128)(2,1)} %collective-permute-done.11.refs_6_), channel_id=1, source_target_pairs={{4,0},{5,1},{6,2},{7,3},{20,16},{21,17},{22,18},{23,19}} | collective-permute-start | bytes 1622024 | tf_op jit(solution)/shard_map/ppermute | solution.py:346
  77.6 1.0 copy-start.9
  78.6 12.2 %copy-start.11 = (bf16[512,512]{1,0:T(8,128)(2,1)S(1)}, bf16[512,512]{1,0:T(8,128)(2,1)}, u32[]{:S(2)}) copy-start(bf16[512,512]{1,0:T(8,128)(2,1)} %copy-done.10) | copy-start | bytes 1572868
  78.6 12.2 %copy-start.13 = (bf16[512,512]{1,0:T(8,128)(2,1)S(1)}, bf16[512,512]{1,0:T(8,128)(2,1)}, u32[]{:S(2)}) copy-start(bf16[512,512]{1,0:T(8,128)(2,1)} %copy-done.12) | copy-start | bytes 1572868
  84.3 1.0 copy-start.7
  96.7 15.5 %copy-start.2 = (f32[2,512,1024]{2,1,0:T(8,128)S(1)}, f32[2,512,1024]{2,1,0:T(8,128)}, u32[]{:S(2)}) copy-start(f32[2,512,1024]{2,1,0:T(8,128)} %copy-done.1) | copy-start | bytes 12582916
  104.4 3.7 %collective-permute-start.17 = (f32[5,1,512]{2,1,0:T(1,128)S(1)}, f32[5,1,512]{2,1,0:T(1,128)S(1)}, u32[]{:S(2)}, u32[]{:S(2)}) collective-permute-start(f32[5,1,512]{2,1,0:T(1,128)S(1)} %get-tuple-element.52.refs_5_), channel_id=1, source_target_pairs={{4,0},{8,4},{12,8},{0,12},{5,1},{9,5},{13,9},{1,13},{6,2},{10,6},{... | collective-permute-start | bytes 30728 | tf_op jit(solution)/shard_map/ppermute | solution.py:319
  105.9 4.7 %collective-permute-start.18 = (f32[5,1,512]{2,1,0:T(1,128)S(1)}, f32[5,1,512]{2,1,0:T(1,128)S(1)}, u32[]{:S(2)}, u32[]{:S(2)}) collective-permute-start(f32[5,1,512]{2,1,0:T(1,128)S(1)} %get-tuple-element.52.refs_5_), channel_id=1, source_target_pairs={{8,0},{12,4},{0,8},{4,12},{9,1},{13,5},{1,9},{5,13},{10,2},{14,6},... | collective-permute-start | bytes 30728 | tf_op jit(solution)/shard_map/ppermute | solution.py:319
  106.7 5.5 %collective-permute-start.19 = (f32[5,1,512]{2,1,0:T(1,128)S(1)}, f32[5,1,512]{2,1,0:T(1,128)S(1)}, u32[]{:S(2)}, u32[]{:S(2)}) collective-permute-start(f32[5,1,512]{2,1,0:T(1,128)S(1)} %get-tuple-element.52.refs_5_), channel_id=1, source_target_pairs={{12,0},{0,4},{4,8},{8,12},{13,1},{1,5},{5,9},{9,13},{14,2},{2,6},{... | collective-permute-start | bytes 30728 | tf_op jit(solution)/shard_map/ppermute | solution.py:319
  (2 other events, 1.6 us)

commit v4 on v3

--- a/solution.py
+++ b/solution.py
@@ -74,66 +74,73 @@
     shard, wide, rep = sc_ref[0], sc_ref[1], sc_ref[2]
     plane, valid = plane_at(sc_ref, planes, hop, way)
 
-    values = []
-    for d in range(width):
-        value = chunk_refs[d][...].astype(jnp.float32)
-        for other in range(1, pairs):
-            value = value + chunk_refs[other * width + d][...].astype(jnp.float32)
-        if d == 1:
-            codes = value[rows:]
-            value = value[:rows]
-        values.append(value)
-    total = sum(jnp.sum(v * v, axis=1, keepdims=True) for v in values)
-    scale = lax.rsqrt(total / D + EPS)
-    for d, v in enumerate(values):
-        tgt[:, d * cols : (d + 1) * cols] = (v * scale).astype(jnp.bfloat16)
-
-    bidx = (codes[:K] * CODE + codes[K : 2 * K]).astype(jnp.int32)
-    base = (plane * reps + rep) * length + wide * rows
-    base = jnp.where(valid, base, 2 * planes * reps * length)
-    lane_ids = lax.broadcasted_iota(jnp.int32, (8, LANES), 1)
-    row_ids = lax.broadcasted_iota(jnp.int32, (8, length), 0)
-    for e in range(reps):
-        place = bidx - (shard * reps + lax.rem(rep + e, reps)) * length
-        hit = (place >= 0) & (place < length)
-        place = jnp.sum(jnp.where(hit, place + 1, 0), axis=0, keepdims=True) - 1
-        place = jnp.broadcast_to(place.astype(jnp.float32), (LANES, rows))
-        picks[...] = jnp.transpose(place).astype(jnp.int32)
-
-        s_ref[e] = lax.dot_general(
-            tgt[...],
-            src_refs[e][...],
-            (((1,), (1,)), ((), ())),
-            preferred_element_type=jnp.float32,
-        )
-        place = fidx_ref[e] - base
-        hit = (place >= 0) & (place < rows)
-        place = jnp.sum(jnp.where(hit, place + 1, 0), axis=0, keepdims=True) - 1
-        away = jnp.broadcast_to(place, (8, length)) - row_ids
-
-        def one_line(i, total):
-            line = pl.ds(pl.multiple_of(i * 8, 8), 8)
-            dots = s_ref[e, line, :]
-            pick = picks[line, :] - lane_ids
-            part = jnp.zeros((8, LANES), jnp.float32)
-            for g in range(groups):
-                one = dots[:, g * LANES : (g + 1) * LANES]
-                part = part + jnp.where(pick == g * LANES, one, 0.0)
-            if e > 0:
-                part = part + bsum[line, :]
-            bsum[line, :] = part
-            return total + jnp.where(away == i * 8, dots, 0.0)
-
-        total = lax.fori_loop(
-            0, rows // 8, one_line, jnp.zeros((8, length), jnp.float32), unroll=4
-        )
-        picked = jnp.sum(total, axis=0, keepdims=True)
-        f_ref[e] = picked if first else f_in[e] + picked
+    @pl.when(valid)
+    def _():
+        values = []
+        for d in range(width):
+            value = chunk_refs[d][...].astype(jnp.float32)
+            for other in range(1, pairs):
+                value = value + chunk_refs[other * width + d][...].astype(jnp.float32)
+            if d == 1:
+                codes = value[rows:]
+                value = value[:rows]
+            values.append(value)
+        total = sum(jnp.sum(v * v, axis=1, keepdims=True) for v in values)
+        scale = lax.rsqrt(total / D + EPS)
+        for d, v in enumerate(values):
+            tgt[:, d * cols : (d + 1) * cols] = (v * scale).astype(jnp.bfloat16)
+
+        bidx = (codes[:K] * CODE + codes[K : 2 * K]).astype(jnp.int32)
+        base = (plane * reps + rep) * length + wide * rows
+        lane_ids = lax.broadcasted_iota(jnp.int32, (8, LANES), 1)
+        row_ids = lax.broadcasted_iota(jnp.int32, (8, length), 0)
+        for e in range(reps):
+            place = bidx - (shard * reps + lax.rem(rep + e, reps)) * length
+            hit = (place >= 0) & (place < length)
+            place = jnp.sum(jnp.where(hit, place + 1, 0), axis=0, keepdims=True) - 1
+            place = jnp.broadcast_to(place.astype(jnp.float32), (LANES, rows))
+            picks[...] = jnp.transpose(place).astype(jnp.int32)
+
+            s_ref[e] = lax.dot_general(
+                tgt[...],
+                src_refs[e][...],
+                (((1,), (1,)), ((), ())),
+                preferred_element_type=jnp.float32,
+            )
+            place = fidx_ref[e] - base
+            hit = (place >= 0) & (place < rows)
+            place = jnp.sum(jnp.where(hit, place + 1, 0), axis=0, keepdims=True) - 1
+            away = jnp.broadcast_to(place, (8, length)) - row_ids
+
+            def one_line(i, total):
+                line = pl.ds(pl.multiple_of(i * 8, 8), 8)
+                dots = s_ref[e, line, :]
+                pick = picks[line, :] - lane_ids
+                part = jnp.zeros((8, LANES), jnp.float32)
+                for g in range(groups):
+                    one = dots[:, g * LANES : (g + 1) * LANES]
+                    part = part + jnp.where(pick == g * LANES, one, 0.0)
+                if e > 0:
+                    part = part + bsum[line, :]
+                bsum[line, :] = part
+                return total + jnp.where(away == i * 8, dots, 0.0)
+
+            total = lax.fori_loop(
+                0, rows // 8, one_line, jnp.zeros((8, length), jnp.float32), unroll=4
+            )
+            picked = jnp.sum(total, axis=0, keepdims=True)
+            f_ref[e] = picked if first else f_in[e] + picked
+
+        if not first:
+            p_ref[...] = p_in[...]
+        p_ref[plane] = jnp.sum(jnp.transpose(bsum[...]), axis=0, keepdims=True)
 
     if not first:
-        p_ref[...] = p_in[...]
-    row = jnp.where(valid, plane, planes)
-    p_ref[row] = jnp.sum(jnp.transpose(bsum[...]), axis=0, keepdims=True)
+
+        @pl.when(jnp.logical_not(valid))
+        def _():
+            p_ref[...] = p_in[...]
+            f_ref[...] = f_in[...]
 
 
 def dots_call(scalars, fidx, sources, chunks, state, planes, hop, way):
@@ -156,7 +163,7 @@
         ],
         out_shape=[
             jax.ShapeDtypeStruct((reps, rows, length), jnp.float32),
-            jax.ShapeDtypeStruct((planes + 1, 1, rows), jnp.float32),
+            jax.ShapeDtypeStruct((planes, 1, rows), jnp.float32),
             jax.ShapeDtypeStruct((reps, 1, length), jnp.float32),
         ],
         compiler_params=pltpu.CompilerParams(vmem_limit_bytes=DOTS_LIMIT),
@@ -174,7 +181,7 @@
     f_ref, e_ref, means, halves = refs
     reps, rows, lanes = s_refs[0].shape
     parts = rows // BLOCK
-    planes = means.shape[0] - 1
+    planes = means.shape[0]
     root = math.sqrt(D)
 
     @pl.when(pl.program_id(0) == 0)
@@ -358,7 +365,7 @@
         heads[hop] = moved(heads[hop - 1], hop)
         if hop < 3:
             tails[hop] = moved(tails[hop - 1], hop)
-    *_, fidx, held = together(*heads[1], *rest, fidx, source_vecs)
+    *_, fidx, held = together(*rest, fidx, source_vecs)
     sources = [held] + [shift(held, "width", width, d) for d in range(1, width)]
     got = together(*sources, *tails[1], *heads[2])
     sources = list(got[:width])

time: 125 us -> 119 us (0.952)
  Pallas kernels: 33.2 us -> 29.6 us
  waiting for transfers between devices: 44.4 us -> 42.1 us
    ppermute x12, waiting for transfers between devices: 36.4 us -> 29.3 us  [moved(): out += [lax.ppermute(c, 'shard', pairs) for c in side]]
    ppermute x8, waiting for transfers between devices: 8.07 us -> 12.9 us  [shift(): lax.ppermute(values, axis, [((i + by) % count, i) for i in range(count)])]
    pallas_call x5, Pallas kernels: 28 us -> 24.4 us  [dots_call(): pl.pallas_call(functools.partial(dots_kernel, reps, width, pairs, planes,...]
  transfers between devices with their start and end apart: 20 -> 20, of which waited for: 10 -> 8; matrix products, arithmetic and copies ran while one was open for 1% -> 1% of each run, Pallas kernels for 18% -> 16%
where the time goes in v4:
time: 119 us
  waiting for transfers between devices  42.1 us (35%)
  Pallas kernels  29.6 us (25%)
  starting transfers between devices  26.2 us (22%)
  local copies, waits for them, and re-layouts  10.9 us (9%)
  blocking collectives  6.51 us (5%)
  other arithmetic  2.32 us (2%)
    ppermute x12, waiting for transfers between devices, moved(): out += [lax.ppermute(c, 'shard', pairs) for c in side]  29.3 us
    pallas_call x5, Pallas kernels, dots_call(): pl.pallas_call(functools.partial(dots_kernel, reps, width, pairs, planes,...  24.4 us
    ppermute x12, starting transfers between devices, moved(): out += [lax.ppermute(c, 'shard', pairs) for c in side]  19 us
    ppermute x8, waiting for transfers between devices, shift(): lax.ppermute(values, axis, [((i + by) % count, i) for i in range(count)])  12.9 us
    unnamed x28, local copies, waits for them, and re-layouts  9.52 us
    ppermute x8, starting transfers between devices, shift(): lax.ppermute(values, axis, [((i + by) % count, i) for i in range(count)])  7.19 us
    all_gather x1, blocking collectives, on_device(): gathered = lax.all_gather(lines, ('width', 'rep'), axis=0, tiled=False)  6.51 us
    pallas_call x1, Pallas kernels, margin_call(): pl.pallas_call(functools.partial(margin_kernel, places, terms), grid=(len...  2.97 us
  transfers between devices with their start and end apart: 20, of which 8 were waited for; matrix products, arithmetic and copies ran while one was open for 1% of the time, Pallas kernels for 16%

profile of v4, /device:TPU:0, one launch (start us, length us, event | category | flops | bytes accessed | tf_op | source)
XLA Modules:
  0.0 118.6 jit_solution(10100739944332307324)
XLA Ops:
  1.5 1.3 %constant_dynamic-slice_fusion = (bf16[512,512]{1,0:T(8,128)(2,1)S(1)}, bf16[512,512]{1,0:T(8,128)(2,1)S(1)}) fusion(bf16[1024,512]{1,0:T(8,128)(2,1)} %param.8, s32[]{:T(128)S(6)} %select_n.19, s32[]{:T(128)S(6)} %select_n.17), kind=kLoop, calls=%fused_computation.21 | loop fusion | bytes 2097160 | tf_op jit(solution)/shard_map/dynamic_slice | solution.py:323
  2.9 3.0 %collective-permute-start = (bf16[528,512]{1,0:T(8,128)(2,1)S(1)}, bf16[528,512]{1,0:T(8,128)(2,1)S(1)}, u32[]{:S(2)}, u32[]{:S(2)}) collective-permute-start(bf16[528,512]{1,0:T(8,128)(2,1)S(1)} %pad_maximum_fusion), channel_id=1, source_target_pairs={{2,0},{0,2},{3,1},{1,3},{6,4},{4,6},{7,5},{5,7},{10,8},{8,10},{11,... | collective-permute-start | bytes 1622024 | tf_op jit(solution)/shard_map/ppermute | solution.py:326
  6.7 3.5 %collective-permute-start.5 = (bf16[512,512]{1,0:T(8,128)(2,1)S(1)}, bf16[512,512]{1,0:T(8,128)(2,1)S(1)}, u32[]{:S(2)}, u32[]{:S(2)}) collective-permute-start(bf16[512,512]{1,0:T(8,128)(2,1)S(1)} %get-tuple-element.57.refs_3_), channel_id=1, source_target_pairs={{0,4},{4,8},{8,12},{1,5},{5,9},{9,13},{2,6},{6,10},{10,14},{3,7},{... | collective-permute-start | bytes 1572872 | tf_op jit(solution)/shard_map/ppermute | solution.py:353
  10.3 1.3 %collective-permute-start.7 = (bf16[512,512]{1,0:T(8,128)(2,1)S(1)}, bf16[512,512]{1,0:T(8,128)(2,1)S(1)}, u32[]{:S(2)}, u32[]{:S(2)}) collective-permute-start(bf16[512,512]{1,0:T(8,128)(2,1)S(1)} %get-tuple-element.57.refs_3_), channel_id=1, source_target_pairs={{4,0},{8,4},{12,8},{5,1},{9,5},{13,9},{6,2},{10,6},{14,10},{7,3},{... | collective-permute-start | bytes 1572872 | tf_op jit(solution)/shard_map/ppermute | solution.py:353
  11.6 6.6 %collective-permute-done.refs_4_ = bf16[528,512]{1,0:T(8,128)(2,1)S(1)} collective-permute-done((bf16[528,512]{1,0:T(8,128)(2,1)S(1)}, bf16[528,512]{1,0:T(8,128)(2,1)S(1)}, u32[]{:S(2)}, u32[]{:S(2)}) %collective-permute-start) | collective-permute-done | bytes 540704 | tf_op jit(solution)/shard_map/ppermute | solution.py:326
  18.2 1.7 %collective-permute-start.2 = (bf16[1024,512]{1,0:T(8,128)(2,1)}, bf16[1024,512]{1,0:T(8,128)(2,1)S(1)}, u32[]{:S(2)}, u32[]{:S(2)}) collective-permute-start(bf16[1024,512]{1,0:T(8,128)(2,1)} %refs_0_), channel_id=1, source_target_pairs={{2,0},{0,2},{3,1},{1,3},{6,4},{4,6},{7,5},{5,7},{10,8},{8,10},{11,... | collective-permute-start | bytes 3145736 | tf_op jit(solution)/shard_map/ppermute | solution.py:326
  19.9 4.3 %collective-permute-start.3 = (bf16[528,512]{1,0:T(8,128)(2,1)S(1)}, bf16[528,512]{1,0:T(8,128)(2,1)}, u32[]{:S(2)}, u32[]{:S(2)}) collective-permute-start(bf16[528,512]{1,0:T(8,128)(2,1)S(1)} %collective-permute-done.refs_4_), channel_id=1, source_target_pairs={{0,4},{4,8},{8,12},{1,5},{5,9},{9,13},{2,6},{6,10},{10,14},{3,7},{... | collective-permute-start | bytes 1622024 | tf_op jit(solution)/shard_map/ppermute | solution.py:353
  24.2 1.3 %collective-permute-start.4 = (bf16[528,512]{1,0:T(8,128)(2,1)S(1)}, bf16[528,512]{1,0:T(8,128)(2,1)S(1)}, u32[]{:S(2)}, u32[]{:S(2)}) collective-permute-start(bf16[528,512]{1,0:T(8,128)(2,1)S(1)} %collective-permute-done.refs_4_), channel_id=1, source_target_pairs={{4,0},{8,4},{12,8},{5,1},{9,5},{13,9},{6,2},{10,6},{14,10},{7,3},{... | collective-permute-start | bytes 1622024 | tf_op jit(solution)/shard_map/ppermute | solution.py:353
  27.8 1.3 %collective-permute-start.8 = (bf16[512,512]{1,0:T(8,128)(2,1)S(1)}, bf16[512,512]{1,0:T(8,128)(2,1)S(1)}, u32[]{:S(2)}, u32[]{:S(2)}) collective-permute-start(bf16[512,512]{1,0:T(8,128)(2,1)S(1)} %collective-permute-done.7.refs_3_), channel_id=1, source_target_pairs={{4,0},{8,4},{5,1},{9,5},{6,2},{10,6},{7,3},{11,7},{20,16},{24,20},... | collective-permute-start | bytes 1572872 | tf_op jit(solution)/shard_map/ppermute | solution.py:353
  29.9 20.0 %collective-permute-done.8.refs_5_ = bf16[512,512]{1,0:T(8,128)(2,1)S(1)} collective-permute-done((bf16[512,512]{1,0:T(8,128)(2,1)S(1)}, bf16[512,512]{1,0:T(8,128)(2,1)S(1)}, u32[]{:S(2)}, u32[]{:S(2)}) %collective-permute-start.8) | collective-permute-done | bytes 524320 | tf_op jit(solution)/shard_map/ppermute | solution.py:353
  50.7 1.2 %copy-done.3 = bf16[1024,512]{1,0:T(8,128)(2,1)S(1)} copy-done((bf16[1024,512]{1,0:T(8,128)(2,1)S(1)}, bf16[1024,512]{1,0:T(8,128)(2,1)}, u32[]{:S(2)}) %copy-start.3) | copy-done | bytes 1048600
  52.9 1.5 %collective-permute-start.10 = (bf16[528,512]{1,0:T(8,128)(2,1)}, bf16[528,512]{1,0:T(8,128)(2,1)}, u32[]{:S(2)}, u32[]{:S(2)}) collective-permute-start(bf16[528,512]{1,0:T(8,128)(2,1)} %collective-permute-done.3.refs_4_), channel_id=1, source_target_pairs={{4,8},{8,12},{5,9},{9,13},{6,10},{10,14},{7,11},{11,15},{20,24},{2... | collective-permute-start | bytes 1622024 | tf_op jit(solution)/shard_map/ppermute | solution.py:353
  54.4 1.3 %collective-permute-start.11 = (bf16[528,512]{1,0:T(8,128)(2,1)S(1)}, bf16[528,512]{1,0:T(8,128)(2,1)}, u32[]{:S(2)}, u32[]{:S(2)}) collective-permute-start(bf16[528,512]{1,0:T(8,128)(2,1)S(1)} %collective-permute-done.4.refs_4_), channel_id=1, source_target_pairs={{4,0},{8,4},{5,1},{9,5},{6,2},{10,6},{7,3},{11,7},{20,16},{24,20},... | collective-permute-start | bytes 1622024 | tf_op jit(solution)/shard_map/ppermute | solution.py:353
  55.7 1.4 %collective-permute-done.9.refs_2_ = bf16[1024,1024]{1,0:T(8,128)(2,1)} collective-permute-done((bf16[1024,1024]{1,0:T(8,128)(2,1)S(1)}, bf16[1024,1024]{1,0:T(8,128)(2,1)}, u32[]{:S(2)}, u32[]{:S(2)}) %collective-permute-start.9) | collective-permute-done | bytes 2097184 | tf_op jit(solution)/shard_map/ppermute | solution.py:326
  57.2 1.0 copy-done.5
  58.2 5.5 %shard_map.95 = (f32[2,512,1024]{2,1,0:T(8,128)S(1)}, f32[4,1,512]{2,1,0:T(1,128)S(1)}, f32[2,1,1024]{2,1,0:T(1,128)S(1)}) custom-call(s32[3]{0:T(128)S(1)} %pad_add_fusion.2.sc_ref, s32[2,4,1024]{2,1,0:T(4,128)S(1)} %pad_add_fusion.refs_0_, bf16[1024,1024]{1,0:T(8,128)(2,1)S(1)} %shard_map.94.refs_1_, bf16[1024,1024]{1,0:T(8,128)(2,1)} %collective-permute-done.9.refs_2_, ...), custom_call_target="tpu_custom_call" | custom-call | flops 2147483648 | bytes 4194304 | tf_op jit(solution)/shard_map/pallas_call | solution.py:155
  63.7 2.0 %copy-done.1 = f32[2,512,1024]{2,1,0:T(8,128)} copy-done((f32[2,512,1024]{2,1,0:T(8,128)}, f32[2,512,1024]{2,1,0:T(8,128)S(1)}, u32[]{:S(2)}) %copy-start.1) | copy-done | bytes 4194328
  66.5 1.3 %collective-permute-start.15 = (bf16[512,512]{1,0:T(8,128)(2,1)}, bf16[512,512]{1,0:T(8,128)(2,1)S(1)}, u32[]{:S(2)}, u32[]{:S(2)}) collective-permute-start(bf16[512,512]{1,0:T(8,128)(2,1)} %copy-done.12), channel_id=1, source_target_pairs={{4,0},{5,1},{6,2},{7,3},{20,16},{21,17},{22,18},{23,19}} | collective-permute-start | bytes 1572872 | tf_op jit(solution)/shard_map/ppermute | solution.py:353
  67.8 3.2 %collective-permute-done.11.refs_6_ = bf16[528,512]{1,0:T(8,128)(2,1)} collective-permute-done((bf16[528,512]{1,0:T(8,128)(2,1)S(1)}, bf16[528,512]{1,0:T(8,128)(2,1)}, u32[]{:S(2)}, u32[]{:S(2)}) %collective-permute-start.11) | collective-permute-done | bytes 540704 | tf_op jit(solution)/shard_map/ppermute | solution.py:353
  71.7 1.3 %collective-permute-start.16 = (bf16[528,512]{1,0:T(8,128)(2,1)}, bf16[528,512]{1,0:T(8,128)(2,1)S(1)}, u32[]{:S(2)}, u32[]{:S(2)}) collective-permute-start(bf16[528,512]{1,0:T(8,128)(2,1)} %collective-permute-done.11.refs_6_), channel_id=1, source_target_pairs={{4,0},{5,1},{6,2},{7,3},{20,16},{21,17},{22,18},{23,19}} | collective-permute-start | bytes 1622024 | tf_op jit(solution)/shard_map/ppermute | solution.py:353
  73.0 1.0 copy-done.9
  74.1 1.8 %shard_map.96 = (f32[2,512,1024]{2,1,0:T(8,128)S(1)}, f32[4,1,512]{2,1,0:T(1,128)S(1)}, f32[2,1,1024]{2,1,0:T(1,128)S(1)}) custom-call(s32[3]{0:T(128)S(1)} %pad_add_fusion.2.sc_ref, s32[2,4,1024]{2,1,0:T(4,128)S(1)} %pad_add_fusion.1.refs_0_, bf16[1024,1024]{1,0:T(8,128)(2,1)S(1)} %shard_map.94.refs_1_, bf16[1024,1024]{1,0:T(8,128)(2,1)} %collective-permute-done.9.refs_2_, ...), custom_call_target="tpu_custom_call" | custom-call | flops 2147483648 | bytes 4194304 | tf_op jit(solution)/shard_map/pallas_call | solution.py:155
  76.9 5.5 %shard_map.97 = (f32[2,512,1024]{2,1,0:T(8,128)S(1)}, f32[4,1,512]{2,1,0:T(1,128)S(1)}, f32[2,1,1024]{2,1,0:T(1,128)S(1)}) custom-call(s32[3]{0:T(128)S(1)} %pad_add_fusion.2.sc_ref, s32[2,4,1024]{2,1,0:T(4,128)S(1)} %pad_add_fusion.1.refs_0_, bf16[1024,1024]{1,0:T(8,128)(2,1)S(1)} %shard_map.94.refs_1_, bf16[1024,1024]{1,0:T(8,128)(2,1)} %collective-permute-done.9.refs_2_, ...), custom_call_target="tpu_custom_call" | custom-call | flops 2147483648 | bytes 4194304 | tf_op jit(solution)/shard_map/pallas_call | solution.py:155
  82.4 5.9 %shard_map.98 = (f32[2,512,1024]{2,1,0:T(8,128)S(1)}, f32[4,1,512]{2,1,0:T(1,128)S(1)}, f32[2,1,1024]{2,1,0:T(1,128)S(1)}) custom-call(s32[3]{0:T(128)S(1)} %pad_add_fusion.2.sc_ref, s32[2,4,1024]{2,1,0:T(4,128)S(1)} %pad_add_fusion.1.refs_0_, bf16[1024,1024]{1,0:T(8,128)(2,1)S(1)} %shard_map.94.refs_1_, bf16[1024,1024]{1,0:T(8,128)(2,1)} %collective-permute-done.9.refs_2_, ...), custom_call_target="tpu_custom_call" | custom-call | flops 2147483648 | bytes 4194304 | tf_op jit(solution)/shard_map/pallas_call | solution.py:155
  88.3 6.1 %collective-permute-done.16.refs_6_ = bf16[528,512]{1,0:T(8,128)(2,1)S(1)} collective-permute-done((bf16[528,512]{1,0:T(8,128)(2,1)}, bf16[528,512]{1,0:T(8,128)(2,1)S(1)}, u32[]{:S(2)}, u32[]{:S(2)}) %collective-permute-start.16) | collective-permute-done | bytes 540704 | tf_op jit(solution)/shard_map/ppermute | solution.py:353
  94.4 5.8 %shard_map.99 = (f32[2,512,1024]{2,1,0:T(8,128)S(1)}, f32[4,1,512]{2,1,0:T(1,128)S(1)}, f32[2,1,1024]{2,1,0:T(1,128)S(1)}) custom-call(s32[3]{0:T(128)S(1)} %pad_add_fusion.2.sc_ref, s32[2,4,1024]{2,1,0:T(4,128)S(1)} %pad_add_fusion.1.refs_0_, bf16[1024,1024]{1,0:T(8,128)(2,1)S(1)} %shard_map.94.refs_1_, bf16[1024,1024]{1,0:T(8,128)(2,1)} %collective-permute-done.9.refs_2_, ...), custom_call_target="tpu_custom_call" | custom-call | flops 2147483648 | bytes 4194304 | tf_op jit(solution)/shard_map/pallas_call | solution.py:155
  100.2 1.5 %collective-permute-start.17 = (f32[4,1,512]{2,1,0:T(1,128)S(1)}, f32[4,1,512]{2,1,0:T(1,128)S(1)}, u32[]{:S(2)}, u32[]{:S(2)}) collective-permute-start(f32[4,1,512]{2,1,0:T(1,128)S(1)} %get-tuple-element.52.refs_5_), channel_id=1, source_target_pairs={{4,0},{8,4},{12,8},{0,12},{5,1},{9,5},{13,9},{1,13},{6,2},{10,6},{... | collective-permute-start | bytes 24584 | tf_op jit(solution)/shard_map/ppermute | solution.py:326
  102.4 1.5 %collective-permute-done.17.refs_6_ = f32[4,1,512]{2,1,0:T(1,128)S(1)} collective-permute-done((f32[4,1,512]{2,1,0:T(1,128)S(1)}, f32[4,1,512]{2,1,0:T(1,128)S(1)}, u32[]{:S(2)}, u32[]{:S(2)}) %collective-permute-start.17) | collective-permute-done | bytes 8224 | tf_op jit(solution)/shard_map/ppermute | solution.py:326
  103.9 2.4 %collective-permute-done.18.refs_7_ = f32[4,1,512]{2,1,0:T(1,128)S(1)} collective-permute-done((f32[4,1,512]{2,1,0:T(1,128)S(1)}, f32[4,1,512]{2,1,0:T(1,128)S(1)}, u32[]{:S(2)}, u32[]{:S(2)}) %collective-permute-start.18) | collective-permute-done | bytes 8224 | tf_op jit(solution)/shard_map/ppermute | solution.py:326
  107.2 3.0 %shard_map.100 = f32[2,16,1024]{2,1,0:T(8,128)S(1)} custom-call(s32[3]{0:T(128)S(1)} %pad_add_fusion.2.sc_ref, f32[2,512,1024]{2,1,0:T(8,128)S(1)} %copy-done.2, f32[2,512,1024]{2,1,0:T(8,128)S(1)} %get-tuple-element.40.refs_1_, f32[2,512,1024]{2,1,0:T(8,128)S(1)} %get-tuple-element.43.refs_2_, f32[2,512,1024]{2,1,0:T(8,128)S(1)} %get-tuple-element.48.refs_3_, ...), custom_call_target="tpu_custom_call" | custom-call | flops 524288 | bytes 524288 | tf_op jit(solution)/shard_map/pallas_call | solution.py:231
  110.2 6.5 %all-gather = f32[8,16,1024]{2,1,0:T(8,128)S(1)} all-gather(f32[2,16,1024]{2,1,0:T(8,128)S(1)} %shard_map.100), channel_id=2, replica_groups=mesh['groups'=2,'shard'=4,'width'=2,'rep'=2] {'width','rep'}, dimensions={0}, use_global_device_ids=true | all-gather | bytes 655360 | tf_op jit(solution)/shard_map/all_gather | solution.py:405
  116.7 1.3 %shard_map.101 = (f32[8,1024]{1,0:T(8,128)}, f32[1,1024]{1,0:T(1,128)}, bf16[1,1024]{1,0:T(2,128)(2,1)S(1)}) custom-call(s32[3]{0:T(128)S(1)} %pad_add_fusion.2.sc_ref, s32[16]{0:T(128)S(1)} %fusion.8.list_ref, f32[4,2,16,1024]{3,2,1,0:T(8,128)S(1)} %bitcast.38), custom_call_target="tpu_custom_call" | custom-call | tf_op jit(solution)/shard_map/pallas_call | solution.py:284
  (57 shorter events, 11.3 us)
Async XLA Ops:
  0.6 101.7 %copy-start = (s32[4,16]{1,0:T(4,128)S(1)}, s32[4,16]{1,0:T(4,128)}, u32[]{:S(2)}) copy-start(s32[4,16]{1,0:T(4,128)} %param.13) | copy-start | bytes 772
  2.9 15.3 %collective-permute-start = (bf16[528,512]{1,0:T(8,128)(2,1)S(1)}, bf16[528,512]{1,0:T(8,128)(2,1)S(1)}, u32[]{:S(2)}, u32[]{:S(2)}) collective-permute-start(bf16[528,512]{1,0:T(8,128)(2,1)S(1)} %pad_maximum_fusion), channel_id=1, source_target_pairs={{2,0},{0,2},{3,1},{1,3},{6,4},{4,6},{7,5},{5,7},{10,8},{8,10},{11,... | collective-permute-start | bytes 1622024 | tf_op jit(solution)/shard_map/ppermute | solution.py:326
  6.7 4.9 %collective-permute-start.1 = (s32[4,1024]{1,0:T(4,128)S(1)}, s32[4,1024]{1,0:T(4,128)S(1)}, u32[]{:S(2)}, u32[]{:S(2)}) collective-permute-start(s32[4,1024]{1,0:T(4,128)S(1)} %get-tuple-element.36), channel_id=1, source_target_pairs={{1,0},{0,1},{3,2},{2,3},{5,4},{4,5},{7,6},{6,7},{9,8},{8,9},{11,10... | collective-permute-start | bytes 49160 | tf_op jit(solution)/shard_map/ppermute | solution.py:326
  6.7 19.6 %collective-permute-start.5 = (bf16[512,512]{1,0:T(8,128)(2,1)S(1)}, bf16[512,512]{1,0:T(8,128)(2,1)S(1)}, u32[]{:S(2)}, u32[]{:S(2)}) collective-permute-start(bf16[512,512]{1,0:T(8,128)(2,1)S(1)} %get-tuple-element.57.refs_3_), channel_id=1, source_target_pairs={{0,4},{4,8},{8,12},{1,5},{5,9},{9,13},{2,6},{6,10},{10,14},{3,7},{... | collective-permute-start | bytes 1572872 | tf_op jit(solution)/shard_map/ppermute | solution.py:353
  10.3 17.5 %collective-permute-start.7 = (bf16[512,512]{1,0:T(8,128)(2,1)S(1)}, bf16[512,512]{1,0:T(8,128)(2,1)S(1)}, u32[]{:S(2)}, u32[]{:S(2)}) collective-permute-start(bf16[512,512]{1,0:T(8,128)(2,1)S(1)} %get-tuple-element.57.refs_3_), channel_id=1, source_target_pairs={{4,0},{8,4},{12,8},{5,1},{9,5},{13,9},{6,2},{10,6},{14,10},{7,3},{... | collective-permute-start | bytes 1572872 | tf_op jit(solution)/shard_map/ppermute | solution.py:353
  18.2 32.5 %collective-permute-start.2 = (bf16[1024,512]{1,0:T(8,128)(2,1)}, bf16[1024,512]{1,0:T(8,128)(2,1)S(1)}, u32[]{:S(2)}, u32[]{:S(2)}) collective-permute-start(bf16[1024,512]{1,0:T(8,128)(2,1)} %refs_0_), channel_id=1, source_target_pairs={{2,0},{0,2},{3,1},{1,3},{6,4},{4,6},{7,5},{5,7},{10,8},{8,10},{11,... | collective-permute-start | bytes 3145736 | tf_op jit(solution)/shard_map/ppermute | solution.py:326
  19.9 30.0 %collective-permute-start.3 = (bf16[528,512]{1,0:T(8,128)(2,1)S(1)}, bf16[528,512]{1,0:T(8,128)(2,1)}, u32[]{:S(2)}, u32[]{:S(2)}) collective-permute-start(bf16[528,512]{1,0:T(8,128)(2,1)S(1)} %collective-permute-done.refs_4_), channel_id=1, source_target_pairs={{0,4},{4,8},{8,12},{1,5},{5,9},{9,13},{2,6},{6,10},{10,14},{3,7},{... | collective-permute-start | bytes 1622024 | tf_op jit(solution)/shard_map/ppermute | solution.py:353
  24.2 25.7 %collective-permute-start.4 = (bf16[528,512]{1,0:T(8,128)(2,1)S(1)}, bf16[528,512]{1,0:T(8,128)(2,1)S(1)}, u32[]{:S(2)}, u32[]{:S(2)}) collective-permute-start(bf16[528,512]{1,0:T(8,128)(2,1)S(1)} %collective-permute-done.refs_4_), channel_id=1, source_target_pairs={{4,0},{8,4},{12,8},{5,1},{9,5},{13,9},{6,2},{10,6},{14,10},{7,3},{... | collective-permute-start | bytes 1622024 | tf_op jit(solution)/shard_map/ppermute | solution.py:353
  26.3 3.6 %collective-permute-start.6 = (bf16[512,512]{1,0:T(8,128)(2,1)S(1)}, bf16[512,512]{1,0:T(8,128)(2,1)S(1)}, u32[]{:S(2)}, u32[]{:S(2)}) collective-permute-start(bf16[512,512]{1,0:T(8,128)(2,1)S(1)} %collective-permute-done.5.refs_3_), channel_id=1, source_target_pairs={{4,8},{8,12},{5,9},{9,13},{6,10},{10,14},{7,11},{11,15},{20,24},{2... | collective-permute-start | bytes 1572872 | tf_op jit(solution)/shard_map/ppermute | solution.py:353
  27.8 22.1 %collective-permute-start.8 = (bf16[512,512]{1,0:T(8,128)(2,1)S(1)}, bf16[512,512]{1,0:T(8,128)(2,1)S(1)}, u32[]{:S(2)}, u32[]{:S(2)}) collective-permute-start(bf16[512,512]{1,0:T(8,128)(2,1)S(1)} %collective-permute-done.7.refs_3_), channel_id=1, source_target_pairs={{4,0},{8,4},{5,1},{9,5},{6,2},{10,6},{7,3},{11,7},{20,16},{24,20},... | collective-permute-start | bytes 1572872 | tf_op jit(solution)/shard_map/ppermute | solution.py:353
  29.1 0.8 copy-start.6
  29.9 20.0 %copy-start.10 = (bf16[512,512]{1,0:T(8,128)(2,1)}, bf16[512,512]{1,0:T(8,128)(2,1)S(1)}, u32[]{:S(2)}) copy-start(bf16[512,512]{1,0:T(8,128)(2,1)S(1)} %collective-permute-done.6.refs_3_) | copy-start | bytes 1572868
  49.9 0.8 copy-start.12
  50.7 1.2 %copy-start.3 = (bf16[1024,512]{1,0:T(8,128)(2,1)S(1)}, bf16[1024,512]{1,0:T(8,128)(2,1)}, u32[]{:S(2)}) copy-start(bf16[1024,512]{1,0:T(8,128)(2,1)} %refs_0_) | copy-start | bytes 3145732
  52.8 4.4 %collective-permute-start.9 = (bf16[1024,1024]{1,0:T(8,128)(2,1)S(1)}, bf16[1024,1024]{1,0:T(8,128)(2,1)}, u32[]{:S(2)}, u32[]{:S(2)}) collective-permute-start(bf16[1024,1024]{1,0:T(8,128)(2,1)S(1)} %shard_map.94.refs_1_), channel_id=1, source_target_pairs={{1,0},{0,1},{3,2},{2,3},{5,4},{4,5},{7,6},{6,7},{9,8},{8,9},{11,10... | collective-permute-start | bytes 6291464 | tf_op jit(solution)/shard_map/ppermute | solution.py:326
  52.9 14.9 %collective-permute-start.10 = (bf16[528,512]{1,0:T(8,128)(2,1)}, bf16[528,512]{1,0:T(8,128)(2,1)}, u32[]{:S(2)}, u32[]{:S(2)}) collective-permute-start(bf16[528,512]{1,0:T(8,128)(2,1)} %collective-permute-done.3.refs_4_), channel_id=1, source_target_pairs={{4,8},{8,12},{5,9},{9,13},{6,10},{10,14},{7,11},{11,15},{20,24},{2... | collective-permute-start | bytes 1622024 | tf_op jit(solution)/shard_map/ppermute | solution.py:353
  54.4 16.7 %collective-permute-start.11 = (bf16[528,512]{1,0:T(8,128)(2,1)S(1)}, bf16[528,512]{1,0:T(8,128)(2,1)}, u32[]{:S(2)}, u32[]{:S(2)}) collective-permute-start(bf16[528,512]{1,0:T(8,128)(2,1)S(1)} %collective-permute-done.4.refs_4_), channel_id=1, source_target_pairs={{4,0},{8,4},{5,1},{9,5},{6,2},{10,6},{7,3},{11,7},{20,16},{24,20},... | collective-permute-start | bytes 1622024 | tf_op jit(solution)/shard_map/ppermute | solution.py:353
  57.2 1.0 copy-start.5
  63.7 2.0 %copy-start.1 = (f32[2,512,1024]{2,1,0:T(8,128)}, f32[2,512,1024]{2,1,0:T(8,128)S(1)}, u32[]{:S(2)}) copy-start(f32[2,512,1024]{2,1,0:T(8,128)S(1)} %get-tuple-element.34.refs_0_) | copy-start | bytes 12582916
  65.7 2.1 %collective-permute-start.12 = (s32[4,1024]{1,0:T(4,128)S(1)}, s32[4,1024]{1,0:T(4,128)S(1)}, u32[]{:S(2)}, u32[]{:S(2)}) collective-permute-start(s32[4,1024]{1,0:T(4,128)S(1)} %get-tuple-element.36), channel_id=1, source_target_pairs={{1,0},{0,1},{3,2},{2,3},{5,4},{4,5},{7,6},{6,7},{9,8},{8,9},{11,10... | collective-permute-start | bytes 49160 | tf_op jit(solution)/shard_map/ppermute | solution.py:326
  65.8 22.5 %collective-permute-start.13 = (bf16[512,512]{1,0:T(8,128)(2,1)}, bf16[512,512]{1,0:T(8,128)(2,1)S(1)}, u32[]{:S(2)}, u32[]{:S(2)}) collective-permute-start(bf16[512,512]{1,0:T(8,128)(2,1)} %copy-done.10), channel_id=1, source_target_pairs={{8,12},{9,13},{10,14},{11,15},{24,28},{25,29},{26,30},{27,31}} | collective-permute-start | bytes 1572872 | tf_op jit(solution)/shard_map/ppermute | solution.py:353
  66.5 21.8 %collective-permute-start.15 = (bf16[512,512]{1,0:T(8,128)(2,1)}, bf16[512,512]{1,0:T(8,128)(2,1)S(1)}, u32[]{:S(2)}, u32[]{:S(2)}) collective-permute-start(bf16[512,512]{1,0:T(8,128)(2,1)} %copy-done.12), channel_id=1, source_target_pairs={{4,0},{5,1},{6,2},{7,3},{20,16},{21,17},{22,18},{23,19}} | collective-permute-start | bytes 1572872 | tf_op jit(solution)/shard_map/ppermute | solution.py:353
  71.0 17.3 %collective-permute-start.14 = (bf16[528,512]{1,0:T(8,128)(2,1)}, bf16[528,512]{1,0:T(8,128)(2,1)S(1)}, u32[]{:S(2)}, u32[]{:S(2)}) collective-permute-start(bf16[528,512]{1,0:T(8,128)(2,1)} %collective-permute-done.10.refs_4_), channel_id=1, source_target_pairs={{8,12},{9,13},{10,14},{11,15},{24,28},{25,29},{26,30},{27,31}} | collective-permute-start | bytes 1622024 | tf_op jit(solution)/shard_map/ppermute | solution.py:353
  71.7 22.7 %collective-permute-start.16 = (bf16[528,512]{1,0:T(8,128)(2,1)}, bf16[528,512]{1,0:T(8,128)(2,1)S(1)}, u32[]{:S(2)}, u32[]{:S(2)}) collective-permute-start(bf16[528,512]{1,0:T(8,128)(2,1)} %collective-permute-done.11.refs_6_), channel_id=1, source_target_pairs={{4,0},{5,1},{6,2},{7,3},{20,16},{21,17},{22,18},{23,19}} | collective-permute-start | bytes 1622024 | tf_op jit(solution)/shard_map/ppermute | solution.py:353
  73.0 1.0 copy-start.9
  74.1 8.3 %copy-start.11 = (bf16[512,512]{1,0:T(8,128)(2,1)S(1)}, bf16[512,512]{1,0:T(8,128)(2,1)}, u32[]{:S(2)}) copy-start(bf16[512,512]{1,0:T(8,128)(2,1)} %copy-done.10) | copy-start | bytes 1572868
  74.1 8.3 %copy-start.13 = (bf16[512,512]{1,0:T(8,128)(2,1)S(1)}, bf16[512,512]{1,0:T(8,128)(2,1)}, u32[]{:S(2)}) copy-start(bf16[512,512]{1,0:T(8,128)(2,1)} %copy-done.12) | copy-start | bytes 1572868
  75.9 1.0 copy-start.7
  88.3 18.9 %copy-start.2 = (f32[2,512,1024]{2,1,0:T(8,128)S(1)}, f32[2,512,1024]{2,1,0:T(8,128)}, u32[]{:S(2)}) copy-start(f32[2,512,1024]{2,1,0:T(8,128)} %copy-done.1) | copy-start | bytes 12582916
  100.2 3.7 %collective-permute-start.17 = (f32[4,1,512]{2,1,0:T(1,128)S(1)}, f32[4,1,512]{2,1,0:T(1,128)S(1)}, u32[]{:S(2)}, u32[]{:S(2)}) collective-permute-start(f32[4,1,512]{2,1,0:T(1,128)S(1)} %get-tuple-element.52.refs_5_), channel_id=1, source_target_pairs={{4,0},{8,4},{12,8},{0,12},{5,1},{9,5},{13,9},{1,13},{6,2},{10,6},{... | collective-permute-start | bytes 24584 | tf_op jit(solution)/shard_map/ppermute | solution.py:326
  101.7 4.6 %collective-permute-start.18 = (f32[4,1,512]{2,1,0:T(1,128)S(1)}, f32[4,1,512]{2,1,0:T(1,128)S(1)}, u32[]{:S(2)}, u32[]{:S(2)}) collective-permute-start(f32[4,1,512]{2,1,0:T(1,128)S(1)} %get-tuple-element.52.refs_5_), channel_id=1, source_target_pairs={{8,0},{12,4},{0,8},{4,12},{9,1},{13,5},{1,9},{5,13},{10,2},{14,6},... | collective-permute-start | bytes 24584 | tf_op jit(solution)/shard_map/ppermute | solution.py:326
  101.7 5.4 %collective-permute-start.19 = (f32[4,1,512]{2,1,0:T(1,128)S(1)}, f32[4,1,512]{2,1,0:T(1,128)S(1)}, u32[]{:S(2)}, u32[]{:S(2)}) collective-permute-start(f32[4,1,512]{2,1,0:T(1,128)S(1)} %get-tuple-element.52.refs_5_), channel_id=1, source_target_pairs={{12,0},{0,4},{4,8},{8,12},{13,1},{1,5},{5,9},{9,13},{14,2},{2,6},{... | collective-permute-start | bytes 24584 | tf_op jit(solution)/shard_map/ppermute | solution.py:326
  (2 other events, 1.6 us)

commit v5 on v4

--- a/solution.py
+++ b/solution.py
@@ -59,15 +59,10 @@
     return plane, (plane >= 0) & (plane < planes)
 
 
-def dots_kernel(reps, width, pairs, planes, hop, way, sc_ref, *refs):
+def dots_of(sc_ref, fidx_ref, src_refs, chunk_refs, width, planes, hop, way, outs):
+    s_ref, p_ref, f_ref, tgt, picks, bsum = outs
     first = hop == 0
-    fidx_ref, src_refs = refs[0], refs[1 : 1 + reps]
-    chunk_refs = refs[1 + reps : 1 + reps + width * pairs]
-    refs = refs[1 + reps + width * pairs :]
-    p_in, f_in = None, None
-    if not first:
-        p_in, f_in, refs = refs[0], refs[1], refs[2:]
-    s_ref, p_ref, f_ref, tgt, picks, bsum = refs
+    reps, pairs = len(src_refs), len(chunk_refs) // width
     rows, cols = chunk_refs[0].shape
     length = src_refs[0].shape[0]
     groups = length // LANES
@@ -129,56 +124,70 @@
                 0, rows // 8, one_line, jnp.zeros((8, length), jnp.float32), unroll=4
             )
             picked = jnp.sum(total, axis=0, keepdims=True)
-            f_ref[e] = picked if first else f_in[e] + picked
-
-        if not first:
-            p_ref[...] = p_in[...]
+            f_ref[e] = picked if first else f_ref[e] + picked
+
         p_ref[plane] = jnp.sum(jnp.transpose(bsum[...]), axis=0, keepdims=True)
 
+
+def dots_kernel(reps, width, planes, entries, sc_ref, *refs):
+    fidx_ref, src_refs, refs = refs[0], refs[1 : 1 + reps], refs[1 + reps :]
+    chunk_refs = []
+    for _, _, pairs in entries:
+        chunk_refs.append(refs[: width * pairs])
+        refs = refs[width * pairs :]
+    first = entries[0][0] == 0
     if not first:
-
-        @pl.when(jnp.logical_not(valid))
-        def _():
-            p_ref[...] = p_in[...]
-            f_ref[...] = f_in[...]
-
-
-def dots_call(scalars, fidx, sources, chunks, state, planes, hop, way):
+        p_in, f_in, refs = refs[0], refs[1], refs[2:]
+    s_refs, (p_ref, f_ref, *scratch) = refs[: len(entries)], refs[len(entries) :]
+    if not first:
+        p_ref[...] = p_in[...]
+        f_ref[...] = f_in[...]
+    for (hop, way, _), chunks, s_ref in zip(entries, chunk_refs, s_refs):
+        outs = (s_ref, p_ref, f_ref, *scratch)
+        dots_of(sc_ref, fidx_ref, src_refs, chunks, width, planes, hop, way, outs)
+
+
+def dots_call(scalars, fidx, sources, parts, state, planes):
     reps = len(sources)
-    pairs, width = len(chunks), len(chunks[0])
     length = sources[0].shape[0]
-    rows = chunks[0][0].shape[0]
-    flat = [c for pair in chunks for c in pair]
+    width = len(parts[0][2][0])
+    rows = length // width
+    flat = [c for _, _, chunks in parts for pair in chunks for c in pair]
+    entries = [(hop, way, len(chunks)) for hop, way, chunks in parts]
     state = [] if state is None else state
     operands = [fidx, *sources, *flat, *state]
     vmem = pl.BlockSpec(memory_space=pltpu.VMEM)
-    return pl.pallas_call(
-        functools.partial(dots_kernel, reps, width, pairs, planes, hop, way),
+    count = len(parts)
+    heavy = 0 if parts[0][0] == 0 else count
+    *dots, p, f = pl.pallas_call(
+        functools.partial(dots_kernel, reps, width, planes, entries),
         in_specs=[pl.BlockSpec(memory_space=pltpu.SMEM)] + [vmem] * len(operands),
-        out_specs=[vmem] * 3,
+        out_specs=[vmem] * (count + 2),
         scratch_shapes=[
             pltpu.VMEM((rows, D), jnp.bfloat16),
             pltpu.VMEM((rows, LANES), jnp.int32),
             pltpu.VMEM((rows, LANES), jnp.float32),
         ],
-        out_shape=[
-            jax.ShapeDtypeStruct((reps, rows, length), jnp.float32),
+        out_shape=[jax.ShapeDtypeStruct((reps, rows, length), jnp.float32)] * count
+        + [
             jax.ShapeDtypeStruct((planes, 1, rows), jnp.float32),
             jax.ShapeDtypeStruct((reps, 1, length), jnp.float32),
         ],
         compiler_params=pltpu.CompilerParams(vmem_limit_bytes=DOTS_LIMIT),
         cost_estimate=pl.CostEstimate(
-            flops=2 * reps * length * rows * D,
-            bytes_accessed=4 * reps * length * rows,
+            flops=(1 + 2 * reps * length * heavy) * rows * D,
+            bytes_accessed=(D + 4 * reps * length * heavy) * rows,
             transcendentals=rows,
         ),
     )(scalars, *operands)
-
-
-def margin_kernel(places, terms, sc_ref, *refs):
+    return dots, [p, f]
+
+
+def margin_kernel(places, terms, width, sc_ref, list_ref, *refs):
     slots = len(places)
     s_refs, p_refs, refs = refs[:slots], refs[slots : slots + terms], refs[slots + terms :]
-    f_ref, e_ref, means, halves = refs
+    count = width * refs[0].shape[0]
+    f_ref, outs, (e_ref, means, halves, peers, rows_of) = refs[0], refs[1 : 1 + count], refs[1 + count :]
     reps, rows, lanes = s_refs[0].shape
     parts = rows // BLOCK
     planes = means.shape[0]
@@ -195,6 +204,19 @@
             row = means[pl.ds(jnp.clip(plane, 0, planes - 1), 1), :]
             halves[t] = (0.5 * root) * jnp.transpose(jnp.broadcast_to(row, (LANES, rows)))
 
+    shard, wide, rep = sc_ref[0], sc_ref[1], sc_ref[2]
+    both = (planes - 1) // 2
+    for c in range(CAND):
+        block = list_ref[c]
+        holder = block // (parts * width)
+        local = block - holder * (parts * width)
+        plane = holder // reps
+        hops = jnp.abs(shard - plane)
+        near = 2 * hops - 1 + jnp.where(plane > shard, 1, 0)
+        slot = jnp.where(hops == 0, 0, jnp.where(hops <= both, near, both + hops))
+        peers[c] = (local // parts) * reps + holder - plane * reps
+        rows_of[c] = slot * parts + local - (local // parts) * parts
+
     for e in range(reps):
         at = lax.rem(sc_ref[2] + e, reps)
         for t in range(slots):
@@ -215,93 +237,92 @@
         for start in range(0, lanes, rows):
             e_ref[at, line + 1 : line + 2, start : start + min(rows, lanes)] = mean[:, :lanes]
 
-
-def margin_call(scalars, dots, bwd_terms, fwd_parts, places, whole):
+    own = wide * reps + rep
+    each = CAND // width
+    line = slots * parts
+    for d, out_ref in enumerate(outs):
+        dest = lax.rem(own + count - d, count)
+        dest_wide = dest // reps
+        dest_rep = dest - dest_wide * reps
+        for c in range(each):
+            at = dest_wide * each + c
+            row = e_ref[dest_rep, pl.ds(rows_of[at], 1), :]
+            out_ref[c : c + 1, :] = jnp.where(peers[at] == own, row, 0.0)
+        out_ref[each : each + 1, :] = e_ref[dest_rep, line : line + 1, :]
+        for v in range(width):
+            row = e_ref[dest_rep, line + 1 : line + 2, :]
+            mine = (wide == v) & (dest_rep == rep)
+            out_ref[each + 1 + v : each + 2 + v, :] = jnp.where(mine, row, 0.0)
+
+
+def margin_call(scalars, own_list, dots, bwd_terms, fwd_parts, places, width, whole):
     terms, slots = len(bwd_terms), len(dots)
     reps, rows, length = dots[0].shape
     lines = -(-(slots * (rows // BLOCK) + 2) // 8) * 8
     tile = length if whole else rows
+    count, taken = width * reps, -(-(CAND // width + 1 + width) // 8) * 8
+    smem = pl.BlockSpec(memory_space=pltpu.SMEM)
     if whole:
         s_spec = p_spec = f_spec = e_spec = pl.BlockSpec(memory_space=pltpu.VMEM)
     else:
         s_spec = pl.BlockSpec((reps, rows, tile), lambda j: (0, 0, j))
         p_spec = pl.BlockSpec(bwd_terms[0].shape, lambda j: (0, 0, 0))
         f_spec = pl.BlockSpec((reps, 1, tile), lambda j: (0, 0, j))
-        e_spec = pl.BlockSpec((reps, lines, tile), lambda j: (0, 0, j))
+        e_spec = pl.BlockSpec((taken, tile), lambda j: (0, j))
     return pl.pallas_call(
-        functools.partial(margin_kernel, places, terms),
+        functools.partial(margin_kernel, places, terms, width),
         grid=(length // tile,),
-        in_specs=[pl.BlockSpec(memory_space=pltpu.SMEM)]
+        in_specs=[smem, smem]
         + [s_spec] * slots
         + [p_spec] * terms
         + [f_spec],
-        out_specs=e_spec,
+        out_specs=[e_spec] * count,
         scratch_shapes=[
+            pltpu.VMEM((reps, lines, tile), jnp.float32),
             pltpu.VMEM((bwd_terms[0].shape[0], rows), jnp.float32),
             pltpu.VMEM((slots, rows, LANES), jnp.float32),
+            pltpu.SMEM((CAND,), jnp.int32),
+            pltpu.SMEM((CAND,), jnp.int32),
         ],
-        out_shape=jax.ShapeDtypeStruct((reps, lines, length), jnp.float32),
+        out_shape=[jax.ShapeDtypeStruct((taken, length), jnp.float32)] * count,
         compiler_params=pltpu.CompilerParams(
             vmem_limit_bytes=DOTS_LIMIT if whole else VMEM_LIMIT
         ),
         cost_estimate=pl.CostEstimate(
             flops=rows * D, bytes_accessed=rows * D, transcendentals=0
         ),
-    )(scalars, *dots, *bwd_terms, fwd_parts)
-
-
-def final_kernel(width, reps, planes, slots, parts, sc_ref, list_ref, g_ref, best_ref, fwd_ref, bwd_ref):
-    shard, wide, rep = sc_ref[0], sc_ref[1], sc_ref[2]
-    both = (planes - 1) // 2
-    fwd_line = slots * parts
-    fwd = g_ref[0, 0, fwd_line : fwd_line + 1, :]
-    for g in range(1, width * reps):
-        fwd = fwd + g_ref[g, 0, fwd_line : fwd_line + 1, :]
-    fwd = fwd / (K * math.sqrt(D))
+    )(scalars, own_list, *dots, *bwd_terms, fwd_parts)
+
+
+def final_kernel(width, *refs):
+    taken, (best_ref, fwd_ref, bwd_ref) = refs[:-3], refs[-3:]
+    total = taken[0][...]
+    for ref in taken[1:]:
+        total = total + ref[...]
+    each, length = best_ref.shape
+    rows = length // width
+    fwd = total[each : each + 1] / (K * math.sqrt(D))
     fwd_ref[...] = fwd
-    rows = parts * BLOCK
     for v in range(width):
-        part = g_ref[v * reps + rep, 0, fwd_line + 1 : fwd_line + 2, 0:rows]
+        part = total[each + 1 + v : each + 2 + v, 0:rows]
         bwd_ref[:, v * rows : (v + 1) * rows] = part.astype(jnp.bfloat16)
-    half = 0.5 * fwd
-    per_width = best_ref.shape[0]
-    for c in range(per_width):
-        block = list_ref[wide * per_width + c]
-        holder = block // (parts * width)
-        local = block - holder * (parts * width)
-        plane = holder // reps
-        peer = (local // parts) * reps + holder - plane * reps
-        hops = jnp.abs(shard - plane)
-        near = 2 * hops - 1 + jnp.where(plane > shard, 1, 0)
-        slot = jnp.where(hops == 0, 0, jnp.where(hops <= both, near, both + hops))
-        line = slot * parts + local - (local // parts) * parts
-        best_ref[c : c + 1, :] = g_ref[peer, 0, pl.ds(line, 1), :] - half
-
-
-def final_call(scalars, own_list, gathered, width, reps, planes, slots, parts):
-    lines, length = gathered.shape[2:]
-    per_width = CAND // width
+    best_ref[...] = total[:each] - 0.5 * fwd
+
+
+def final_call(taken, width):
+    length = taken[0].shape[1]
+    vmem = pl.BlockSpec(memory_space=pltpu.VMEM)
     return pl.pallas_call(
-        functools.partial(final_kernel, width, reps, planes, slots, parts),
-        grid_spec=pltpu.PrefetchScalarGridSpec(
-            num_scalar_prefetch=2,
-            grid=(1,),
-            in_specs=[
-                pl.BlockSpec((width * reps, 1, lines, length), lambda j, sc, ls: (0, sc[2], 0, 0))
-            ],
-            out_specs=[
-                pl.BlockSpec((per_width, length), lambda j, sc, ls: (0, 0)),
-                pl.BlockSpec((1, length), lambda j, sc, ls: (0, 0)),
-                pl.BlockSpec((1, length), lambda j, sc, ls: (0, 0)),
-            ],
-        ),
+        functools.partial(final_kernel, width),
+        in_specs=[vmem] * len(taken),
+        out_specs=[vmem] * 3,
         out_shape=[
-            jax.ShapeDtypeStruct((per_width, length), jnp.float32),
+            jax.ShapeDtypeStruct((CAND // width, length), jnp.float32),
             jax.ShapeDtypeStruct((1, length), jnp.float32),
             jax.ShapeDtypeStruct((1, length), jnp.bfloat16),
         ],
         compiler_params=pltpu.CompilerParams(vmem_limit_bytes=16 * MIB),
-    )(scalars, own_list, gathered)
+    )(*taken)
 
 
 def together(*values):
@@ -357,7 +378,7 @@
     queue = [(0, "own")]
     for hop in range(1, planes):
         queue += [(hop, "up"), (hop, "down")] if hop <= both else [(hop, "one")]
-    dots, places, state = [], [], None
+    dots, places, state, waiting = [], [], None, []
     scalars = jnp.stack([shard, wide, rep]).astype(jnp.int32)
 
     heads, tails = {0: first}, {0: rest}
@@ -390,23 +411,26 @@
         else:
             sides = {"up": (0,), "down": (1,), "one": (0, 1)}[way]
             chunks = [arrived(hop, side) for side in sides]
-        out, *state = dots_call(scalars, fidx, src, chunks, state, planes, hop, way)
-        dots.append(out)
-        places.append((hop, way))
+        waiting.append((hop, way, chunks))
+        if place == 0 or place >= len(queue) - 2 or len(waiting) == 3:
+            out, state = dots_call(scalars, fidx, src, waiting, state, planes)
+            dots += out
+            places += [(hop, way) for hop, way, _ in waiting]
+            waiting = []
 
     def over_planes(values):
         if planes > 4:
             return [lax.psum(values, "shard")]
         return [values] + [shift(values, "shard", planes, d) for d in range(1, planes)]
 
-    lines = margin_call(
-        scalars, dots, over_planes(state[0]), state[1], tuple(places), planes <= 4
+    own_list = lax.dynamic_index_in_dim(cand_lists, shard, 0, keepdims=False)
+    outs = margin_call(
+        scalars, own_list, dots, over_planes(state[0]), state[1], tuple(places), width, planes <= 4
     )
-    gathered = lax.all_gather(lines, ("width", "rep"), axis=0, tiled=False)
-    own_list = lax.dynamic_index_in_dim(cand_lists, shard, 0, keepdims=False)
-    best, fwd_mean, bwd_mean = final_call(
-        scalars, own_list, gathered, width, reps, planes, len(dots), parts
-    )
+    taken = [outs[0]]
+    for d in range(1, width * reps):
+        taken.append(shift(outs[d], ("width", "rep"), width * reps, d))
+    best, fwd_mean, bwd_mean = final_call(taken, width)
     return (jnp.transpose(best), fwd_mean.reshape(-1), bwd_mean.reshape(-1))
 
 

time: 119 us -> 117 us (0.983)
  blocking collectives: 6.51 us -> 0 us
  waiting for transfers between devices: 42.1 us -> 48.4 us
  Pallas kernels: 29.6 us -> 26.1 us
    all_gather x1 -> x0, blocking collectives: 6.51 us -> none  [on_device(): gathered = lax.all_gather(lines, ('width', 'rep'), axis=0, tiled=False)]
    ppermute x8 -> x11, waiting for transfers between devices: 12.9 us -> 16.7 us  [shift(): lax.ppermute(values, axis, [((i + by) % count, i) for i in range(count)])]
    pallas_call x7 -> x5, Pallas kernels: 28.7 us -> 25.2 us  [the longest x3 21.3 us: dots_call(): pl.pallas_call(functools.partial(dots_kernel, reps, width, planes, entrie...]
    ppermute x12, waiting for transfers between devices: 29.3 us -> 31.7 us  [moved(): out += [lax.ppermute(c, 'shard', pairs) for c in side]]
    ppermute x8 -> x11, starting transfers between devices: 7.19 us -> 7.92 us  [shift(): lax.ppermute(values, axis, [((i + by) % count, i) for i in range(count)])]
    unnamed x28 -> x24, local copies, waits for them, and re-layouts: 9.52 us -> 9.76 us
  transfers between devices with their start and end apart: 20 -> 23, of which waited for: 8 -> 11; matrix products, arithmetic and copies ran while one was open for 1% -> 1% of each run, Pallas kernels for 16% -> 13%
where the time goes in v5:
time: 117 us; the launch traced here: 116 us
  waiting for transfers between devices  48.4 us (41%)
  starting transfers between devices  27 us (23%)
  Pallas kernels  26.1 us (22%)
  local copies, waits for them, and re-layouts  11.1 us (9%)
  other arithmetic  2.32 us (2%)
    ppermute x12, waiting for transfers between devices, moved(): out += [lax.ppermute(c, 'shard', pairs) for c in side]  31.7 us
    pallas_call x3, Pallas kernels, dots_call(): pl.pallas_call(functools.partial(dots_kernel, reps, width, planes, entrie...  21.3 us
    ppermute x12, starting transfers between devices, moved(): out += [lax.ppermute(c, 'shard', pairs) for c in side]  19.1 us
    ppermute x11, waiting for transfers between devices, shift(): lax.ppermute(values, axis, [((i + by) % count, i) for i in range(count)])  16.7 us
    unnamed x24, local copies, waits for them, and re-layouts  9.76 us
    ppermute x11, starting transfers between devices, shift(): lax.ppermute(values, axis, [((i + by) % count, i) for i in range(count)])  7.92 us
    pallas_call x1, Pallas kernels, margin_call(): pl.pallas_call(functools.partial(margin_kernel, places, terms, width), gr...  3.28 us
  transfers between devices with their start and end apart: 23, of which 11 were waited for; matrix products, arithmetic and copies ran while one was open for 1% of the time, Pallas kernels for 13%

profile of v5, /device:TPU:0, one launch (start us, length us, event | category | flops | bytes accessed | tf_op | source)
XLA Modules:
  0.0 115.9 jit_solution(3783523307582699505)
XLA Ops:
  1.5 1.3 %constant_dynamic-slice_fusion = (bf16[512,512]{1,0:T(8,128)(2,1)S(1)}, bf16[512,512]{1,0:T(8,128)(2,1)S(1)}) fusion(bf16[1024,512]{1,0:T(8,128)(2,1)} %param.8, s32[]{:T(128)S(6)} %select_n.19, s32[]{:T(128)S(6)} %select_n.17), kind=kLoop, calls=%fused_computation.21 | loop fusion | bytes 2097160 | tf_op jit(solution)/shard_map/dynamic_slice | solution.py:344
  2.9 3.0 %collective-permute-start = (bf16[528,512]{1,0:T(8,128)(2,1)S(1)}, bf16[528,512]{1,0:T(8,128)(2,1)S(1)}, u32[]{:S(2)}, u32[]{:S(2)}) collective-permute-start(bf16[528,512]{1,0:T(8,128)(2,1)S(1)} %pad_maximum_fusion), channel_id=1, source_target_pairs={{2,0},{0,2},{3,1},{1,3},{6,4},{4,6},{7,5},{5,7},{10,8},{8,10},{11,... | collective-permute-start | bytes 1622024 | tf_op jit(solution)/shard_map/ppermute | solution.py:347
  6.7 3.5 %collective-permute-start.5 = (bf16[512,512]{1,0:T(8,128)(2,1)S(1)}, bf16[512,512]{1,0:T(8,128)(2,1)S(1)}, u32[]{:S(2)}, u32[]{:S(2)}) collective-permute-start(bf16[512,512]{1,0:T(8,128)(2,1)S(1)} %get-tuple-element.57.refs_3_), channel_id=1, source_target_pairs={{0,4},{4,8},{8,12},{1,5},{5,9},{9,13},{2,6},{6,10},{10,14},{3,7},{... | collective-permute-start | bytes 1572872 | tf_op jit(solution)/shard_map/ppermute | solution.py:374
  10.3 1.3 %collective-permute-start.7 = (bf16[512,512]{1,0:T(8,128)(2,1)S(1)}, bf16[512,512]{1,0:T(8,128)(2,1)S(1)}, u32[]{:S(2)}, u32[]{:S(2)}) collective-permute-start(bf16[512,512]{1,0:T(8,128)(2,1)S(1)} %get-tuple-element.57.refs_3_), channel_id=1, source_target_pairs={{4,0},{8,4},{12,8},{5,1},{9,5},{13,9},{6,2},{10,6},{14,10},{7,3},{... | collective-permute-start | bytes 1572872 | tf_op jit(solution)/shard_map/ppermute | solution.py:374
  11.6 6.6 %collective-permute-done.refs_4_ = bf16[528,512]{1,0:T(8,128)(2,1)S(1)} collective-permute-done((bf16[528,512]{1,0:T(8,128)(2,1)S(1)}, bf16[528,512]{1,0:T(8,128)(2,1)S(1)}, u32[]{:S(2)}, u32[]{:S(2)}) %collective-permute-start) | collective-permute-done | bytes 540704 | tf_op jit(solution)/shard_map/ppermute | solution.py:347
  18.2 1.7 %collective-permute-start.2 = (bf16[1024,512]{1,0:T(8,128)(2,1)}, bf16[1024,512]{1,0:T(8,128)(2,1)S(1)}, u32[]{:S(2)}, u32[]{:S(2)}) collective-permute-start(bf16[1024,512]{1,0:T(8,128)(2,1)} %refs_0_), channel_id=1, source_target_pairs={{2,0},{0,2},{3,1},{1,3},{6,4},{4,6},{7,5},{5,7},{10,8},{8,10},{11,... | collective-permute-start | bytes 3145736 | tf_op jit(solution)/shard_map/ppermute | solution.py:347
  19.9 4.3 %collective-permute-start.3 = (bf16[528,512]{1,0:T(8,128)(2,1)S(1)}, bf16[528,512]{1,0:T(8,128)(2,1)}, u32[]{:S(2)}, u32[]{:S(2)}) collective-permute-start(bf16[528,512]{1,0:T(8,128)(2,1)S(1)} %collective-permute-done.refs_4_), channel_id=1, source_target_pairs={{0,4},{4,8},{8,12},{1,5},{5,9},{9,13},{2,6},{6,10},{10,14},{3,7},{... | collective-permute-start | bytes 1622024 | tf_op jit(solution)/shard_map/ppermute | solution.py:374
  24.2 1.3 %collective-permute-start.4 = (bf16[528,512]{1,0:T(8,128)(2,1)S(1)}, bf16[528,512]{1,0:T(8,128)(2,1)}, u32[]{:S(2)}, u32[]{:S(2)}) collective-permute-start(bf16[528,512]{1,0:T(8,128)(2,1)S(1)} %collective-permute-done.refs_4_), channel_id=1, source_target_pairs={{4,0},{8,4},{12,8},{5,1},{9,5},{13,9},{6,2},{10,6},{14,10},{7,3},{... | collective-permute-start | bytes 1622024 | tf_op jit(solution)/shard_map/ppermute | solution.py:374
  27.0 1.3 %collective-permute-start.8 = (bf16[512,512]{1,0:T(8,128)(2,1)S(1)}, bf16[512,512]{1,0:T(8,128)(2,1)S(1)}, u32[]{:S(2)}, u32[]{:S(2)}) collective-permute-start(bf16[512,512]{1,0:T(8,128)(2,1)S(1)} %collective-permute-done.7.refs_5_), channel_id=1, source_target_pairs={{4,0},{8,4},{5,1},{9,5},{6,2},{10,6},{7,3},{11,7},{20,16},{24,20},... | collective-permute-start | bytes 1572872 | tf_op jit(solution)/shard_map/ppermute | solution.py:374
  29.1 20.8 %collective-permute-done.8.refs_9_ = bf16[512,512]{1,0:T(8,128)(2,1)S(1)} collective-permute-done((bf16[512,512]{1,0:T(8,128)(2,1)S(1)}, bf16[512,512]{1,0:T(8,128)(2,1)S(1)}, u32[]{:S(2)}, u32[]{:S(2)}) %collective-permute-start.8) | collective-permute-done | bytes 524320 | tf_op jit(solution)/shard_map/ppermute | solution.py:374
  50.7 1.2 %copy-done.3 = bf16[1024,512]{1,0:T(8,128)(2,1)S(1)} copy-done((bf16[1024,512]{1,0:T(8,128)(2,1)S(1)}, bf16[1024,512]{1,0:T(8,128)(2,1)}, u32[]{:S(2)}) %copy-start.3) | copy-done | bytes 1048600
  52.9 1.5 %collective-permute-start.10 = (bf16[528,512]{1,0:T(8,128)(2,1)}, bf16[528,512]{1,0:T(8,128)(2,1)}, u32[]{:S(2)}, u32[]{:S(2)}) collective-permute-start(bf16[528,512]{1,0:T(8,128)(2,1)} %collective-permute-done.3.refs_4_), channel_id=1, source_target_pairs={{4,8},{8,12},{5,9},{9,13},{6,10},{10,14},{7,11},{11,15},{20,24},{2... | collective-permute-start | bytes 1622024 | tf_op jit(solution)/shard_map/ppermute | solution.py:374
  54.4 1.3 %collective-permute-start.11 = (bf16[528,512]{1,0:T(8,128)(2,1)}, bf16[528,512]{1,0:T(8,128)(2,1)}, u32[]{:S(2)}, u32[]{:S(2)}) collective-permute-start(bf16[528,512]{1,0:T(8,128)(2,1)} %collective-permute-done.4.refs_6_), channel_id=1, source_target_pairs={{4,0},{8,4},{5,1},{9,5},{6,2},{10,6},{7,3},{11,7},{20,16},{24,20},... | collective-permute-start | bytes 1622024 | tf_op jit(solution)/shard_map/ppermute | solution.py:374
  55.8 1.4 %collective-permute-done.9.refs_2_ = bf16[1024,1024]{1,0:T(8,128)(2,1)} collective-permute-done((bf16[1024,1024]{1,0:T(8,128)(2,1)S(1)}, bf16[1024,1024]{1,0:T(8,128)(2,1)}, u32[]{:S(2)}, u32[]{:S(2)}) %collective-permute-start.9) | collective-permute-done | bytes 2097184 | tf_op jit(solution)/shard_map/ppermute | solution.py:347
  57.2 5.5 %shard_map.95 = (f32[2,512,1024]{2,1,0:T(8,128)S(1)}, f32[4,1,512]{2,1,0:T(1,128)S(1)}, f32[2,1,1024]{2,1,0:T(1,128)S(1)}) custom-call(s32[3]{0:T(128)S(1)} %pad_add_fusion.2.sc_ref, s32[2,4,1024]{2,1,0:T(4,128)S(1)} %pad_add_fusion.refs_0_, bf16[1024,1024]{1,0:T(8,128)(2,1)S(1)} %shard_map.94.refs_1_, bf16[1024,1024]{1,0:T(8,128)(2,1)} %collective-permute-done.9.refs_2_, ...), custom_call_target="tpu_custom_call" | custom-call | flops 524288 | bytes 524288 | tf_op jit(solution)/shard_map/pallas_call | solution.py:162
  62.7 2.0 %copy-done.1 = f32[2,512,1024]{2,1,0:T(8,128)} copy-done((f32[2,512,1024]{2,1,0:T(8,128)}, f32[2,512,1024]{2,1,0:T(8,128)S(1)}, u32[]{:S(2)}) %copy-start.1) | copy-done | bytes 4194328
  65.5 1.3 %collective-permute-start.15 = (bf16[512,512]{1,0:T(8,128)(2,1)}, bf16[512,512]{1,0:T(8,128)(2,1)S(1)}, u32[]{:S(2)}, u32[]{:S(2)}) collective-permute-start(bf16[512,512]{1,0:T(8,128)(2,1)} %copy-done.10), channel_id=1, source_target_pairs={{4,0},{5,1},{6,2},{7,3},{20,16},{21,17},{22,18},{23,19}} | collective-permute-start | bytes 1572872 | tf_op jit(solution)/shard_map/ppermute | solution.py:374
  66.8 4.9 %collective-permute-done.11.refs_10_ = bf16[528,512]{1,0:T(8,128)(2,1)} collective-permute-done((bf16[528,512]{1,0:T(8,128)(2,1)}, bf16[528,512]{1,0:T(8,128)(2,1)}, u32[]{:S(2)}, u32[]{:S(2)}) %collective-permute-start.11) | collective-permute-done | bytes 540704 | tf_op jit(solution)/shard_map/ppermute | solution.py:374
  72.4 1.3 %collective-permute-start.16 = (bf16[528,512]{1,0:T(8,128)(2,1)}, bf16[528,512]{1,0:T(8,128)(2,1)S(1)}, u32[]{:S(2)}, u32[]{:S(2)}) collective-permute-start(bf16[528,512]{1,0:T(8,128)(2,1)} %collective-permute-done.11.refs_10_), channel_id=1, source_target_pairs={{4,0},{5,1},{6,2},{7,3},{20,16},{21,17},{22,18},{23,19}} | collective-permute-start | bytes 1622024 | tf_op jit(solution)/shard_map/ppermute | solution.py:374
  73.7 1.0 copy-done.5
  74.7 1.0 copy-done.7
  75.8 1.0 copy-done.9
  76.8 1.0 copy-done.11
  77.9 10.1 %shard_map.96 = (f32[2,512,1024]{2,1,0:T(8,128)S(1)}, f32[2,512,1024]{2,1,0:T(8,128)S(1)}, f32[2,512,1024]{2,1,0:T(8,128)S(1)}, f32[4,1,512]{2,1,0:T(1,128)S(1)}, f32[2,1,1024]{2,1,0:T(1,128)S(1)}) custom-call(s32[3]{0:T(128)S(1)} %pad_add_fusion.2.sc_ref, s32[2,4,1024]{2,1,0:T(4,128)S(1)} %pad_add_fusion.1.refs_0_, ...), custom_call_target="tpu_custom_call" | custom-call | flops 6442975232 | bytes 13107200 | tf_op jit(solution)/shard_map/pallas_call | solution.py:162
  88.0 6.0 %collective-permute-done.16.refs_6_ = bf16[528,512]{1,0:T(8,128)(2,1)S(1)} collective-permute-done((bf16[528,512]{1,0:T(8,128)(2,1)}, bf16[528,512]{1,0:T(8,128)(2,1)S(1)}, u32[]{:S(2)}, u32[]{:S(2)}) %collective-permute-start.16) | collective-permute-done | bytes 540704 | tf_op jit(solution)/shard_map/ppermute | solution.py:374
  94.0 5.8 %shard_map.97 = (f32[2,512,1024]{2,1,0:T(8,128)S(1)}, f32[4,1,512]{2,1,0:T(1,128)S(1)}, f32[2,1,1024]{2,1,0:T(1,128)S(1)}) custom-call(s32[3]{0:T(128)S(1)} %pad_add_fusion.2.sc_ref, s32[2,4,1024]{2,1,0:T(4,128)S(1)} %pad_add_fusion.1.refs_0_, bf16[1024,1024]{1,0:T(8,128)(2,1)S(1)} %shard_map.94.refs_1_, bf16[1024,1024]{1,0:T(8,128)(2,1)} %collective-permute-done.9.refs_2_, ...), custom_call_target="tpu_custom_call" | custom-call | flops 2148007936 | bytes 4718592 | tf_op jit(solution)/shard_map/pallas_call | solution.py:162
  100.7 1.2 %collective-permute-start.19 = (f32[4,1,512]{2,1,0:T(1,128)S(1)}, f32[4,1,512]{2,1,0:T(1,128)S(1)}, u32[]{:S(2)}, u32[]{:S(2)}) collective-permute-start(f32[4,1,512]{2,1,0:T(1,128)S(1)} %get-tuple-element.48.refs_5_), channel_id=1, source_target_pairs={{12,0},{0,4},{4,8},{8,12},{13,1},{1,5},{5,9},{9,13},{14,2},{2,6},{... | collective-permute-start | bytes 24584 | tf_op jit(solution)/shard_map/ppermute | solution.py:347
  101.9 1.6 %collective-permute-done.17.refs_6_ = f32[4,1,512]{2,1,0:T(1,128)S(1)} collective-permute-done((f32[4,1,512]{2,1,0:T(1,128)S(1)}, f32[4,1,512]{2,1,0:T(1,128)S(1)}, u32[]{:S(2)}, u32[]{:S(2)}) %collective-permute-start.17) | collective-permute-done | bytes 8224 | tf_op jit(solution)/shard_map/ppermute | solution.py:347
  103.5 1.8 %collective-permute-done.18.refs_7_ = f32[4,1,512]{2,1,0:T(1,128)S(1)} collective-permute-done((f32[4,1,512]{2,1,0:T(1,128)S(1)}, f32[4,1,512]{2,1,0:T(1,128)S(1)}, u32[]{:S(2)}, u32[]{:S(2)}) %collective-permute-start.18) | collective-permute-done | bytes 8224 | tf_op jit(solution)/shard_map/ppermute | solution.py:347
  106.1 3.3 %shard_map.98 = (f32[16,1024]{1,0:T(8,128)S(1)}, f32[16,1024]{1,0:T(8,128)S(1)}, f32[16,1024]{1,0:T(8,128)S(1)}, f32[16,1024]{1,0:T(8,128)S(1)}) custom-call(s32[3]{0:T(128)S(1)} %pad_add_fusion.2.sc_ref, s32[16]{0:T(128)S(1)} %fusion.8.list_ref, f32[2,512,1024]{2,1,0:T(8,128)S(1)} %copy-done.2, f32[2,512,1024]{2,1,0:T(8,128)S(1)} %get-tuple-element.42.refs_1_, ...), custom_call_target="tpu_custom_call" | custom-call | flops 524288 | bytes 524288 | tf_op jit(solution)/shard_map/pallas_call | solution.py:272
  110.3 1.6 %collective-permute-done.20.refs_1_ = f32[16,1024]{1,0:T(8,128)S(1)} collective-permute-done((f32[16,1024]{1,0:T(8,128)S(1)}, f32[16,1024]{1,0:T(8,128)S(1)}, u32[]{:S(2)}, u32[]{:S(2)}) %collective-permute-start.20) | collective-permute-done | bytes 65568 | tf_op jit(solution)/shard_map/ppermute | solution.py:347
  111.9 2.6 %collective-permute-done.21.refs_2_ = f32[16,1024]{1,0:T(8,128)S(1)} collective-permute-done((f32[16,1024]{1,0:T(8,128)S(1)}, f32[16,1024]{1,0:T(8,128)S(1)}, u32[]{:S(2)}, u32[]{:S(2)}) %collective-permute-start.21) | collective-permute-done | bytes 65568 | tf_op jit(solution)/shard_map/ppermute | solution.py:347
  (56 shorter events, 11.6 us)
Async XLA Ops:
  0.6 101.2 %copy-start = (s32[4,16]{1,0:T(4,128)S(1)}, s32[4,16]{1,0:T(4,128)}, u32[]{:S(2)}) copy-start(s32[4,16]{1,0:T(4,128)} %param.13) | copy-start | bytes 772
  2.9 15.3 %collective-permute-start = (bf16[528,512]{1,0:T(8,128)(2,1)S(1)}, bf16[528,512]{1,0:T(8,128)(2,1)S(1)}, u32[]{:S(2)}, u32[]{:S(2)}) collective-permute-start(bf16[528,512]{1,0:T(8,128)(2,1)S(1)} %pad_maximum_fusion), channel_id=1, source_target_pairs={{2,0},{0,2},{3,1},{1,3},{6,4},{4,6},{7,5},{5,7},{10,8},{8,10},{11,... | collective-permute-start | bytes 1622024 | tf_op jit(solution)/shard_map/ppermute | solution.py:347
  6.7 4.9 %collective-permute-start.1 = (s32[4,1024]{1,0:T(4,128)S(1)}, s32[4,1024]{1,0:T(4,128)S(1)}, u32[]{:S(2)}, u32[]{:S(2)}) collective-permute-start(s32[4,1024]{1,0:T(4,128)S(1)} %get-tuple-element.36), channel_id=1, source_target_pairs={{1,0},{0,1},{3,2},{2,3},{5,4},{4,5},{7,6},{6,7},{9,8},{8,9},{11,10... | collective-permute-start | bytes 49160 | tf_op jit(solution)/shard_map/ppermute | solution.py:347
  6.7 18.8 %collective-permute-start.5 = (bf16[512,512]{1,0:T(8,128)(2,1)S(1)}, bf16[512,512]{1,0:T(8,128)(2,1)S(1)}, u32[]{:S(2)}, u32[]{:S(2)}) collective-permute-start(bf16[512,512]{1,0:T(8,128)(2,1)S(1)} %get-tuple-element.57.refs_3_), channel_id=1, source_target_pairs={{0,4},{4,8},{8,12},{1,5},{5,9},{9,13},{2,6},{6,10},{10,14},{3,7},{... | collective-permute-start | bytes 1572872 | tf_op jit(solution)/shard_map/ppermute | solution.py:374
  10.3 16.8 %collective-permute-start.7 = (bf16[512,512]{1,0:T(8,128)(2,1)S(1)}, bf16[512,512]{1,0:T(8,128)(2,1)S(1)}, u32[]{:S(2)}, u32[]{:S(2)}) collective-permute-start(bf16[512,512]{1,0:T(8,128)(2,1)S(1)} %get-tuple-element.57.refs_3_), channel_id=1, source_target_pairs={{4,0},{8,4},{12,8},{5,1},{9,5},{13,9},{6,2},{10,6},{14,10},{7,3},{... | collective-permute-start | bytes 1572872 | tf_op jit(solution)/shard_map/ppermute | solution.py:374
  18.2 32.5 %collective-permute-start.2 = (bf16[1024,512]{1,0:T(8,128)(2,1)}, bf16[1024,512]{1,0:T(8,128)(2,1)S(1)}, u32[]{:S(2)}, u32[]{:S(2)}) collective-permute-start(bf16[1024,512]{1,0:T(8,128)(2,1)} %refs_0_), channel_id=1, source_target_pairs={{2,0},{0,2},{3,1},{1,3},{6,4},{4,6},{7,5},{5,7},{10,8},{8,10},{11,... | collective-permute-start | bytes 3145736 | tf_op jit(solution)/shard_map/ppermute | solution.py:347
  19.9 30.0 %collective-permute-start.3 = (bf16[528,512]{1,0:T(8,128)(2,1)S(1)}, bf16[528,512]{1,0:T(8,128)(2,1)}, u32[]{:S(2)}, u32[]{:S(2)}) collective-permute-start(bf16[528,512]{1,0:T(8,128)(2,1)S(1)} %collective-permute-done.refs_4_), channel_id=1, source_target_pairs={{0,4},{4,8},{8,12},{1,5},{5,9},{9,13},{2,6},{6,10},{10,14},{3,7},{... | collective-permute-start | bytes 1622024 | tf_op jit(solution)/shard_map/ppermute | solution.py:374
  24.2 25.7 %collective-permute-start.4 = (bf16[528,512]{1,0:T(8,128)(2,1)S(1)}, bf16[528,512]{1,0:T(8,128)(2,1)}, u32[]{:S(2)}, u32[]{:S(2)}) collective-permute-start(bf16[528,512]{1,0:T(8,128)(2,1)S(1)} %collective-permute-done.refs_4_), channel_id=1, source_target_pairs={{4,0},{8,4},{12,8},{5,1},{9,5},{13,9},{6,2},{10,6},{14,10},{7,3},{... | collective-permute-start | bytes 1622024 | tf_op jit(solution)/shard_map/ppermute | solution.py:374
  25.5 3.6 %collective-permute-start.6 = (bf16[512,512]{1,0:T(8,128)(2,1)S(1)}, bf16[512,512]{1,0:T(8,128)(2,1)S(1)}, u32[]{:S(2)}, u32[]{:S(2)}) collective-permute-start(bf16[512,512]{1,0:T(8,128)(2,1)S(1)} %collective-permute-done.5.refs_3_), channel_id=1, source_target_pairs={{4,8},{8,12},{5,9},{9,13},{6,10},{10,14},{7,11},{11,15},{20,24},{2... | collective-permute-start | bytes 1572872 | tf_op jit(solution)/shard_map/ppermute | solution.py:374
  27.0 22.9 %collective-permute-start.8 = (bf16[512,512]{1,0:T(8,128)(2,1)S(1)}, bf16[512,512]{1,0:T(8,128)(2,1)S(1)}, u32[]{:S(2)}, u32[]{:S(2)}) collective-permute-start(bf16[512,512]{1,0:T(8,128)(2,1)S(1)} %collective-permute-done.7.refs_5_), channel_id=1, source_target_pairs={{4,0},{8,4},{5,1},{9,5},{6,2},{10,6},{7,3},{11,7},{20,16},{24,20},... | collective-permute-start | bytes 1572872 | tf_op jit(solution)/shard_map/ppermute | solution.py:374
  29.1 20.8 %copy-start.8 = (bf16[512,512]{1,0:T(8,128)(2,1)}, bf16[512,512]{1,0:T(8,128)(2,1)S(1)}, u32[]{:S(2)}) copy-start(bf16[512,512]{1,0:T(8,128)(2,1)S(1)} %collective-permute-done.6.refs_7_) | copy-start | bytes 1572868
  50.7 1.2 %copy-start.3 = (bf16[1024,512]{1,0:T(8,128)(2,1)S(1)}, bf16[1024,512]{1,0:T(8,128)(2,1)}, u32[]{:S(2)}) copy-start(bf16[1024,512]{1,0:T(8,128)(2,1)} %refs_0_) | copy-start | bytes 3145732
  52.8 4.4 %collective-permute-start.9 = (bf16[1024,1024]{1,0:T(8,128)(2,1)S(1)}, bf16[1024,1024]{1,0:T(8,128)(2,1)}, u32[]{:S(2)}, u32[]{:S(2)}) collective-permute-start(bf16[1024,1024]{1,0:T(8,128)(2,1)S(1)} %shard_map.94.refs_1_), channel_id=1, source_target_pairs={{1,0},{0,1},{3,2},{2,3},{5,4},{4,5},{7,6},{6,7},{9,8},{8,9},{11,10... | collective-permute-start | bytes 6291464 | tf_op jit(solution)/shard_map/ppermute | solution.py:347
  52.9 13.9 %collective-permute-start.10 = (bf16[528,512]{1,0:T(8,128)(2,1)}, bf16[528,512]{1,0:T(8,128)(2,1)}, u32[]{:S(2)}, u32[]{:S(2)}) collective-permute-start(bf16[528,512]{1,0:T(8,128)(2,1)} %collective-permute-done.3.refs_4_), channel_id=1, source_target_pairs={{4,8},{8,12},{5,9},{9,13},{6,10},{10,14},{7,11},{11,15},{20,24},{2... | collective-permute-start | bytes 1622024 | tf_op jit(solution)/shard_map/ppermute | solution.py:374
  54.4 17.3 %collective-permute-start.11 = (bf16[528,512]{1,0:T(8,128)(2,1)}, bf16[528,512]{1,0:T(8,128)(2,1)}, u32[]{:S(2)}, u32[]{:S(2)}) collective-permute-start(bf16[528,512]{1,0:T(8,128)(2,1)} %collective-permute-done.4.refs_6_), channel_id=1, source_target_pairs={{4,0},{8,4},{5,1},{9,5},{6,2},{10,6},{7,3},{11,7},{20,16},{24,20},... | collective-permute-start | bytes 1622024 | tf_op jit(solution)/shard_map/ppermute | solution.py:374
  62.7 2.0 %copy-start.1 = (f32[2,512,1024]{2,1,0:T(8,128)}, f32[2,512,1024]{2,1,0:T(8,128)S(1)}, u32[]{:S(2)}) copy-start(f32[2,512,1024]{2,1,0:T(8,128)S(1)} %get-tuple-element.34.refs_0_) | copy-start | bytes 12582916
  64.6 2.1 %collective-permute-start.12 = (s32[4,1024]{1,0:T(4,128)S(1)}, s32[4,1024]{1,0:T(4,128)S(1)}, u32[]{:S(2)}, u32[]{:S(2)}) collective-permute-start(s32[4,1024]{1,0:T(4,128)S(1)} %get-tuple-element.36), channel_id=1, source_target_pairs={{1,0},{0,1},{3,2},{2,3},{5,4},{4,5},{7,6},{6,7},{9,8},{8,9},{11,10... | collective-permute-start | bytes 49160 | tf_op jit(solution)/shard_map/ppermute | solution.py:347
  64.8 23.2 %collective-permute-start.13 = (bf16[512,512]{1,0:T(8,128)(2,1)}, bf16[512,512]{1,0:T(8,128)(2,1)S(1)}, u32[]{:S(2)}, u32[]{:S(2)}) collective-permute-start(bf16[512,512]{1,0:T(8,128)(2,1)} %copy-done.8), channel_id=1, source_target_pairs={{8,12},{9,13},{10,14},{11,15},{24,28},{25,29},{26,30},{27,31}} | collective-permute-start | bytes 1572872 | tf_op jit(solution)/shard_map/ppermute | solution.py:374
  65.5 22.5 %collective-permute-start.15 = (bf16[512,512]{1,0:T(8,128)(2,1)}, bf16[512,512]{1,0:T(8,128)(2,1)S(1)}, u32[]{:S(2)}, u32[]{:S(2)}) collective-permute-start(bf16[512,512]{1,0:T(8,128)(2,1)} %copy-done.10), channel_id=1, source_target_pairs={{4,0},{5,1},{6,2},{7,3},{20,16},{21,17},{22,18},{23,19}} | collective-permute-start | bytes 1572872 | tf_op jit(solution)/shard_map/ppermute | solution.py:374
  71.7 16.3 %collective-permute-start.14 = (bf16[528,512]{1,0:T(8,128)(2,1)}, bf16[528,512]{1,0:T(8,128)(2,1)S(1)}, u32[]{:S(2)}, u32[]{:S(2)}) collective-permute-start(bf16[528,512]{1,0:T(8,128)(2,1)} %collective-permute-done.10.refs_8_), channel_id=1, source_target_pairs={{8,12},{9,13},{10,14},{11,15},{24,28},{25,29},{26,30},{27,31}} | collective-permute-start | bytes 1622024 | tf_op jit(solution)/shard_map/ppermute | solution.py:374
  72.4 21.6 %collective-permute-start.16 = (bf16[528,512]{1,0:T(8,128)(2,1)}, bf16[528,512]{1,0:T(8,128)(2,1)S(1)}, u32[]{:S(2)}, u32[]{:S(2)}) collective-permute-start(bf16[528,512]{1,0:T(8,128)(2,1)} %collective-permute-done.11.refs_10_), channel_id=1, source_target_pairs={{4,0},{5,1},{6,2},{7,3},{20,16},{21,17},{22,18},{23,19}} | collective-permute-start | bytes 1622024 | tf_op jit(solution)/shard_map/ppermute | solution.py:374
  73.7 1.0 copy-start.5
  74.7 1.0 copy-start.7
  75.8 1.0 copy-start.9
  76.8 1.0 copy-start.11
  87.9 18.2 %copy-start.2 = (f32[2,512,1024]{2,1,0:T(8,128)S(1)}, f32[2,512,1024]{2,1,0:T(8,128)}, u32[]{:S(2)}) copy-start(f32[2,512,1024]{2,1,0:T(8,128)} %copy-done.1) | copy-start | bytes 12582916
  99.8 3.7 %collective-permute-start.17 = (f32[4,1,512]{2,1,0:T(1,128)S(1)}, f32[4,1,512]{2,1,0:T(1,128)S(1)}, u32[]{:S(2)}, u32[]{:S(2)}) collective-permute-start(f32[4,1,512]{2,1,0:T(1,128)S(1)} %get-tuple-element.48.refs_5_), channel_id=1, source_target_pairs={{4,0},{8,4},{12,8},{0,12},{5,1},{9,5},{13,9},{1,13},{6,2},{10,6},{... | collective-permute-start | bytes 24584 | tf_op jit(solution)/shard_map/ppermute | solution.py:347
  100.7 4.5 %collective-permute-start.18 = (f32[4,1,512]{2,1,0:T(1,128)S(1)}, f32[4,1,512]{2,1,0:T(1,128)S(1)}, u32[]{:S(2)}, u32[]{:S(2)}) collective-permute-start(f32[4,1,512]{2,1,0:T(1,128)S(1)} %get-tuple-element.48.refs_5_), channel_id=1, source_target_pairs={{8,0},{12,4},{0,8},{4,12},{9,1},{13,5},{1,9},{5,13},{10,2},{14,6},... | collective-permute-start | bytes 24584 | tf_op jit(solution)/shard_map/ppermute | solution.py:347
  100.7 5.4 %collective-permute-start.19 = (f32[4,1,512]{2,1,0:T(1,128)S(1)}, f32[4,1,512]{2,1,0:T(1,128)S(1)}, u32[]{:S(2)}, u32[]{:S(2)}) collective-permute-start(f32[4,1,512]{2,1,0:T(1,128)S(1)} %get-tuple-element.48.refs_5_), channel_id=1, source_target_pairs={{12,0},{0,4},{4,8},{8,12},{13,1},{1,5},{5,9},{9,13},{14,2},{2,6},{... | collective-permute-start | bytes 24584 | tf_op jit(solution)/shard_map/ppermute | solution.py:347
  109.4 2.5 %collective-permute-start.20 = (f32[16,1024]{1,0:T(8,128)S(1)}, f32[16,1024]{1,0:T(8,128)S(1)}, u32[]{:S(2)}, u32[]{:S(2)}) collective-permute-start(f32[16,1024]{1,0:T(8,128)S(1)} %get-tuple-element.51), channel_id=1, source_target_pairs={{1,0},{2,1},{3,2},{0,3},{5,4},{6,5},{7,6},{4,7},{9,8},{10,9},{11,1... | collective-permute-start | bytes 196616 | tf_op jit(solution)/shard_map/ppermute | solution.py:347
  109.5 5.0 %collective-permute-start.21 = (f32[16,1024]{1,0:T(8,128)S(1)}, f32[16,1024]{1,0:T(8,128)S(1)}, u32[]{:S(2)}, u32[]{:S(2)}) collective-permute-start(f32[16,1024]{1,0:T(8,128)S(1)} %get-tuple-element.52), channel_id=1, source_target_pairs={{2,0},{3,1},{0,2},{1,3},{6,4},{7,5},{4,6},{5,7},{10,8},{11,9},{8,1... | collective-permute-start | bytes 196616 | tf_op jit(solution)/shard_map/ppermute | solution.py:347
  110.1 4.6 %collective-permute-start.22 = (f32[16,1024]{1,0:T(8,128)S(1)}, f32[16,1024]{1,0:T(8,128)S(1)}, u32[]{:S(2)}, u32[]{:S(2)}) collective-permute-start(f32[16,1024]{1,0:T(8,128)S(1)} %get-tuple-element.53), channel_id=1, source_target_pairs={{3,0},{0,1},{1,2},{2,3},{7,4},{4,5},{5,6},{6,7},{11,8},{8,9},{9,10... | collective-permute-start | bytes 196616 | tf_op jit(solution)/shard_map/ppermute | solution.py:347
  (3 other events, 2.4 us)

commit v6 on v5

--- a/solution.py
+++ b/solution.py
@@ -304,8 +304,8 @@
     fwd = total[each : each + 1] / (K * math.sqrt(D))
     fwd_ref[...] = fwd
     for v in range(width):
-        part = total[each + 1 + v : each + 2 + v, 0:rows]
-        bwd_ref[:, v * rows : (v + 1) * rows] = part.astype(jnp.bfloat16)
+        part = total[each + 1 + v, 0:rows]
+        bwd_ref[v * rows : (v + 1) * rows] = part.astype(jnp.bfloat16)
     best_ref[...] = total[:each] - 0.5 * fwd
 
 
@@ -319,7 +319,7 @@
         out_shape=[
             jax.ShapeDtypeStruct((CAND // width, length), jnp.float32),
             jax.ShapeDtypeStruct((1, length), jnp.float32),
-            jax.ShapeDtypeStruct((1, length), jnp.bfloat16),
+            jax.ShapeDtypeStruct((length,), jnp.bfloat16),
         ],
         compiler_params=pltpu.CompilerParams(vmem_limit_bytes=16 * MIB),
     )(*taken)
@@ -412,7 +412,7 @@
             sides = {"up": (0,), "down": (1,), "one": (0, 1)}[way]
             chunks = [arrived(hop, side) for side in sides]
         waiting.append((hop, way, chunks))
-        if place == 0 or place >= len(queue) - 2 or len(waiting) == 3:
+        if place == 0 or place >= len(queue) - 2 or len(waiting) == 1:
             out, state = dots_call(scalars, fidx, src, waiting, state, planes)
             dots += out
             places += [(hop, way) for hop, way, _ in waiting]
@@ -431,7 +431,7 @@
     for d in range(1, width * reps):
         taken.append(shift(outs[d], ("width", "rep"), width * reps, d))
     best, fwd_mean, bwd_mean = final_call(taken, width)
-    return (jnp.transpose(best), fwd_mean.reshape(-1), bwd_mean.reshape(-1))
+    return (jnp.transpose(best), fwd_mean.reshape(-1), bwd_mean)
 
 
 def solution(mesh):

time: 117 us -> 116 us (level)
  Pallas kernels: 26.1 us -> 29.2 us
  local copies, waits for them, and re-layouts: 11.1 us -> 9.03 us
    pallas_call x3 -> x5, Pallas kernels: 21.3 us -> 24.5 us  [dots_call(): pl.pallas_call(functools.partial(dots_kernel, reps, width, planes, entrie...]
    unnamed x24, local copies, waits for them, and re-layouts: 9.76 us -> 7.67 us
  transfers between devices with their start and end apart: 23 -> 23, of which waited for: 11 -> 11; matrix products, arithmetic and copies ran while one was open for 1% -> 1% of each run, Pallas kernels for 13% -> 16%
where the time goes in v6:
time: 116 us; the launch traced here: 115 us
  waiting for transfers between devices  47.4 us (41%)
  Pallas kernels  29.2 us (25%)
  starting transfers between devices  27 us (23%)
  local copies, waits for them, and re-layouts  9.03 us (8%)
  other arithmetic  1.72 us (1%)
    ppermute x12, waiting for transfers between devices, moved(): out += [lax.ppermute(c, 'shard', pairs) for c in side]  30.6 us
    pallas_call x5, Pallas kernels, dots_call(): pl.pallas_call(functools.partial(dots_kernel, reps, width, planes, entrie...  24.5 us
    ppermute x12, starting transfers between devices, moved(): out += [lax.ppermute(c, 'shard', pairs) for c in side]  19.1 us
    ppermute x11, waiting for transfers between devices, shift(): lax.ppermute(values, axis, [((i + by) % count, i) for i in range(count)])  16.7 us
    ppermute x11, starting transfers between devices, shift(): lax.ppermute(values, axis, [((i + by) % count, i) for i in range(count)])  7.91 us
    unnamed x24, local copies, waits for them, and re-layouts  7.67 us
    pallas_call x1, Pallas kernels, margin_call(): pl.pallas_call(functools.partial(margin_kernel, places, terms, width), gr...  3.28 us
  transfers between devices with their start and end apart: 23, of which 11 were waited for; matrix products, arithmetic and copies ran while one was open for 1% of the time, Pallas kernels for 16%

profile of v6, /device:TPU:0, one launch (start us, length us, event | category | flops | bytes accessed | tf_op | source)
XLA Modules:
  0.0 115.3 jit_solution(13154842269675334477)
XLA Ops:
  1.5 1.3 %constant_dynamic-slice_fusion = (bf16[512,512]{1,0:T(8,128)(2,1)S(1)}, bf16[512,512]{1,0:T(8,128)(2,1)S(1)}) fusion(bf16[1024,512]{1,0:T(8,128)(2,1)} %param.8, s32[]{:T(128)S(6)} %select_n.19, s32[]{:T(128)S(6)} %select_n.17), kind=kLoop, calls=%fused_computation.21 | loop fusion | bytes 2097160 | tf_op jit(solution)/shard_map/dynamic_slice | solution.py:344
  2.9 3.0 %collective-permute-start = (bf16[528,512]{1,0:T(8,128)(2,1)S(1)}, bf16[528,512]{1,0:T(8,128)(2,1)S(1)}, u32[]{:S(2)}, u32[]{:S(2)}) collective-permute-start(bf16[528,512]{1,0:T(8,128)(2,1)S(1)} %pad_maximum_fusion), channel_id=1, source_target_pairs={{2,0},{0,2},{3,1},{1,3},{6,4},{4,6},{7,5},{5,7},{10,8},{8,10},{11,... | collective-permute-start | bytes 1622024 | tf_op jit(solution)/shard_map/ppermute | solution.py:347
  6.7 3.5 %collective-permute-start.5 = (bf16[512,512]{1,0:T(8,128)(2,1)S(1)}, bf16[512,512]{1,0:T(8,128)(2,1)S(1)}, u32[]{:S(2)}, u32[]{:S(2)}) collective-permute-start(bf16[512,512]{1,0:T(8,128)(2,1)S(1)} %get-tuple-element.65.refs_3_), channel_id=1, source_target_pairs={{0,4},{4,8},{8,12},{1,5},{5,9},{9,13},{2,6},{6,10},{10,14},{3,7},{... | collective-permute-start | bytes 1572872 | tf_op jit(solution)/shard_map/ppermute | solution.py:374
  10.3 1.3 %collective-permute-start.7 = (bf16[512,512]{1,0:T(8,128)(2,1)S(1)}, bf16[512,512]{1,0:T(8,128)(2,1)S(1)}, u32[]{:S(2)}, u32[]{:S(2)}) collective-permute-start(bf16[512,512]{1,0:T(8,128)(2,1)S(1)} %get-tuple-element.65.refs_3_), channel_id=1, source_target_pairs={{4,0},{8,4},{12,8},{5,1},{9,5},{13,9},{6,2},{10,6},{14,10},{7,3},{... | collective-permute-start | bytes 1572872 | tf_op jit(solution)/shard_map/ppermute | solution.py:374
  11.6 6.6 %collective-permute-done.refs_4_ = bf16[528,512]{1,0:T(8,128)(2,1)S(1)} collective-permute-done((bf16[528,512]{1,0:T(8,128)(2,1)S(1)}, bf16[528,512]{1,0:T(8,128)(2,1)S(1)}, u32[]{:S(2)}, u32[]{:S(2)}) %collective-permute-start) | collective-permute-done | bytes 540704 | tf_op jit(solution)/shard_map/ppermute | solution.py:347
  18.2 1.7 %collective-permute-start.2 = (bf16[1024,512]{1,0:T(8,128)(2,1)}, bf16[1024,512]{1,0:T(8,128)(2,1)S(1)}, u32[]{:S(2)}, u32[]{:S(2)}) collective-permute-start(bf16[1024,512]{1,0:T(8,128)(2,1)} %refs_0_), channel_id=1, source_target_pairs={{2,0},{0,2},{3,1},{1,3},{6,4},{4,6},{7,5},{5,7},{10,8},{8,10},{11,... | collective-permute-start | bytes 3145736 | tf_op jit(solution)/shard_map/ppermute | solution.py:347
  19.9 4.3 %collective-permute-start.3 = (bf16[528,512]{1,0:T(8,128)(2,1)S(1)}, bf16[528,512]{1,0:T(8,128)(2,1)}, u32[]{:S(2)}, u32[]{:S(2)}) collective-permute-start(bf16[528,512]{1,0:T(8,128)(2,1)S(1)} %collective-permute-done.refs_4_), channel_id=1, source_target_pairs={{0,4},{4,8},{8,12},{1,5},{5,9},{9,13},{2,6},{6,10},{10,14},{3,7},{... | collective-permute-start | bytes 1622024 | tf_op jit(solution)/shard_map/ppermute | solution.py:374
  24.2 1.3 %collective-permute-start.4 = (bf16[528,512]{1,0:T(8,128)(2,1)S(1)}, bf16[528,512]{1,0:T(8,128)(2,1)}, u32[]{:S(2)}, u32[]{:S(2)}) collective-permute-start(bf16[528,512]{1,0:T(8,128)(2,1)S(1)} %collective-permute-done.refs_4_), channel_id=1, source_target_pairs={{4,0},{8,4},{12,8},{5,1},{9,5},{13,9},{6,2},{10,6},{14,10},{7,3},{... | collective-permute-start | bytes 1622024 | tf_op jit(solution)/shard_map/ppermute | solution.py:374
  27.0 1.3 %collective-permute-start.8 = (bf16[512,512]{1,0:T(8,128)(2,1)S(1)}, bf16[512,512]{1,0:T(8,128)(2,1)S(1)}, u32[]{:S(2)}, u32[]{:S(2)}) collective-permute-start(bf16[512,512]{1,0:T(8,128)(2,1)S(1)} %collective-permute-done.7.refs_3_), channel_id=1, source_target_pairs={{4,0},{8,4},{5,1},{9,5},{6,2},{10,6},{7,3},{11,7},{20,16},{24,20},... | collective-permute-start | bytes 1572872 | tf_op jit(solution)/shard_map/ppermute | solution.py:374
  29.1 20.8 %collective-permute-done.8.refs_5_ = bf16[512,512]{1,0:T(8,128)(2,1)S(1)} collective-permute-done((bf16[512,512]{1,0:T(8,128)(2,1)S(1)}, bf16[512,512]{1,0:T(8,128)(2,1)S(1)}, u32[]{:S(2)}, u32[]{:S(2)}) %collective-permute-start.8) | collective-permute-done | bytes 524320 | tf_op jit(solution)/shard_map/ppermute | solution.py:374
  50.7 1.2 %copy-done.3 = bf16[1024,512]{1,0:T(8,128)(2,1)S(1)} copy-done((bf16[1024,512]{1,0:T(8,128)(2,1)S(1)}, bf16[1024,512]{1,0:T(8,128)(2,1)}, u32[]{:S(2)}) %copy-start.3) | copy-done | bytes 1048600
  52.9 1.5 %collective-permute-start.10 = (bf16[528,512]{1,0:T(8,128)(2,1)}, bf16[528,512]{1,0:T(8,128)(2,1)}, u32[]{:S(2)}, u32[]{:S(2)}) collective-permute-start(bf16[528,512]{1,0:T(8,128)(2,1)} %collective-permute-done.3.refs_4_), channel_id=1, source_target_pairs={{4,8},{8,12},{5,9},{9,13},{6,10},{10,14},{7,11},{11,15},{20,24},{2... | collective-permute-start | bytes 1622024 | tf_op jit(solution)/shard_map/ppermute | solution.py:374
  54.4 1.3 %collective-permute-start.11 = (bf16[528,512]{1,0:T(8,128)(2,1)}, bf16[528,512]{1,0:T(8,128)(2,1)}, u32[]{:S(2)}, u32[]{:S(2)}) collective-permute-start(bf16[528,512]{1,0:T(8,128)(2,1)} %collective-permute-done.4.refs_4_), channel_id=1, source_target_pairs={{4,0},{8,4},{5,1},{9,5},{6,2},{10,6},{7,3},{11,7},{20,16},{24,20},... | collective-permute-start | bytes 1622024 | tf_op jit(solution)/shard_map/ppermute | solution.py:374
  55.8 1.4 %collective-permute-done.9.refs_2_ = bf16[1024,1024]{1,0:T(8,128)(2,1)} collective-permute-done((bf16[1024,1024]{1,0:T(8,128)(2,1)S(1)}, bf16[1024,1024]{1,0:T(8,128)(2,1)}, u32[]{:S(2)}, u32[]{:S(2)}) %collective-permute-start.9) | collective-permute-done | bytes 2097184 | tf_op jit(solution)/shard_map/ppermute | solution.py:347
  57.2 5.5 %shard_map.95 = (f32[2,512,1024]{2,1,0:T(8,128)S(1)}, f32[4,1,512]{2,1,0:T(1,128)S(1)}, f32[2,1,1024]{2,1,0:T(1,128)S(1)}) custom-call(s32[3]{0:T(128)S(1)} %pad_add_fusion.2.sc_ref, s32[2,4,1024]{2,1,0:T(4,128)S(1)} %pad_add_fusion.refs_0_, bf16[1024,1024]{1,0:T(8,128)(2,1)S(1)} %shard_map.94.refs_1_, bf16[1024,1024]{1,0:T(8,128)(2,1)} %collective-permute-done.9.refs_2_, ...), custom_call_target="tpu_custom_call" | custom-call | flops 524288 | bytes 524288 | tf_op jit(solution)/shard_map/pallas_call | solution.py:162
  62.7 2.0 %copy-done.1 = f32[2,512,1024]{2,1,0:T(8,128)} copy-done((f32[2,512,1024]{2,1,0:T(8,128)}, f32[2,512,1024]{2,1,0:T(8,128)S(1)}, u32[]{:S(2)}) %copy-start.1) | copy-done | bytes 4194328
  65.5 1.3 %collective-permute-start.15 = (bf16[512,512]{1,0:T(8,128)(2,1)}, bf16[512,512]{1,0:T(8,128)(2,1)S(1)}, u32[]{:S(2)}, u32[]{:S(2)}) collective-permute-start(bf16[512,512]{1,0:T(8,128)(2,1)} %copy-done.10), channel_id=1, source_target_pairs={{4,0},{5,1},{6,2},{7,3},{20,16},{21,17},{22,18},{23,19}} | collective-permute-start | bytes 1572872 | tf_op jit(solution)/shard_map/ppermute | solution.py:374
  66.8 4.9 %collective-permute-done.11.refs_6_ = bf16[528,512]{1,0:T(8,128)(2,1)} collective-permute-done((bf16[528,512]{1,0:T(8,128)(2,1)}, bf16[528,512]{1,0:T(8,128)(2,1)}, u32[]{:S(2)}, u32[]{:S(2)}) %collective-permute-start.11) | collective-permute-done | bytes 540704 | tf_op jit(solution)/shard_map/ppermute | solution.py:374
  72.4 1.3 %collective-permute-start.16 = (bf16[528,512]{1,0:T(8,128)(2,1)}, bf16[528,512]{1,0:T(8,128)(2,1)S(1)}, u32[]{:S(2)}, u32[]{:S(2)}) collective-permute-start(bf16[528,512]{1,0:T(8,128)(2,1)} %collective-permute-done.11.refs_6_), channel_id=1, source_target_pairs={{4,0},{5,1},{6,2},{7,3},{20,16},{21,17},{22,18},{23,19}} | collective-permute-start | bytes 1622024 | tf_op jit(solution)/shard_map/ppermute | solution.py:374
  73.7 1.0 copy-done.7
  74.7 1.8 %shard_map.96 = (f32[2,512,1024]{2,1,0:T(8,128)S(1)}, f32[4,1,512]{2,1,0:T(1,128)S(1)}, f32[2,1,1024]{2,1,0:T(1,128)S(1)}) custom-call(s32[3]{0:T(128)S(1)} %pad_add_fusion.2.sc_ref, s32[2,4,1024]{2,1,0:T(4,128)S(1)} %pad_add_fusion.1.refs_0_, bf16[1024,1024]{1,0:T(8,128)(2,1)S(1)} %shard_map.94.refs_1_, bf16[1024,1024]{1,0:T(8,128)(2,1)} %collective-permute-done.9.refs_2_, ...), custom_call_target="tpu_custom_call" | custom-call | flops 2148007936 | bytes 4718592 | tf_op jit(solution)/shard_map/pallas_call | solution.py:162
  76.5 1.0 copy-done.5
  77.6 5.6 %shard_map.97 = (f32[2,512,1024]{2,1,0:T(8,128)S(1)}, f32[4,1,512]{2,1,0:T(1,128)S(1)}, f32[2,1,1024]{2,1,0:T(1,128)S(1)}) custom-call(s32[3]{0:T(128)S(1)} %pad_add_fusion.2.sc_ref, s32[2,4,1024]{2,1,0:T(4,128)S(1)} %pad_add_fusion.1.refs_0_, bf16[1024,1024]{1,0:T(8,128)(2,1)S(1)} %shard_map.94.refs_1_, bf16[1024,1024]{1,0:T(8,128)(2,1)} %collective-permute-done.9.refs_2_, ...), custom_call_target="tpu_custom_call" | custom-call | flops 2148007936 | bytes 4718592 | tf_op jit(solution)/shard_map/pallas_call | solution.py:162
  83.2 5.9 %shard_map.98 = (f32[2,512,1024]{2,1,0:T(8,128)S(1)}, f32[4,1,512]{2,1,0:T(1,128)S(1)}, f32[2,1,1024]{2,1,0:T(1,128)S(1)}) custom-call(s32[3]{0:T(128)S(1)} %pad_add_fusion.2.sc_ref, s32[2,4,1024]{2,1,0:T(4,128)S(1)} %pad_add_fusion.1.refs_0_, bf16[1024,1024]{1,0:T(8,128)(2,1)S(1)} %shard_map.94.refs_1_, bf16[1024,1024]{1,0:T(8,128)(2,1)} %collective-permute-done.9.refs_2_, ...), custom_call_target="tpu_custom_call" | custom-call | flops 2148007936 | bytes 4718592 | tf_op jit(solution)/shard_map/pallas_call | solution.py:162
  89.1 4.9 %collective-permute-done.16.refs_6_ = bf16[528,512]{1,0:T(8,128)(2,1)S(1)} collective-permute-done((bf16[528,512]{1,0:T(8,128)(2,1)}, bf16[528,512]{1,0:T(8,128)(2,1)S(1)}, u32[]{:S(2)}, u32[]{:S(2)}) %collective-permute-start.16) | collective-permute-done | bytes 540704 | tf_op jit(solution)/shard_map/ppermute | solution.py:374
  94.0 5.8 %shard_map.99 = (f32[2,512,1024]{2,1,0:T(8,128)S(1)}, f32[4,1,512]{2,1,0:T(1,128)S(1)}, f32[2,1,1024]{2,1,0:T(1,128)S(1)}) custom-call(s32[3]{0:T(128)S(1)} %pad_add_fusion.2.sc_ref, s32[2,4,1024]{2,1,0:T(4,128)S(1)} %pad_add_fusion.1.refs_0_, bf16[1024,1024]{1,0:T(8,128)(2,1)S(1)} %shard_map.94.refs_1_, bf16[1024,1024]{1,0:T(8,128)(2,1)} %collective-permute-done.9.refs_2_, ...), custom_call_target="tpu_custom_call" | custom-call | flops 2148007936 | bytes 4718592 | tf_op jit(solution)/shard_map/pallas_call | solution.py:162
  100.7 1.2 %collective-permute-start.19 = (f32[4,1,512]{2,1,0:T(1,128)S(1)}, f32[4,1,512]{2,1,0:T(1,128)S(1)}, u32[]{:S(2)}, u32[]{:S(2)}) collective-permute-start(f32[4,1,512]{2,1,0:T(1,128)S(1)} %get-tuple-element.56.refs_5_), channel_id=1, source_target_pairs={{12,0},{0,4},{4,8},{8,12},{13,1},{1,5},{5,9},{9,13},{14,2},{2,6},{... | collective-permute-start | bytes 24584 | tf_op jit(solution)/shard_map/ppermute | solution.py:347
  101.9 1.6 %collective-permute-done.17.refs_6_ = f32[4,1,512]{2,1,0:T(1,128)S(1)} collective-permute-done((f32[4,1,512]{2,1,0:T(1,128)S(1)}, f32[4,1,512]{2,1,0:T(1,128)S(1)}, u32[]{:S(2)}, u32[]{:S(2)}) %collective-permute-start.17) | collective-permute-done | bytes 8224 | tf_op jit(solution)/shard_map/ppermute | solution.py:347
  103.5 1.8 %collective-permute-done.18.refs_7_ = f32[4,1,512]{2,1,0:T(1,128)S(1)} collective-permute-done((f32[4,1,512]{2,1,0:T(1,128)S(1)}, f32[4,1,512]{2,1,0:T(1,128)S(1)}, u32[]{:S(2)}, u32[]{:S(2)}) %collective-permute-start.18) | collective-permute-done | bytes 8224 | tf_op jit(solution)/shard_map/ppermute | solution.py:347
  106.1 3.3 %shard_map.100 = (f32[16,1024]{1,0:T(8,128)S(1)}, f32[16,1024]{1,0:T(8,128)S(1)}, f32[16,1024]{1,0:T(8,128)S(1)}, f32[16,1024]{1,0:T(8,128)S(1)}) custom-call(s32[3]{0:T(128)S(1)} %pad_add_fusion.2.sc_ref, s32[16]{0:T(128)S(1)} %fusion.8.list_ref, f32[2,512,1024]{2,1,0:T(8,128)S(1)} %copy-done.2, f32[2,512,1024]{2,1,0:T(8,128)S(1)} %get-tuple-element.44.refs_1_, ...), custom_call_target="tpu_custom_call" | custom-call | flops 524288 | bytes 524288 | tf_op jit(solution)/shard_map/pallas_call | solution.py:272
  110.2 1.6 %collective-permute-done.20.refs_1_ = f32[16,1024]{1,0:T(8,128)S(1)} collective-permute-done((f32[16,1024]{1,0:T(8,128)S(1)}, f32[16,1024]{1,0:T(8,128)S(1)}, u32[]{:S(2)}, u32[]{:S(2)}) %collective-permute-start.20) | collective-permute-done | bytes 65568 | tf_op jit(solution)/shard_map/ppermute | solution.py:347
  111.9 2.6 %collective-permute-done.21.refs_2_ = f32[16,1024]{1,0:T(8,128)S(1)} collective-permute-done((f32[16,1024]{1,0:T(8,128)S(1)}, f32[16,1024]{1,0:T(8,128)S(1)}, u32[]{:S(2)}, u32[]{:S(2)}) %collective-permute-start.21) | collective-permute-done | bytes 65568 | tf_op jit(solution)/shard_map/ppermute | solution.py:347
  (57 shorter events, 11.0 us)
Async XLA Ops:
  0.6 101.2 %copy-start = (s32[4,16]{1,0:T(4,128)S(1)}, s32[4,16]{1,0:T(4,128)}, u32[]{:S(2)}) copy-start(s32[4,16]{1,0:T(4,128)} %param.13) | copy-start | bytes 772
  2.9 15.3 %collective-permute-start = (bf16[528,512]{1,0:T(8,128)(2,1)S(1)}, bf16[528,512]{1,0:T(8,128)(2,1)S(1)}, u32[]{:S(2)}, u32[]{:S(2)}) collective-permute-start(bf16[528,512]{1,0:T(8,128)(2,1)S(1)} %pad_maximum_fusion), channel_id=1, source_target_pairs={{2,0},{0,2},{3,1},{1,3},{6,4},{4,6},{7,5},{5,7},{10,8},{8,10},{11,... | collective-permute-start | bytes 1622024 | tf_op jit(solution)/shard_map/ppermute | solution.py:347
  6.7 4.9 %collective-permute-start.1 = (s32[4,1024]{1,0:T(4,128)S(1)}, s32[4,1024]{1,0:T(4,128)S(1)}, u32[]{:S(2)}, u32[]{:S(2)}) collective-permute-start(s32[4,1024]{1,0:T(4,128)S(1)} %get-tuple-element.40), channel_id=1, source_target_pairs={{1,0},{0,1},{3,2},{2,3},{5,4},{4,5},{7,6},{6,7},{9,8},{8,9},{11,10... | collective-permute-start | bytes 49160 | tf_op jit(solution)/shard_map/ppermute | solution.py:347
  6.7 18.8 %collective-permute-start.5 = (bf16[512,512]{1,0:T(8,128)(2,1)S(1)}, bf16[512,512]{1,0:T(8,128)(2,1)S(1)}, u32[]{:S(2)}, u32[]{:S(2)}) collective-permute-start(bf16[512,512]{1,0:T(8,128)(2,1)S(1)} %get-tuple-element.65.refs_3_), channel_id=1, source_target_pairs={{0,4},{4,8},{8,12},{1,5},{5,9},{9,13},{2,6},{6,10},{10,14},{3,7},{... | collective-permute-start | bytes 1572872 | tf_op jit(solution)/shard_map/ppermute | solution.py:374
  10.3 16.8 %collective-permute-start.7 = (bf16[512,512]{1,0:T(8,128)(2,1)S(1)}, bf16[512,512]{1,0:T(8,128)(2,1)S(1)}, u32[]{:S(2)}, u32[]{:S(2)}) collective-permute-start(bf16[512,512]{1,0:T(8,128)(2,1)S(1)} %get-tuple-element.65.refs_3_), channel_id=1, source_target_pairs={{4,0},{8,4},{12,8},{5,1},{9,5},{13,9},{6,2},{10,6},{14,10},{7,3},{... | collective-permute-start | bytes 1572872 | tf_op jit(solution)/shard_map/ppermute | solution.py:374
  18.2 32.5 %collective-permute-start.2 = (bf16[1024,512]{1,0:T(8,128)(2,1)}, bf16[1024,512]{1,0:T(8,128)(2,1)S(1)}, u32[]{:S(2)}, u32[]{:S(2)}) collective-permute-start(bf16[1024,512]{1,0:T(8,128)(2,1)} %refs_0_), channel_id=1, source_target_pairs={{2,0},{0,2},{3,1},{1,3},{6,4},{4,6},{7,5},{5,7},{10,8},{8,10},{11,... | collective-permute-start | bytes 3145736 | tf_op jit(solution)/shard_map/ppermute | solution.py:347
  19.9 30.0 %collective-permute-start.3 = (bf16[528,512]{1,0:T(8,128)(2,1)S(1)}, bf16[528,512]{1,0:T(8,128)(2,1)}, u32[]{:S(2)}, u32[]{:S(2)}) collective-permute-start(bf16[528,512]{1,0:T(8,128)(2,1)S(1)} %collective-permute-done.refs_4_), channel_id=1, source_target_pairs={{0,4},{4,8},{8,12},{1,5},{5,9},{9,13},{2,6},{6,10},{10,14},{3,7},{... | collective-permute-start | bytes 1622024 | tf_op jit(solution)/shard_map/ppermute | solution.py:374
  24.2 25.7 %collective-permute-start.4 = (bf16[528,512]{1,0:T(8,128)(2,1)S(1)}, bf16[528,512]{1,0:T(8,128)(2,1)}, u32[]{:S(2)}, u32[]{:S(2)}) collective-permute-start(bf16[528,512]{1,0:T(8,128)(2,1)S(1)} %collective-permute-done.refs_4_), channel_id=1, source_target_pairs={{4,0},{8,4},{12,8},{5,1},{9,5},{13,9},{6,2},{10,6},{14,10},{7,3},{... | collective-permute-start | bytes 1622024 | tf_op jit(solution)/shard_map/ppermute | solution.py:374
  25.5 3.6 %collective-permute-start.6 = (bf16[512,512]{1,0:T(8,128)(2,1)S(1)}, bf16[512,512]{1,0:T(8,128)(2,1)S(1)}, u32[]{:S(2)}, u32[]{:S(2)}) collective-permute-start(bf16[512,512]{1,0:T(8,128)(2,1)S(1)} %collective-permute-done.5.refs_3_), channel_id=1, source_target_pairs={{4,8},{8,12},{5,9},{9,13},{6,10},{10,14},{7,11},{11,15},{20,24},{2... | collective-permute-start | bytes 1572872 | tf_op jit(solution)/shard_map/ppermute | solution.py:374
  27.0 22.9 %collective-permute-start.8 = (bf16[512,512]{1,0:T(8,128)(2,1)S(1)}, bf16[512,512]{1,0:T(8,128)(2,1)S(1)}, u32[]{:S(2)}, u32[]{:S(2)}) collective-permute-start(bf16[512,512]{1,0:T(8,128)(2,1)S(1)} %collective-permute-done.7.refs_3_), channel_id=1, source_target_pairs={{4,0},{8,4},{5,1},{9,5},{6,2},{10,6},{7,3},{11,7},{20,16},{24,20},... | collective-permute-start | bytes 1572872 | tf_op jit(solution)/shard_map/ppermute | solution.py:374
  29.1 20.8 %copy-start.8 = (bf16[512,512]{1,0:T(8,128)(2,1)}, bf16[512,512]{1,0:T(8,128)(2,1)S(1)}, u32[]{:S(2)}) copy-start(bf16[512,512]{1,0:T(8,128)(2,1)S(1)} %collective-permute-done.6.refs_3_) | copy-start | bytes 1572868
  50.7 1.2 %copy-start.3 = (bf16[1024,512]{1,0:T(8,128)(2,1)S(1)}, bf16[1024,512]{1,0:T(8,128)(2,1)}, u32[]{:S(2)}) copy-start(bf16[1024,512]{1,0:T(8,128)(2,1)} %refs_0_) | copy-start | bytes 3145732
  52.8 4.4 %collective-permute-start.9 = (bf16[1024,1024]{1,0:T(8,128)(2,1)S(1)}, bf16[1024,1024]{1,0:T(8,128)(2,1)}, u32[]{:S(2)}, u32[]{:S(2)}) collective-permute-start(bf16[1024,1024]{1,0:T(8,128)(2,1)S(1)} %shard_map.94.refs_1_), channel_id=1, source_target_pairs={{1,0},{0,1},{3,2},{2,3},{5,4},{4,5},{7,6},{6,7},{9,8},{8,9},{11,10... | collective-permute-start | bytes 6291464 | tf_op jit(solution)/shard_map/ppermute | solution.py:347
  52.9 13.9 %collective-permute-start.10 = (bf16[528,512]{1,0:T(8,128)(2,1)}, bf16[528,512]{1,0:T(8,128)(2,1)}, u32[]{:S(2)}, u32[]{:S(2)}) collective-permute-start(bf16[528,512]{1,0:T(8,128)(2,1)} %collective-permute-done.3.refs_4_), channel_id=1, source_target_pairs={{4,8},{8,12},{5,9},{9,13},{6,10},{10,14},{7,11},{11,15},{20,24},{2... | collective-permute-start | bytes 1622024 | tf_op jit(solution)/shard_map/ppermute | solution.py:374
  54.4 17.3 %collective-permute-start.11 = (bf16[528,512]{1,0:T(8,128)(2,1)}, bf16[528,512]{1,0:T(8,128)(2,1)}, u32[]{:S(2)}, u32[]{:S(2)}) collective-permute-start(bf16[528,512]{1,0:T(8,128)(2,1)} %collective-permute-done.4.refs_4_), channel_id=1, source_target_pairs={{4,0},{8,4},{5,1},{9,5},{6,2},{10,6},{7,3},{11,7},{20,16},{24,20},... | collective-permute-start | bytes 1622024 | tf_op jit(solution)/shard_map/ppermute | solution.py:374
  62.7 2.0 %copy-start.1 = (f32[2,512,1024]{2,1,0:T(8,128)}, f32[2,512,1024]{2,1,0:T(8,128)S(1)}, u32[]{:S(2)}) copy-start(f32[2,512,1024]{2,1,0:T(8,128)S(1)} %get-tuple-element.38.refs_0_) | copy-start | bytes 12582916
  64.6 2.1 %collective-permute-start.12 = (s32[4,1024]{1,0:T(4,128)S(1)}, s32[4,1024]{1,0:T(4,128)S(1)}, u32[]{:S(2)}, u32[]{:S(2)}) collective-permute-start(s32[4,1024]{1,0:T(4,128)S(1)} %get-tuple-element.40), channel_id=1, source_target_pairs={{1,0},{0,1},{3,2},{2,3},{5,4},{4,5},{7,6},{6,7},{9,8},{8,9},{11,10... | collective-permute-start | bytes 49160 | tf_op jit(solution)/shard_map/ppermute | solution.py:347
  64.8 24.3 %collective-permute-start.13 = (bf16[512,512]{1,0:T(8,128)(2,1)}, bf16[512,512]{1,0:T(8,128)(2,1)S(1)}, u32[]{:S(2)}, u32[]{:S(2)}) collective-permute-start(bf16[512,512]{1,0:T(8,128)(2,1)} %copy-done.8), channel_id=1, source_target_pairs={{8,12},{9,13},{10,14},{11,15},{24,28},{25,29},{26,30},{27,31}} | collective-permute-start | bytes 1572872 | tf_op jit(solution)/shard_map/ppermute | solution.py:374
  65.5 23.6 %collective-permute-start.15 = (bf16[512,512]{1,0:T(8,128)(2,1)}, bf16[512,512]{1,0:T(8,128)(2,1)S(1)}, u32[]{:S(2)}, u32[]{:S(2)}) collective-permute-start(bf16[512,512]{1,0:T(8,128)(2,1)} %copy-done.10), channel_id=1, source_target_pairs={{4,0},{5,1},{6,2},{7,3},{20,16},{21,17},{22,18},{23,19}} | collective-permute-start | bytes 1572872 | tf_op jit(solution)/shard_map/ppermute | solution.py:374
  71.7 17.4 %collective-permute-start.14 = (bf16[528,512]{1,0:T(8,128)(2,1)}, bf16[528,512]{1,0:T(8,128)(2,1)S(1)}, u32[]{:S(2)}, u32[]{:S(2)}) collective-permute-start(bf16[528,512]{1,0:T(8,128)(2,1)} %collective-permute-done.10.refs_4_), channel_id=1, source_target_pairs={{8,12},{9,13},{10,14},{11,15},{24,28},{25,29},{26,30},{27,31}} | collective-permute-start | bytes 1622024 | tf_op jit(solution)/shard_map/ppermute | solution.py:374
  72.4 21.6 %collective-permute-start.16 = (bf16[528,512]{1,0:T(8,128)(2,1)}, bf16[528,512]{1,0:T(8,128)(2,1)S(1)}, u32[]{:S(2)}, u32[]{:S(2)}) collective-permute-start(bf16[528,512]{1,0:T(8,128)(2,1)} %collective-permute-done.11.refs_6_), channel_id=1, source_target_pairs={{4,0},{5,1},{6,2},{7,3},{20,16},{21,17},{22,18},{23,19}} | collective-permute-start | bytes 1622024 | tf_op jit(solution)/shard_map/ppermute | solution.py:374
  73.7 1.0 copy-start.7
  74.7 8.4 %copy-start.9 = (bf16[512,512]{1,0:T(8,128)(2,1)S(1)}, bf16[512,512]{1,0:T(8,128)(2,1)}, u32[]{:S(2)}) copy-start(bf16[512,512]{1,0:T(8,128)(2,1)} %copy-done.8) | copy-start | bytes 1572868
  74.7 8.4 %copy-start.11 = (bf16[512,512]{1,0:T(8,128)(2,1)S(1)}, bf16[512,512]{1,0:T(8,128)(2,1)}, u32[]{:S(2)}) copy-start(bf16[512,512]{1,0:T(8,128)(2,1)} %copy-done.10) | copy-start | bytes 1572868
  76.5 1.0 copy-start.5
  89.0 17.1 %copy-start.2 = (f32[2,512,1024]{2,1,0:T(8,128)S(1)}, f32[2,512,1024]{2,1,0:T(8,128)}, u32[]{:S(2)}) copy-start(f32[2,512,1024]{2,1,0:T(8,128)} %copy-done.1) | copy-start | bytes 12582916
  99.8 3.7 %collective-permute-start.17 = (f32[4,1,512]{2,1,0:T(1,128)S(1)}, f32[4,1,512]{2,1,0:T(1,128)S(1)}, u32[]{:S(2)}, u32[]{:S(2)}) collective-permute-start(f32[4,1,512]{2,1,0:T(1,128)S(1)} %get-tuple-element.56.refs_5_), channel_id=1, source_target_pairs={{4,0},{8,4},{12,8},{0,12},{5,1},{9,5},{13,9},{1,13},{6,2},{10,6},{... | collective-permute-start | bytes 24584 | tf_op jit(solution)/shard_map/ppermute | solution.py:347
  100.7 4.5 %collective-permute-start.18 = (f32[4,1,512]{2,1,0:T(1,128)S(1)}, f32[4,1,512]{2,1,0:T(1,128)S(1)}, u32[]{:S(2)}, u32[]{:S(2)}) collective-permute-start(f32[4,1,512]{2,1,0:T(1,128)S(1)} %get-tuple-element.56.refs_5_), channel_id=1, source_target_pairs={{8,0},{12,4},{0,8},{4,12},{9,1},{13,5},{1,9},{5,13},{10,2},{14,6},... | collective-permute-start | bytes 24584 | tf_op jit(solution)/shard_map/ppermute | solution.py:347
  100.7 5.4 %collective-permute-start.19 = (f32[4,1,512]{2,1,0:T(1,128)S(1)}, f32[4,1,512]{2,1,0:T(1,128)S(1)}, u32[]{:S(2)}, u32[]{:S(2)}) collective-permute-start(f32[4,1,512]{2,1,0:T(1,128)S(1)} %get-tuple-element.56.refs_5_), channel_id=1, source_target_pairs={{12,0},{0,4},{4,8},{8,12},{13,1},{1,5},{5,9},{9,13},{14,2},{2,6},{... | collective-permute-start | bytes 24584 | tf_op jit(solution)/shard_map/ppermute | solution.py:347
  109.4 2.5 %collective-permute-start.20 = (f32[16,1024]{1,0:T(8,128)S(1)}, f32[16,1024]{1,0:T(8,128)S(1)}, u32[]{:S(2)}, u32[]{:S(2)}) collective-permute-start(f32[16,1024]{1,0:T(8,128)S(1)} %get-tuple-element.59), channel_id=1, source_target_pairs={{1,0},{2,1},{3,2},{0,3},{5,4},{6,5},{7,6},{4,7},{9,8},{10,9},{11,1... | collective-permute-start | bytes 196616 | tf_op jit(solution)/shard_map/ppermute | solution.py:347
  109.5 5.0 %collective-permute-start.21 = (f32[16,1024]{1,0:T(8,128)S(1)}, f32[16,1024]{1,0:T(8,128)S(1)}, u32[]{:S(2)}, u32[]{:S(2)}) collective-permute-start(f32[16,1024]{1,0:T(8,128)S(1)} %get-tuple-element.60), channel_id=1, source_target_pairs={{2,0},{3,1},{0,2},{1,3},{6,4},{7,5},{4,6},{5,7},{10,8},{11,9},{8,1... | collective-permute-start | bytes 196616 | tf_op jit(solution)/shard_map/ppermute | solution.py:347
  110.1 4.6 %collective-permute-start.22 = (f32[16,1024]{1,0:T(8,128)S(1)}, f32[16,1024]{1,0:T(8,128)S(1)}, u32[]{:S(2)}, u32[]{:S(2)}) collective-permute-start(f32[16,1024]{1,0:T(8,128)S(1)} %get-tuple-element.61), channel_id=1, source_target_pairs={{3,0},{0,1},{1,2},{2,3},{7,4},{4,5},{5,6},{6,7},{11,8},{8,9},{9,10... | collective-permute-start | bytes 196616 | tf_op jit(solution)/shard_map/ppermute | solution.py:347
  (3 other events, 2.4 us)
